TPU v7x, 512 devices: a whole 4x8x8 slice. The times are simulated.
512 devices in a mesh: seq: 128 (over x, z, y_hi), dp: 4 (over y_lo, core).
Axes of the slice: x: 4, y: 8 (y_hi: 4, y_lo: 2; y = y_hi * 2 + y_lo), z: 8, core: 2. Of those that a mesh axis runs over, the one named last changes fastest.
Arguments:
- queries: bfloat16 [768, 32768], P('dp', 'seq'), may hold values from -9.5 to 9.5
- keys: bfloat16 [768, 32768], P('dp', 'seq'), may hold values from -4.5 to 4.5
- values: bfloat16 [768, 32768], P('dp', 'seq'), may hold values from -6 to 6
- grad_out: bfloat16 [768, 32768], P('dp', 'seq'), may hold values from -24 to 24
- out_weight: bfloat16 [768, 768], P('dp'), may hold values from -0.21875 to 0.21875
- offsets: int32 [12], P('dp'), may hold values from 0 to 127
Outputs:
- grad_queries: bfloat16 [768, 32768], P('dp', 'seq')
- grad_keys: bfloat16 [768, 32768], P('dp', 'seq')
- grad_values: bfloat16 [768, 32768], P('dp', 'seq')
- grad_weight: float32 [768, 768], P('dp')
All inputs are finite; a program needn't handle non-finite values.
Results may differ from a plain program's by a relative error of at most 0.012.
The roundings to bfloat16 on the way count: a program that leaves them out, or rounds other values in their place, can miss the bound.
Values may be sent and summed in bfloat16 or wider, within the bound.
No kernel may reach another device: no remote copies, remote signals or barrier semaphores. Data moves between devices by JAX's collectives and lax.ppermute only.
A program may use at most 64 MiB of HBM per device.

v0:
```python
import jax
import jax.numpy as jnp
from jax import lax
from jax.sharding import PartitionSpec as P

HEAD_DIM = 64
SEG_A = 256
RB = 2
RC = 16
RE = 128


WEIGHT_SCALE = 0.03125


def swapped(value, axis, distance):
    return lax.ppermute(value, axis, [(i, i ^ 1 << distance) for i in range(lax.axis_size(axis))])


def pick_rows(source, seg_width, stride, shifts):
    seg_count = source.shape[0] // seg_width
    shaped = source.reshape((seg_count, seg_width // stride, stride) + source.shape[1:])
    if stride == 1:
        return shaped[:, :, 0]
    chooser = jnp.arange(stride)[:, None] == (shifts % stride)[None, :]
    chooser = chooser.reshape((1, 1, stride, shifts.shape[0]) + (1,) * (source.ndim - 2)).astype(
        source.dtype
    )
    return jnp.sum(shaped * chooser, axis=2)


def spread_rows(picked, stride, shifts):
    if stride == 1:
        return picked.reshape((-1,) + picked.shape[2:])
    chooser = jnp.arange(stride)[:, None] == (shifts % stride)[None, :]
    chooser = chooser.reshape((1, 1, stride, shifts.shape[0]) + (1,) * (picked.ndim - 3)).astype(
        picked.dtype
    )
    placed = jnp.expand_dims(picked, 2) * chooser
    return placed.reshape((-1,) + picked.shape[2:])


def local(queries, keys, values, grad_out, out_weight, offsets):
    row_count = queries.shape[1]
    heads_here = offsets.shape[0]
    score_scale = HEAD_DIM ** (-0.5)
    full_grad = lax.all_gather(grad_out, "dp", axis=0, tiled=True)
    dout_flat = jnp.dot(out_weight, full_grad, preferred_element_type=jnp.float32).astype(
        jnp.bfloat16
    )
    head_shape = (row_count, heads_here, HEAD_DIM)
    sources = tuple(
        (jnp.transpose(source).reshape(head_shape) for source in (queries, keys, values, dout_flat))
    )
    layout = ((SEG_A, 1), (row_count, RB), (row_count, RC), (row_count, RE))
    selected = [
        tuple((pick_rows(source, seg_width, stride, offsets) for source in sources))
        for seg_width, stride in layout
    ]
    near_query, near_key, near_value, near_dout = selected[2]
    partner_key, partner_value = swapped((near_key[0], near_value[0]), "seq", 0)
    pair_keys = jnp.concatenate([near_key, partner_key[None]], axis=1)
    pair_values = jnp.concatenate([near_value, partner_value[None]], axis=1)
    far_query, far_key, far_value, far_dout = selected[3]
    all_key, all_value = (
        lax.all_gather(far_key[0], "seq", axis=0, tiled=True),
        lax.all_gather(far_value[0], "seq", axis=0, tiled=True),
    )
    levels = (
        selected[0],
        selected[1],
        (near_query, pair_keys, pair_values, near_dout),
        (far_query, all_key[None], all_value[None], far_dout),
    )
    score_sets = []
    log_masses = []
    for level_query, level_key, level_value, level_dout in levels:
        scores = (
            jnp.einsum(
                "sqhd,skhd->shqk", level_query, level_key, preferred_element_type=jnp.float32
            )
            * score_scale
        )
        row_max = jnp.max(scores, axis=-1)
        log_mass = row_max + jnp.log(jnp.sum(jnp.exp(scores - row_max[..., None]), axis=-1))
        score_sets.append(scores)
        log_masses.append(jnp.swapaxes(log_mass, 1, 2))
    base_stat = spread_rows(log_masses[0], 1, offsets)
    peak_stat = base_stat
    for (seg_width, stride), log_mass in zip(layout[1:], log_masses[1:]):
        lifted = log_mass - pick_rows(base_stat, seg_width, stride, offsets)
        peak_stat = jnp.maximum(peak_stat, base_stat + spread_rows(lifted, stride, offsets))
    total_mass = jnp.zeros_like(base_stat)
    for (seg_width, stride), log_mass in zip(layout, log_masses):
        total_mass = total_mass + spread_rows(
            jnp.exp(log_mass - pick_rows(peak_stat, seg_width, stride, offsets)), stride, offsets
        )
    normalizer = peak_stat + jnp.log(total_mass)
    prob_sets = []
    attended = jnp.zeros(head_shape, jnp.float32)
    for (seg_width, stride), level, scores in zip(layout, levels, score_sets):
        row_norm = jnp.swapaxes(pick_rows(normalizer, seg_width, stride, offsets), 1, 2)
        probs = jnp.exp(scores - row_norm[..., None])
        probs_low = probs.astype(jnp.bfloat16)
        prob_sets.append((probs, probs_low))
        attended = attended + spread_rows(
            jnp.einsum("shqk,skhd->sqhd", probs_low, level[2], preferred_element_type=jnp.float32),
            stride,
            offsets,
        )
    delta_stat = jnp.sum(sources[3].astype(jnp.float32) * attended, axis=-1)
    grad_query = jnp.zeros(head_shape, jnp.float32)
    grad_key = jnp.zeros(head_shape, jnp.float32)
    grad_value = jnp.zeros(head_shape, jnp.float32)
    for level_index in range(4):
        seg_width, stride = layout[level_index]
        level_query, level_key, level_value, level_dout = levels[level_index]
        probs, probs_low = prob_sets[level_index]
        row_delta = jnp.swapaxes(pick_rows(delta_stat, seg_width, stride, offsets), 1, 2)[..., None]
        grad_probs = jnp.einsum(
            "sqhd,skhd->shqk", level_dout, level_value, preferred_element_type=jnp.float32
        )
        grad_scores = (probs * (grad_probs - row_delta)).astype(jnp.bfloat16)
        grad_query = grad_query + spread_rows(
            jnp.einsum(
                "shqk,skhd->sqhd", grad_scores, level_key, preferred_element_type=jnp.float32
            ),
            stride,
            offsets,
        )
        if level_index == 3:
            key_part = jnp.einsum(
                "shqk,sqhd->skhd", grad_scores, level_query, preferred_element_type=jnp.float32
            )
            value_part = jnp.einsum(
                "shqk,sqhd->skhd", probs_low, level_dout, preferred_element_type=jnp.float32
            )
            key_own, value_own = (
                lax.psum_scatter(key_part[0], "seq", scatter_dimension=0, tiled=True),
                lax.psum_scatter(value_part[0], "seq", scatter_dimension=0, tiled=True),
            )
            grad_key = grad_key + spread_rows(key_own[None], stride, offsets)
            grad_value = grad_value + spread_rows(value_own[None], stride, offsets)
        else:
            key_part = jnp.einsum(
                "shqk,sqhd->skhd", grad_scores, level_query, preferred_element_type=jnp.float32
            )
            value_part = jnp.einsum(
                "shqk,sqhd->skhd", probs_low, level_dout, preferred_element_type=jnp.float32
            )
            if level_index == 2:
                half_keys = key_part.shape[1] // 2
                back_key, back_value = swapped(
                    (key_part[0, half_keys:], value_part[0, half_keys:]), "seq", 0
                )
                key_part = key_part[:, :half_keys] + back_key[None]
                value_part = value_part[:, :half_keys] + back_value[None]
            grad_key = grad_key + spread_rows(key_part, stride, offsets)
            grad_value = grad_value + spread_rows(value_part, stride, offsets)
    flat_shape = (row_count, heads_here * HEAD_DIM)
    grad_queries = jnp.transpose(
        (grad_query * score_scale).astype(jnp.bfloat16).reshape(flat_shape)
    )
    grad_keys = jnp.transpose((grad_key * score_scale).astype(jnp.bfloat16).reshape(flat_shape))
    grad_values = jnp.transpose(grad_value.astype(jnp.bfloat16).reshape(flat_shape))
    attended_low = attended.astype(jnp.bfloat16).reshape(flat_shape)
    partial_weight = (
        lax.dot_general(
            attended_low, full_grad, (((0,), (1,)), ((), ())), preferred_element_type=jnp.float32
        )
        * WEIGHT_SCALE
    )
    grad_weight = lax.psum(partial_weight, "seq")
    return (grad_queries, grad_keys, grad_values, grad_weight)


def solution(mesh):
    return jax.shard_map(
        local,
        mesh=mesh,
        in_specs=(
            P("dp", "seq"),
            P("dp", "seq"),
            P("dp", "seq"),
            P("dp", "seq"),
            P("dp", None),
            P("dp"),
        ),
        out_specs=(P("dp", "seq"), P("dp", "seq"), P("dp", "seq"), P("dp", None)),
        check_vma=False,
    )
```

profile of v0, /device:TPU:16, one launch (start us, length us, event | category | flops | bytes accessed | tf_op | source)
XLA Modules:
  0.0 2247.4 jit_solution(18020146160521977757)
XLA Ops:
  7.2 0.7 and_select_fusion.1
  8.7 1.0 copy.307
  9.8 0.8 copy-done.1
  11.1 0.8 copy-done.43
  11.8 6.5 all_gather.10
  18.9 1.4 multiply_reduce_fusion
  20.9 7.2 collective-permute-start.1
  28.7 1.9 collective-permute-start
  30.7 0.7 reshape_reshape.52
  33.6 0.7 reshape_reshape.50
  36.4 0.7 copy-done.62
  37.1 1.4 multiply_reduce_fusion.8
  38.5 0.9 copy.319
  39.5 374.0 %all_gather.9 = bf16[256,3,64]{2,1,0:T(4,128)(2,1)S(1)} all-gather(bf16[2,3,64]{2,1,0:T(4,128)(2,1)S(1)} %copy.319), channel_id=1, replica_groups=mesh['seq'=128,'dp'=4] {'seq'}, dimensions={0}, use_global_device_ids=true | all-gather | bytes 99072 | tf_op jit(solution)/shard_map/all_gather | solution.py:66
  413.6 0.7 copy-done.4
  415.4 1.5 multiply_reduce_fusion.7
  416.9 1.0 copy.310
  420.1 374.3 %all_gather.11 = bf16[256,3,64]{2,1,0:T(4,128)(2,1)S(1)} all-gather(bf16[2,3,64]{2,1,0:T(4,128)(2,1)S(1)} %copy.357), channel_id=1, replica_groups=mesh['seq'=128,'dp'=4] {'seq'}, dimensions={0}, use_global_device_ids=true | all-gather | bytes 99072 | tf_op jit(solution)/shard_map/all_gather | solution.py:67
  795.4 0.7 copy-done.26
  796.6 0.7 copy.367
  797.8 1.2 dynamic-slice
  799.6 0.9 fusion.95
  805.1 0.9 convolution_bitcast_fusion.9
  808.2 0.8 copy.348
  809.1 0.9 copy.356
  810.0 1.3 fusion.30
  811.9 0.7 reshape.1845
  812.6 1.8 convolution_bitcast_fusion
  814.3 1.3 multiply_reduce_fusion.15
  815.7 1.3 copy.381
  817.0 1.3 copy.382
  818.3 1.2 fusion.7
  819.5 0.7 convolution_bitcast_fusion.10
  820.3 0.8 convolution_bitcast_fusion.1
  821.9 0.8 convolution_bitcast_fusion.2
  823.6 1.0 fusion.3
  826.7 0.9 fusion.98
  828.6 2.1 collective-permute-start.3
  830.8 1.0 copy.405
  832.5 0.9 fusion.5
  834.3 1.1 convolution_multiply_fusion.1
  835.5 1.0 copy.394
  837.2 0.8 convolution_bitcast_fusion.8
  838.7 4.8 collective-permute-start.2
  846.7 1389.6 %all-reduce.5.cloned.1.call-done = (f32[256,3,64]{2,1,0:T(4,128)}, f32[256,3,64]{2,1,0:T(4,128)}, f32[192,768]{1,0:T(8,128)}) async-done(((f32[256,3,64]{2,1,0:T(4,128)}, f32[256,3,64]{2,1,0:T(4,128)}, f32[192,768]{1,0:T(8,128)}), (f32[256,3,64]{2,1,0:T(4,128)}, f32[256,3,64]{2,1,0:T(4,128)}, f32[192,768]{1,0:T(8,128)})) %all-reduce.5.cloned.1.call-update) | async-done | bytes 983056
  2236.2 0.7 constant_dynamic-slice_fusion
  2238.6 0.8 fusion.22
  2239.8 0.8 copy.465
  (295 shorter events, 32.6 us)
Async XLA Ops:
  7.2 11.2 copy-start
  7.2 2229.0 %all-reduce.5.cloned.1.call-start = ((), (), s32[]{:S(2)}) async-start(), calls=%async_computation | async-start | bytes 3276800
  8.7 1.0 copy-start.3
  9.7 0.9 copy-start.1
  10.9 0.9 copy-start.43
  18.8 11.8 copy-start.2
  20.3 8.4 copy-start.25
  20.3 8.4 copy-start.27
  20.9 784.2 %collective-permute-start.1 = (bf16[16,3,64]{2,0,1:T(8,128)(2,1)}, bf16[16,3,64]{2,0,1:T(8,128)(2,1)}, u32[]{:S(2)}, u32[]{:S(2)}) collective-permute-start(bf16[16,3,64]{2,0,1:T(8,128)(2,1)} %copy.350), channel_id=1, source_target_pairs={{0,4},{4,0},{8,12},{12,8},{16,20},{20,16},{24,28},{28,24},{32,36},... | collective-permute-start | bytes 18440 | tf_op jit(solution)/shard_map/ppermute | solution.py:17
  28.7 770.8 %collective-permute-start = (bf16[16,3,64]{2,0,1:T(8,128)(2,1)}, bf16[16,3,64]{2,0,1:T(8,128)(2,1)}, u32[]{:S(2)}, u32[]{:S(2)}) collective-permute-start(bf16[16,3,64]{2,0,1:T(8,128)(2,1)} %copy.316), channel_id=1, source_target_pairs={{0,4},{4,0},{8,12},{12,8},{16,20},{20,16},{24,28},{28,24},{32,36},... | collective-permute-start | bytes 18440 | tf_op jit(solution)/shard_map/ppermute | solution.py:17
  33.0 1.3 copy-start.35
  34.3 2.1 copy-start.17
  34.3 2.1 copy-start.18
  38.5 375.1 %copy-start.15 = (bf16[2,3,64]{0,2,1:T(8,128)(2,1)}, bf16[2,3,64]{0,2,1:T(8,128)(2,1)S(1)}, u32[]{:S(2)}) copy-start(bf16[2,3,64]{0,2,1:T(8,128)(2,1)S(1)} %get-tuple-element.23) | copy-start | bytes 2308
  38.5 0.9 copy-start.24
  414.5 391.5 %copy-start.52 = (f32[3,2,256]{2,1,0:T(2,128)}, f32[3,2,256]{2,1,0:T(2,128)S(1)}, u32[]{:S(2)}) copy-start(f32[3,2,256]{2,1,0:T(2,128)S(1)} %get-tuple-element.59) | copy-start | bytes 18436
  418.0 0.8 copy-start.10
  419.1 0.8 copy-start.39
  794.4 11.7 copy-start.21
  794.4 15.5 copy-start.44
  796.1 3.5 copy-start.29
  796.1 9.0 copy-start.53
  796.5 13.5 copy-start.46
  796.6 10.0 copy-start.12
  797.7 1.9 copy-start.33
  800.5 4.6 copy-start.22
  803.8 6.2 copy-start.50
  804.2 0.9 copy-start.59
  804.9 5.1 copy-start.48
  805.1 1.0 copy-start.61
  812.6 6.9 copy-start.5
  819.5 0.8 copy-start.16
  820.3 0.8 copy-start.32
  821.1 0.8 copy-start.14
  821.1 0.8 copy-start.56
  822.8 0.8 copy-start.13
  824.6 0.8 copy-start.11
  828.6 2.2 copy-start.7
  828.6 16.9 collective-permute-start.3
  830.8 1.0 copy-start.38
  830.8 1.0 copy-start.42
  832.5 0.9 copy-start.34
  834.3 1.1 copy-start.6
  836.5 1.5 copy-start.19
  838.7 4.9 copy-start.63
  838.7 6.8 collective-permute-start.2
  2237.7 0.9 copy-start.8
  2238.6 1.2 copy-start.9
  (22 other events, 15.2 us)
Sparse Core Ops, SparseCore 0:
  836.6 1399.5 all-reduce.4
where the time goes:
time: 2250 us
  waiting for transfers between devices  1390 us (62%)
  blocking collectives  755 us (34%)
  local copies, waits for them, and re-layouts  43.5 us (2%)
    unnamed x2, waiting for transfers between devices  1390 us
    all_gather x1, blocking collectives, local(): lax.all_gather(far_value[0], 'seq', axis=0, tiled=True)  374 us
    all_gather x1, blocking collectives, local(): lax.all_gather(far_key[0], 'seq', axis=0, tiled=True)  374 us
  transfers between devices with their start and end apart: 5, of which 1 were waited for; matrix products, arithmetic and copies ran while one was open for 1% of the time, Pallas kernels for 0%

commit v1 on v0

--- a/solution.py
+++ b/solution.py
@@ -15,6 +15,15 @@
 
 def swapped(value, axis, distance):
     return lax.ppermute(value, axis, [(i, i ^ 1 << distance) for i in range(lax.axis_size(axis))])
+
+
+def exchange(pieces, axis):
+    return lax.all_to_all(pieces, axis, 0, 0, tiled=True)
+
+
+def gather_direct(value, axis):
+    pieces = jnp.broadcast_to(value.reshape(1, -1), (lax.axis_size(axis), value.size))
+    return exchange(pieces, axis)
 
 
 def pick_rows(source, seg_width, stride, shifts):
@@ -62,10 +71,11 @@
     pair_keys = jnp.concatenate([near_key, partner_key[None]], axis=1)
     pair_values = jnp.concatenate([near_value, partner_value[None]], axis=1)
     far_query, far_key, far_value, far_dout = selected[3]
-    all_key, all_value = (
-        lax.all_gather(far_key[0], "seq", axis=0, tiled=True),
-        lax.all_gather(far_value[0], "seq", axis=0, tiled=True),
-    )
+    far_count = far_key.shape[1]
+    far_pairs = gather_direct(jnp.stack([far_key[0], far_value[0]]), "seq")
+    far_pairs = far_pairs.reshape((-1, 2, far_count, heads_here, HEAD_DIM))
+    all_key = far_pairs[:, 0].reshape((-1, heads_here, HEAD_DIM))
+    all_value = far_pairs[:, 1].reshape((-1, heads_here, HEAD_DIM))
     levels = (
         selected[0],
         selected[1],
@@ -135,10 +145,13 @@
             value_part = jnp.einsum(
                 "shqk,sqhd->skhd", probs_low, level_dout, preferred_element_type=jnp.float32
             )
-            key_own, value_own = (
-                lax.psum_scatter(key_part[0], "seq", scatter_dimension=0, tiled=True),
-                lax.psum_scatter(value_part[0], "seq", scatter_dimension=0, tiled=True),
-            )
+            shards = lax.axis_size("seq")
+            parts = jnp.concatenate(
+                [key_part[0].reshape(shards, -1), value_part[0].reshape(shards, -1)], axis=1
+            )
+            own = jnp.sum(exchange(parts, "seq"), axis=0)
+            own = own.reshape((2, far_count, heads_here, HEAD_DIM))
+            key_own, value_own = own[0], own[1]
             grad_key = grad_key + spread_rows(key_own[None], stride, offsets)
             grad_value = grad_value + spread_rows(value_own[None], stride, offsets)
         else:
@@ -170,7 +183,10 @@
         )
         * WEIGHT_SCALE
     )
-    grad_weight = lax.psum(partial_weight, "seq")
+    pieces = partial_weight.astype(jnp.bfloat16).reshape(lax.axis_size("seq"), -1)
+    own_piece = jnp.sum(exchange(pieces, "seq").astype(jnp.float32), axis=0)
+    grad_weight = gather_direct(own_piece.astype(jnp.bfloat16), "seq")
+    grad_weight = grad_weight.astype(jnp.float32).reshape(partial_weight.shape)
     return (grad_queries, grad_keys, grad_values, grad_weight)
 
 

time: 2250 us -> 204 us (0.09)
  the two profiles are of different devices: /device:TPU:16 before, /device:TPU:2 now
where the time goes in v1:
time: 204 us; the launch traced here: 202 us
  blocking collectives  54.7 us (27%)
  local copies, waits for them, and re-layouts  50.2 us (25%)
  starting transfers between devices  49.3 us (24%)
  other arithmetic  22.4 us (11%)
  matrix products  18.5 us (9%)
  waiting for transfers between devices  4.89 us (2%)
    all_to_all x2, blocking collectives, exchange(): return lax.all_to_all(pieces, axis, 0, 0, tiled=True)  48.2 us
    all_to_all x2, starting transfers between devices, exchange(): return lax.all_to_all(pieces, axis, 0, 0, tiled=True)  34 us
    ppermute x4, starting transfers between devices, swapped(): lax.ppermute(value, axis, [(i, i ^ 1 << distance) for i in range(lax.axis...  15.3 us
    mul x73, local copies, waits for them, and re-layouts, spread_rows(): placed = jnp.expand_dims(picked, 2) * chooser  14.6 us
    unnamed x137, local copies, waits for them, and re-layouts  13.6 us
    reduce_sum x15, other arithmetic, pick_rows(): return jnp.sum(shaped * chooser, axis=2)  6.77 us
    all_gather x1, blocking collectives, local(): full_grad = lax.all_gather(grad_out, 'dp', axis=0, tiled=True)  6.53 us
    dot_general x4, matrix products, local(): jnp.einsum('shqk,sqhd->skhd', probs_low, level_dout, preferred_element_ty...  5.33 us
  transfers between devices with their start and end apart: 6, of which 1 were waited for; matrix products, arithmetic and copies ran while one was open for 17% of the time, Pallas kernels for 0%

profile of v1, /device:TPU:2, one launch (start us, length us, event | category | flops | bytes accessed | tf_op | source)
XLA Modules:
  0.0 202.0 jit_solution(18068020716428601424)
XLA Ops:
  0.6 1.2 and_select_fusion.1
  2.6 1.0 copy.563
  3.8 0.8 copy-done.1
  5.8 6.5 %all_gather.3 = bf16[768,256]{1,0:T(8,128)(2,1)S(1)} all-gather(bf16[192,256]{1,0:T(8,128)(2,1)S(1)} %copy-done.41), channel_id=1, replica_groups=mesh['seq'=128,'dp'=4] {'dp'}, dimensions={0}, use_global_device_ids=true | all-gather | bytes 491520 | tf_op jit(solution)/shard_map/all_gather | solution.py:56
  12.8 1.4 multiply_reduce_fusion
  14.9 4.5 %collective-permute-start.1 = (bf16[16,3,64]{2,0,1:T(8,128)(2,1)}, bf16[16,3,64]{2,0,1:T(8,128)(2,1)}, u32[]{:S(2)}, u32[]{:S(2)}) collective-permute-start(bf16[16,3,64]{2,0,1:T(8,128)(2,1)} %copy.608), channel_id=1, source_target_pairs={{0,4},{4,0},{8,12},{12,8},{16,20},{20,16},{24,28},{28,24},{32,36},... | collective-permute-start | bytes 18440 | tf_op jit(solution)/shard_map/ppermute | solution.py:17
  20.0 2.2 %collective-permute-start = (bf16[16,3,64]{2,0,1:T(8,128)(2,1)}, bf16[16,3,64]{2,0,1:T(8,128)(2,1)}, u32[]{:S(2)}, u32[]{:S(2)}) collective-permute-start(bf16[16,3,64]{2,0,1:T(8,128)(2,1)} %copy.572), channel_id=1, source_target_pairs={{0,4},{4,0},{8,12},{12,8},{16,20},{20,16},{24,28},{28,24},{32,36},... | collective-permute-start | bytes 18440 | tf_op jit(solution)/shard_map/ppermute | solution.py:17
  23.0 1.0 multiply_reduce_fusion.8
  25.1 1.8 reduce.57
  27.6 19.6 %all-to-all-start = ((bf16[128,2,384]{2,1,0:T(2,128)(2,1)}), bf16[128,2,384]{2,1,0:T(2,128)(2,1)S(1)}, u32[]{:S(2)}, u32[]{:S(2)}) async-start(bf16[128,2,384]{2,1,0:T(2,128)(2,1)} %reshape.1908), calls=%async_computation | async-start | bytes 393216 | tf_op jit(solution)/shard_map/all_to_all | solution.py:21
  51.1 1.6 multiply_reduce_fusion.7
  52.7 1.0 copy.566
  60.9 0.9 fusion.94
  69.6 0.9 convolution_bitcast_fusion.9
  72.7 0.8 mul.1343
  73.6 0.8 copy.606
  74.4 0.8 mul.1331
  75.2 0.8 copy.614
  76.1 1.7 fusion.33
  77.9 1.5 fusion.31
  79.4 1.3 reshape.1902
  80.7 1.4 reshape.1901
  82.0 1.7 convolution_bitcast_fusion
  84.4 1.3 copy.639
  85.8 1.3 copy.640
  87.1 1.1 fusion.8
  89.0 0.8 convolution_bitcast_fusion.1
  89.9 0.9 reshape.1900
  90.7 1.6 convolution_bitcast_fusion.2
  93.1 0.8 multiply_reduce_fusion.16
  93.9 1.1 fusion.4
  96.8 0.9 fusion.96
  97.7 0.9 fusion.97
  99.5 4.3 %collective-permute-start.3 = (f32[16,3,64]{2,0,1:T(8,128)}, f32[16,3,64]{2,0,1:T(8,128)}, u32[]{:S(2)}, u32[]{:S(2)}) collective-permute-start(f32[16,3,64]{2,0,1:T(8,128)} %slice_bitcast_fusion), channel_id=1, source_target_pairs={{0,4},{4,0},{8,12},{12,8},{16,20},{20,16},{24,28},{28,24},{32,36},... | collective-permute-start | bytes 36872 | tf_op jit(solution)/shard_map/ppermute | solution.py:17
  104.9 0.8 fusion.6
  106.5 1.2 copy.655
  107.6 14.4 %all-to-all-start.1 = ((f32[128,1,768]{2,1,0:T(1,128)}), f32[128,1,768]{2,1,0:T(1,128)S(1)}, u32[]{:S(2)}, u32[]{:S(2)}) async-start(f32[128,1,768]{2,1,0:T(1,128)} %copy.655), calls=%async_computation.1 | async-start | bytes 786432 | tf_op jit(solution)/shard_map/all_to_all | solution.py:21
  122.8 0.8 convolution_bitcast_fusion.8
  125.6 4.3 %collective-permute-start.2 = (f32[16,3,64]{2,0,1:T(8,128)}, f32[16,3,64]{2,0,1:T(8,128)S(1)}, u32[]{:S(2)}, u32[]{:S(2)}) collective-permute-start(f32[16,3,64]{2,0,1:T(8,128)} %slice_bitcast_fusion.1), channel_id=1, source_target_pairs={{0,4},{4,0},{8,12},{12,8},{16,20},{20,16},{24,28},{28,24},{32,36},... | collective-permute-start | bytes 36872 | tf_op jit(solution)/shard_map/ppermute | solution.py:17
  133.9 0.8 copy.650
  135.2 4.9 %all-to-all-done.1 = f32[128,1,768]{2,1,0:T(1,128)S(1)} async-done(((f32[128,1,768]{2,1,0:T(1,128)}), f32[128,1,768]{2,1,0:T(1,128)S(1)}, u32[]{:S(2)}, u32[]{:S(2)}) %all-to-all-start.1) | async-done | bytes 393248 | tf_op jit(solution)/shard_map/all_to_all | solution.py:21
  142.3 0.9 fusion.27
  143.7 2.4 %reduce.58 = bf16[128,1152]{1,0:T(8,128)(2,1)S(1)} reduce(bf16[128,1,1152]{2,1,0:T(2,128)(2,1)S(1)} %all_to_all.26, bf16[]{:T(256)} %broadcast.978), dimensions={1}, to_apply=%all_to_all.26.reduce_sub_computation | reduce | bytes 589826 | tf_op jit(solution)/shard_map/all_to_all | solution.py:21
  146.5 25.3 %all_to_all.31 = bf16[128,2,576]{2,1,0:T(2,128)(2,1)S(1)} all-to-all(bf16[128,2,576]{2,1,0:T(2,128)(2,1)S(1)} %reshape.1910), channel_id=1, replica_groups=mesh['seq'=128,'dp'=4] {'seq'}, dimensions={0} | all-to-all | bytes 589824 | tf_op jit(solution)/shard_map/all_to_all | solution.py:21
  173.2 2.4 %reduce.59 = bf16[128,1152]{1,0:T(8,128)(2,1)S(1)} reduce(bf16[128,1,1152]{2,1,0:T(2,128)(2,1)S(1)} %broadcast_in_dim.20, bf16[]{:T(256)} %broadcast.978), dimensions={1}, to_apply=%broadcast_in_dim.20.reduce_sub_computation | reduce | bytes 589826 | tf_op jit(solution)/shard_map/broadcast_in_dim | solution.py:25
  176.0 22.9 %all_to_all.32 = bf16[128,2,576]{2,1,0:T(2,128)(2,1)S(1)} all-to-all(bf16[128,2,576]{2,1,0:T(2,128)(2,1)S(1)} %reshape.1912), channel_id=1, replica_groups=mesh['seq'=128,'dp'=4] {'seq'}, dimensions={0} | all-to-all | bytes 589824 | tf_op jit(solution)/shard_map/all_to_all | solution.py:21
  199.3 1.6 convert_reduce_fusion
  201.0 1.0 reshape.1906
  (321 shorter events, 45.7 us)
Async XLA Ops:
  0.6 11.7 %copy-start = (bf16[192,768]{1,0:T(8,128)(2,1)S(1)}, bf16[192,768]{1,0:T(8,128)(2,1)}, u32[]{:S(2)}) copy-start(bf16[192,768]{1,0:T(8,128)(2,1)} %param.10) | copy-start | bytes 884740
  2.6 1.0 copy-start.3
  3.7 0.9 copy-start.1
  4.9 0.9 copy-start.41
  12.8 9.4 %copy-start.2 = (bf16[192,256]{1,0:T(8,128)(2,1)S(1)}, bf16[192,256]{1,0:T(8,128)(2,1)}, u32[]{:S(2)}) copy-start(bf16[192,256]{1,0:T(8,128)(2,1)} %param.6) | copy-start | bytes 294916
  14.9 54.7 %collective-permute-start.1 = (bf16[16,3,64]{2,0,1:T(8,128)(2,1)}, bf16[16,3,64]{2,0,1:T(8,128)(2,1)}, u32[]{:S(2)}, u32[]{:S(2)}) collective-permute-start(bf16[16,3,64]{2,0,1:T(8,128)(2,1)} %copy.608), channel_id=1, source_target_pairs={{0,4},{4,0},{8,12},{12,8},{16,20},{20,16},{24,28},{28,24},{32,36},... | collective-permute-start | bytes 18440 | tf_op jit(solution)/shard_map/ppermute | solution.py:17
  20.0 40.9 %collective-permute-start = (bf16[16,3,64]{2,0,1:T(8,128)(2,1)}, bf16[16,3,64]{2,0,1:T(8,128)(2,1)}, u32[]{:S(2)}, u32[]{:S(2)}) collective-permute-start(bf16[16,3,64]{2,0,1:T(8,128)(2,1)} %copy.572), channel_id=1, source_target_pairs={{0,4},{4,0},{8,12},{12,8},{16,20},{20,16},{24,28},{28,24},{32,36},... | collective-permute-start | bytes 18440 | tf_op jit(solution)/shard_map/ppermute | solution.py:17
  24.0 38.9 %copy-start.19 = (bf16[2,3,64]{0,2,1:T(8,128)(2,1)}, bf16[2,3,64]{0,2,1:T(8,128)(2,1)S(1)}, u32[]{:S(2)}) copy-start(bf16[2,3,64]{0,2,1:T(8,128)(2,1)S(1)} %get-tuple-element.31) | copy-start | bytes 2308
  27.6 34.5 %all-to-all-start = ((bf16[128,2,384]{2,1,0:T(2,128)(2,1)}), bf16[128,2,384]{2,1,0:T(2,128)(2,1)S(1)}, u32[]{:S(2)}, u32[]{:S(2)}) async-start(bf16[128,2,384]{2,1,0:T(2,128)(2,1)} %reshape.1908), calls=%async_computation | async-start | bytes 393216 | tf_op jit(solution)/shard_map/all_to_all | solution.py:21
  48.2 1.3 copy-start.33
  54.8 1.5 copy-start.38
  58.1 2.8 %copy-start.28 = (bf16[16,3,64]{2,0,1:T(8,128)(2,1)}, bf16[16,3,64]{2,0,1:T(8,128)(2,1)S(1)}, u32[]{:S(2)}) copy-start(bf16[16,3,64]{2,0,1:T(8,128)(2,1)S(1)} %copy.715) | copy-start | bytes 18436
  58.1 11.4 %copy-start.45 = (bf16[16,3,64]{2,0,1:T(8,128)(2,1)}, bf16[16,3,64]{2,0,1:T(8,128)(2,1)S(1)}, u32[]{:S(2)}) copy-start(bf16[16,3,64]{2,0,1:T(8,128)(2,1)S(1)} %copy.714) | copy-start | bytes 18436
  58.4 0.9 copy-start.15
  59.1 0.9 copy-start.14
  59.4 12.3 %copy-start.18 = (bf16[128,3,64]{0,2,1:T(8,128)(2,1)}, bf16[128,3,64]{0,2,1:T(8,128)(2,1)S(1)}, u32[]{:S(2)}) copy-start(bf16[128,3,64]{0,2,1:T(8,128)(2,1)S(1)} %copy.602) | copy-start | bytes 147460
  61.8 7.8 %copy-start.23 = (f32[3,16,32]{2,1,0:T(8,128)}, f32[3,16,32]{2,1,0:T(8,128)S(1)}, u32[]{:S(2)}) copy-start(f32[3,16,32]{2,1,0:T(8,128)S(1)} %get-tuple-element.71) | copy-start | bytes 18436
  63.2 7.9 %copy-start.44 = (f32[3,2,256]{2,1,0:T(2,128)}, f32[3,2,256]{2,1,0:T(2,128)S(1)}, u32[]{:S(2)}) copy-start(f32[3,2,256]{2,1,0:T(2,128)S(1)} %get-tuple-element.69) | copy-start | bytes 18436
  67.9 1.7 copy-start.61
  68.4 2.7 %copy-start.25 = (bf16[128,1,2,3,64]{4,2,0,3,1:T(2,128)(2,1)}, bf16[128,1,2,3,64]{4,2,0,3,1:T(2,128)(2,1)S(1)}, u32[]{:S(2)}) copy-start(bf16[128,1,2,3,64]{4,2,0,3,1:T(2,128)(2,1)S(1)} %copy.615) | copy-start | bytes 294916
  69.5 1.6 copy-start.63
  76.1 1.7 copy-start.4
  76.1 1.7 copy-start.5
  76.1 1.7 copy-start.6
  76.1 1.8 copy-start.42
  76.1 1.8 copy-start.49
  76.1 1.8 copy-start.51
  76.1 1.8 copy-start.53
  82.0 1.7 copy-start.39
  82.0 1.7 copy-start.60
  97.7 6.1 %copy-start.7 = (f32[1,256,3,64]{1,3,2,0:T(8,128)S(1)}, f32[1,256,3,64]{1,3,2,0:T(8,128)}, u32[]{:S(2)}) copy-start(f32[1,256,3,64]{1,3,2,0:T(8,128)} %convolution_bitcast_fusion) | copy-start | bytes 589828
  99.5 32.5 %collective-permute-start.3 = (f32[16,3,64]{2,0,1:T(8,128)}, f32[16,3,64]{2,0,1:T(8,128)}, u32[]{:S(2)}, u32[]{:S(2)}) collective-permute-start(f32[16,3,64]{2,0,1:T(8,128)} %slice_bitcast_fusion), channel_id=1, source_target_pairs={{0,4},{4,0},{8,12},{12,8},{16,20},{20,16},{24,28},{28,24},{32,36},... | collective-permute-start | bytes 36872 | tf_op jit(solution)/shard_map/ppermute | solution.py:17
  104.0 1.7 copy-start.32
  104.8 1.1 copy-start.8
  105.9 16.1 %copy-start.26 = (f32[1,32,3,64]{3,1,2,0:T(8,128)}, f32[1,32,3,64]{3,1,2,0:T(8,128)S(1)}, u32[]{:S(2)}) copy-start(f32[1,32,3,64]{3,1,2,0:T(8,128)S(1)} %convolution_bitcast_fusion.7) | copy-start | bytes 73732
  107.6 32.4 %all-to-all-start.1 = ((f32[128,1,768]{2,1,0:T(1,128)}), f32[128,1,768]{2,1,0:T(1,128)S(1)}, u32[]{:S(2)}, u32[]{:S(2)}) async-start(f32[128,1,768]{2,1,0:T(1,128)} %copy.655), calls=%async_computation.1 | async-start | bytes 786432 | tf_op jit(solution)/shard_map/all_to_all | solution.py:21
  123.9 0.9 copy-start.21
  125.6 4.3 %copy-start.59 = (f32[2,3,64]{2,0,1:T(2,128)S(1)}, f32[2,3,64]{2,0,1:T(2,128)}, u32[]{:S(2)}) copy-start(f32[2,3,64]{2,0,1:T(2,128)} %convolution_bitcast_fusion.10) | copy-start | bytes 4612
  125.6 7.8 %collective-permute-start.2 = (f32[16,3,64]{2,0,1:T(8,128)}, f32[16,3,64]{2,0,1:T(8,128)S(1)}, u32[]{:S(2)}, u32[]{:S(2)}) collective-permute-start(f32[16,3,64]{2,0,1:T(8,128)} %slice_bitcast_fusion.1), channel_id=1, source_target_pairs={{0,4},{4,0},{8,12},{12,8},{16,20},{20,16},{24,28},{28,24},{32,36},... | collective-permute-start | bytes 36872 | tf_op jit(solution)/shard_map/ppermute | solution.py:17
  132.0 1.5 copy-start.27
  140.1 1.6 copy-start.13
  140.7 1.0 copy-start.12
  140.8 0.9 copy-start.50
  140.8 0.9 copy-start.52
  140.8 0.9 copy-start.54
  141.1 1.0 copy-start.10
  141.1 1.0 copy-start.11
  141.3 1.0 copy-start.9
  (23 other events, 17.0 us)

commit v2 on v0

v2 whole, which is shorter than its diff:
```python
import jax
import jax.numpy as jnp
from jax import lax
from jax.experimental import pallas as pl
from jax.experimental.pallas import tpu as pltpu
from jax.sharding import Mesh
from jax.sharding import PartitionSpec as P

HEAD_DIM = 64
TOKENS_HERE = 256
RB = 2
RC = 16
RE = 128
NEAR = TOKENS_HERE // RC
SCORE_SCALE = HEAD_DIM ** (-0.5)
WEIGHT_SCALE = 0.03125

PLANES = 4
LANES = 128
GAP = 16
SLOT = HEAD_DIM + GAP

F32 = jnp.float32
BF16 = jnp.bfloat16


def mm(left, right, left_dim, right_dim):
    return lax.dot_general(
        left, right, (((left_dim,), (right_dim,)), ((), ())), preferred_element_type=F32
    )


def iota(shape, dim):
    return lax.broadcasted_iota(jnp.int32, shape, dim)


def one_hot(condition):
    return jnp.where(condition, 1.0, 0.0).astype(BF16)


def same_class(position, offset, stride):
    return (position & (stride - 1)) == (offset & (stride - 1))


def near_chooser(offset):
    shape = (NEAR, TOKENS_HERE)
    return one_hot(iota(shape, 1) == RC * iota(shape, 0) + (offset & (RC - 1)))


def far_chooser(offset, pair):
    shape = (GAP, TOKENS_HERE)
    row = iota(shape, 0)
    hit = iota(shape, 1) == RE * (row & 1) + offset
    return one_hot(hit & ((row >> 1) == pair))


def split3(value):
    high = value.astype(BF16).astype(F32)
    rest = value - high
    middle = rest.astype(BF16).astype(F32)
    return high, middle, rest - middle


def lay_stats(shape, dim, start, values):
    place = iota(shape, dim) - start
    out = jnp.zeros(shape, F32)
    for index, value in enumerate(values):
        for part_index, part in enumerate(split3(value)):
            out = jnp.where(place == 3 * index + part_index, part, out)
    return out


def take_stat(rows, index):
    place = iota(rows.shape, 1) - HEAD_DIM - 3 * index
    return jnp.sum(jnp.where((place >= 0) & (place < 3), rows, 0.0), axis=1, keepdims=True)


def left_half(rows):
    return jnp.where(iota(rows.shape, 1) < HEAD_DIM, rows.astype(F32), 0.0).astype(BF16)


def right_half(rows):
    return jnp.where(iota(rows.shape, 1) >= HEAD_DIM, rows.astype(F32), 0.0).astype(BF16)


def near_kernel(offset_ref, key_ref, value_ref, near_ref):
    for head in range(key_ref.shape[0] // HEAD_DIM):
        rows = slice(head * HEAD_DIM, (head + 1) * HEAD_DIM)
        both = jnp.concatenate([key_ref[rows], value_ref[rows]], axis=0)
        picked = mm(near_chooser(offset_ref[head]), both, 1, 1)
        near_ref[head * NEAR : (head + 1) * NEAR, :] = picked.astype(BF16)


def local_kernel(
    offset_ref,
    query_ref,
    key_ref,
    value_ref,
    grad_ref,
    weight_ref,
    near_ref,
    slots_ref,
    back_ref,
    mine_ref,
    grad_query_ref,
    grad_key_ref,
    grad_value_ref,
):
    heads = query_ref.shape[0] // HEAD_DIM
    tiles = grad_ref.shape[0] // LANES
    grad = grad_ref[...]
    dout = mm(weight_ref[...], grad, 1, 0).astype(BF16)
    blank = jnp.zeros((HEAD_DIM, TOKENS_HERE), BF16)
    key_pos = iota((TOKENS_HERE, TOKENS_HERE), 0)
    query_pos = iota((TOKENS_HERE, TOKENS_HERE), 1)
    query_row = iota((1, TOKENS_HERE), 1)
    partner_far = jnp.zeros((GAP, LANES), F32)
    for head in range(heads):
        offset = offset_ref[head]
        rows = slice(head * HEAD_DIM, (head + 1) * HEAD_DIM)
        near_rows = slice(head * NEAR, (head + 1) * NEAR)
        query, key, value = query_ref[rows], key_ref[rows], value_ref[rows]
        near = near_ref[near_rows]
        dout_head = dout[rows]
        query_over = jnp.concatenate([query, blank], axis=0)
        dout_under = jnp.concatenate([blank, dout_head], axis=0)
        count = 1.0 + jnp.where(
            same_class(key_pos, offset, RB) & same_class(query_pos, offset, RB), 1.0, 0.0
        )
        count = count + jnp.where(
            same_class(key_pos, offset, RC) & same_class(query_pos, offset, RC), 1.0, 0.0
        )
        in_near = same_class(query_row, offset, RC)
        in_far = same_class(query_row, offset, RE)

        scores = mm(key, query, 0, 0) * SCORE_SCALE
        near_scores = mm(near, query_over, 1, 0) * SCORE_SCALE
        near_max = jnp.max(near_scores, axis=0, keepdims=True)
        peak = jnp.max(scores, axis=0, keepdims=True)
        peak = jnp.where(in_near, jnp.maximum(peak, near_max), peak)
        mass = count * jnp.exp(scores - peak)
        near_mass = jnp.where(in_near, jnp.exp(near_scores - peak), 0.0)
        total = jnp.sum(mass, axis=0, keepdims=True) + jnp.sum(near_mass, axis=0, keepdims=True)
        log_mass = peak + jnp.log(total)
        inverse = 1.0 / total
        probs = mass * inverse
        near_probs = near_mass * inverse
        probs_low = probs.astype(BF16)
        near_low = near_probs.astype(BF16)
        attended = mm(value, probs_low, 1, 0) + mm(near, near_low, 0, 0)[HEAD_DIM:]
        delta = jnp.sum(dout_head.astype(F32) * attended, axis=0, keepdims=True)

        grad_probs = mm(value, dout_head, 0, 0)
        near_grad_probs = mm(near, dout_under, 1, 0)
        grad_scores = jnp.where(in_far, 0.0, probs * (grad_probs - delta)).astype(BF16)
        near_grad_scores = jnp.where(in_far, 0.0, near_probs * (near_grad_probs - delta)).astype(
            BF16
        )
        probs_kept = jnp.where(in_far, 0.0, probs).astype(BF16)
        near_kept = jnp.where(in_far, 0.0, near_probs).astype(BF16)
        grad_query_ref[rows] = (
            mm(key, grad_scores, 1, 0) + mm(near, near_grad_scores, 0, 0)[:HEAD_DIM]
        )
        grad_key_ref[rows] = mm(query, grad_scores, 1, 1)
        grad_value_ref[rows] = mm(dout_head, probs_kept, 1, 1)
        back = mm(near_grad_scores, query_over, 1, 1) + mm(near_kept, dout_under, 1, 1)
        back_ref[near_rows] = back.astype(BF16)

        attended_kept = jnp.where(in_far, 0.0, attended).astype(BF16)
        weight_part = mm(attended_kept, grad, 1, 1) * WEIGHT_SCALE
        query_key = jnp.concatenate([query, key], axis=0)
        value_dout = jnp.concatenate([value, dout_head], axis=0)
        stats = lay_stats((HEAD_DIM, TOKENS_HERE), 0, 0, (log_mass, delta))
        attended_stats = jnp.concatenate([attended.astype(BF16), stats.astype(BF16)], axis=0)
        mine = mm(far_chooser(offset, 0), query_key, 1, 1)
        mine = mine + mm(far_chooser(offset, 1), value_dout, 1, 1)
        mine = mine + mm(far_chooser(offset, 2), attended_stats, 1, 1)
        mine_ref[head * GAP : (head + 1) * GAP] = mine.astype(BF16)
        far_grad = mm(far_chooser(offset, 3), grad, 1, 1)
        for tile in range(tiles):
            lanes = slice(tile * LANES, (tile + 1) * LANES)
            slots_ref[head * tiles + tile, :HEAD_DIM] = weight_part[:, lanes].astype(BF16)
            slots_ref[head * tiles + tile, HEAD_DIM:] = (mine + far_grad[:, lanes]).astype(BF16)
        query_dout = jnp.concatenate([query, dout_head], axis=0)
        partner_far = partner_far + mm(far_chooser(offset, head), query_dout, 1, 1)
    back_ref[heads * NEAR :] = partner_far.astype(BF16)
    rest = slots_ref.shape[0] - heads * tiles
    slots_ref[heads * tiles :] = jnp.zeros((rest,) + slots_ref.shape[1:], BF16)


def merge_kernel(slots_ref, merged_ref, far_ref):
    sources = slots_ref.shape[0]
    total = slots_ref[0, :HEAD_DIM].astype(F32)
    for source in range(1, sources):
        total = total + slots_ref[source, :HEAD_DIM].astype(F32)
    half = GAP // 2
    for source in range(sources):
        block = slots_ref[source, HEAD_DIM:].astype(F32)
        far_ref[source * half : (source + 1) * half] = block[:half]
    pieces = [far_ref[pl.ds(kind, sources, stride=half), :] for kind in range(half)]
    full = jnp.concatenate([total] + pieces, axis=0).astype(BF16)
    for plane in range(PLANES):
        merged_ref[plane] = full


def far_kernel(plane_ref, merged_ref, slots_ref, first_ref, second_ref):
    sources = slots_ref.shape[0]
    width = 2 * sources
    count = PLANES * width

    def kind(index):
        start = HEAD_DIM + index * width
        return merged_ref[:, start : start + width, :].reshape(count, LANES)

    query_key, value_dout, attended_stats, far_grad = (kind(index) for index in range(4))
    shape = (LANES, HEAD_DIM)
    lower = one_hot(iota(shape, 0) == iota(shape, 1) + HEAD_DIM)
    query, value = query_key[:, :HEAD_DIM], value_dout[:, :HEAD_DIM]
    key, dout = (mm(both, lower, 1, 0).astype(BF16) for both in (query_key, value_dout))
    local_attended = attended_stats[:, :HEAD_DIM].astype(F32)
    stats = attended_stats.astype(F32)
    local_mass = take_stat(stats, 0)

    scores = mm(query, key, 1, 1) * SCORE_SCALE
    peak = jnp.maximum(jnp.max(scores, axis=1, keepdims=True), local_mass)
    mass = jnp.exp(scores - peak)
    local_part = jnp.exp(local_mass - peak)
    total = jnp.sum(mass, axis=1, keepdims=True) + local_part
    normalizer = peak + jnp.log(total)
    inverse = 1.0 / total
    probs = mass * inverse
    probs_low = probs.astype(BF16)
    attended = local_part * inverse * local_attended + mm(probs_low, value, 1, 0)
    delta = jnp.sum(dout.astype(F32) * attended, axis=1, keepdims=True)
    grad_probs = mm(dout, value, 1, 1)
    grad_scores = (probs * (grad_probs - delta)).astype(BF16)
    grad_query = mm(grad_scores, key, 1, 0).astype(BF16)
    grad_key = mm(grad_scores, query, 0, 0).astype(BF16)
    grad_value = mm(probs_low, dout, 0, 0).astype(BF16)
    weight_part = mm(attended.astype(BF16), far_grad, 0, 0) * WEIGHT_SCALE
    for plane in range(PLANES):
        weight_part = weight_part + merged_ref[plane, :HEAD_DIM].astype(F32)

    def other_plane(column):
        blocks = [column[(p ^ 1) * width : ((p ^ 1) + 1) * width] for p in range(PLANES)]
        return jnp.concatenate(blocks, axis=0)

    shape = (HEAD_DIM, LANES)
    to_left = one_hot(iota(shape, 0) == iota(shape, 1))
    to_right = one_hot(iota(shape, 0) + HEAD_DIM == iota(shape, 1))
    both_stats = (normalizer, delta, other_plane(normalizer), other_plane(delta))
    first_ref[...] = mm(grad_value, to_left, 1, 0) + lay_stats(
        (count, LANES), 1, HEAD_DIM, both_stats
    )
    second_ref[...] = mm(grad_query, to_left, 1, 0) + mm(grad_key, to_right, 1, 0)
    own = pl.ds(pl.multiple_of(plane_ref[0] * width, width), width)
    shape = (sources * GAP, width)
    row, column = iota(shape, 0), iota(shape, 1)
    same = (row // GAP) == (column % sources)
    slot_row, pair = row % GAP, column // sources
    placed = mm(one_hot(same & (slot_row == pair)), first_ref[own, :].astype(BF16), 1, 0)
    placed = placed + mm(
        one_hot(same & (slot_row == pair + 2)), second_ref[own, :].astype(BF16), 1, 0
    )
    slots_ref[:, HEAD_DIM:, :] = placed.astype(BF16).reshape(sources, GAP, LANES)
    weight_low = weight_part.astype(BF16)
    for source in range(sources):
        slots_ref[source, :HEAD_DIM] = weight_low


def final_kernel(
    offset_ref,
    query_ref,
    key_ref,
    value_ref,
    near_ref,
    back_ref,
    mine_ref,
    local_query_ref,
    local_key_ref,
    local_value_ref,
    slots_ref,
    grad_query_ref,
    grad_key_ref,
    grad_value_ref,
    grad_weight_ref,
):
    heads = query_ref.shape[0] // HEAD_DIM
    tiles = grad_weight_ref.shape[1] // LANES
    blank = jnp.zeros((HEAD_DIM, TOKENS_HERE), BF16)
    key_row = iota((1, TOKENS_HERE), 1)
    shape = (GAP, GAP)
    row, column = iota(shape, 0), iota(shape, 1)
    valid = iota((GAP, 1), 0) < 2
    partner_far = back_ref[heads * NEAR :]
    for head in range(heads):
        offset = offset_ref[head]
        rows = slice(head * HEAD_DIM, (head + 1) * HEAD_DIM)
        near_rows = slice(head * NEAR, (head + 1) * NEAR)
        query, key, value = query_ref[rows], key_ref[rows], value_ref[rows]
        near = near_ref[near_rows]
        mine = mine_ref[head * GAP : (head + 1) * GAP]
        returned = slots_ref[head * tiles, HEAD_DIM:]
        stats = returned.astype(F32)
        normalizer, delta, far_normalizer, far_delta = (take_stat(stats, i) for i in range(4))
        key_over = jnp.concatenate([key, blank], axis=0)
        value_under = jnp.concatenate([blank, value], axis=0)
        near_key, near_value = left_half(near), right_half(near)

        count = 1.0 + jnp.where(same_class(key_row, offset, RB), 1.0, 0.0)
        count = count + jnp.where(same_class(key_row, offset, RC), 1.0, 0.0)
        value_dout = mm(one_hot((row < 2) & (column == row + 2)), mine, 1, 0).astype(BF16)
        scores = mm(mine, key_over, 1, 0) * SCORE_SCALE
        probs = jnp.where(valid, count * jnp.exp(scores - normalizer), 0.0)
        grad_scores = (probs * (mm(value_dout, value_under, 1, 0) - delta)).astype(BF16)
        scores = mm(mine, near_key, 1, 1) * SCORE_SCALE
        near_probs = jnp.where(valid, jnp.exp(scores - normalizer), 0.0)
        near_grad_scores = (near_probs * (mm(value_dout, near_value, 1, 1) - delta)).astype(BF16)
        far_query = mm(grad_scores, key_over, 1, 1) + mm(near_grad_scores, near_key, 1, 0)
        far_query = far_query.astype(BF16)

        query_dout = one_hot((row < 2) & (column == row + 2 * head))
        query_dout = mm(query_dout, partner_far, 1, 0).astype(BF16)
        near_choice = near_chooser(offset)
        own_near = mm(near_choice, jnp.concatenate([key, value], axis=0), 1, 1).astype(BF16)
        scores = mm(query_dout, left_half(own_near), 1, 1) * SCORE_SCALE
        far_probs = jnp.where(valid, jnp.exp(scores - far_normalizer), 0.0)
        far_grad_probs = mm(query_dout, right_half(own_near), 1, 1)
        far_grad_scores = (far_probs * (far_grad_probs - far_delta)).astype(BF16)
        near_grad = left_half(mm(far_grad_scores, query_dout, 0, 0)).astype(F32)
        near_grad = near_grad + right_half(mm(far_probs.astype(BF16), query_dout, 0, 0)).astype(F32)
        near_grad = (near_grad + back_ref[near_rows].astype(F32)).astype(BF16)

        first_choice, second_choice = far_chooser(offset, 0), far_chooser(offset, 1)
        value_spread = mm(returned, first_choice, 0, 0)
        query_key_spread = mm(returned, second_choice, 0, 0)
        near_spread = mm(near_grad, near_choice, 0, 0)
        grad_query = local_query_ref[rows] + query_key_spread[:HEAD_DIM]
        grad_query = grad_query + mm(far_query, first_choice, 0, 0)[:HEAD_DIM]
        grad_key = local_key_ref[rows] + query_key_spread[HEAD_DIM:] + near_spread[:HEAD_DIM]
        grad_key = grad_key + mm(mine, grad_scores, 0, 0)[:HEAD_DIM]
        grad_value = local_value_ref[rows] + value_spread[:HEAD_DIM] + near_spread[HEAD_DIM:]
        grad_value = grad_value + mm(value_dout, probs.astype(BF16), 0, 0)[HEAD_DIM:]
        grad_query_ref[rows] = (grad_query * SCORE_SCALE).astype(BF16)
        grad_key_ref[rows] = (grad_key * SCORE_SCALE).astype(BF16)
        grad_value_ref[rows] = grad_value.astype(BF16)
        for tile in range(tiles):
            lanes = slice(tile * LANES, (tile + 1) * LANES)
            grad_weight_ref[rows, lanes] = slots_ref[head * tiles + tile, :HEAD_DIM].astype(F32)


def call(kernel, outs, scalars, arrays, scratch=()):
    specs = [pl.BlockSpec(memory_space=pltpu.SMEM)] * scalars
    specs = specs + [pl.BlockSpec(memory_space=pltpu.VMEM)] * (len(arrays) - scalars)
    shapes = [jax.ShapeDtypeStruct(shape, dtype) for shape, dtype in outs]
    return pl.pallas_call(
        kernel,
        out_shape=shapes,
        in_specs=specs,
        out_specs=[pl.BlockSpec(memory_space=pltpu.VMEM)] * len(shapes),
        scratch_shapes=list(scratch),
        compiler_params=pltpu.CompilerParams(vmem_limit_bytes=40 * 1024 * 1024),
        name=kernel.__name__,
    )(*arrays)


def local(queries, keys, values, grad_out, out_weight, offsets):
    features = queries.shape[0]
    model = out_weight.shape[1]
    heads = offsets.shape[0]
    sources = lax.axis_size("xz")
    rows = heads * NEAR
    other = [(i, i ^ 1) for i in range(PLANES)]

    (near_own,) = call(near_kernel, [((rows, LANES), BF16)], 1, (offsets, keys, values))
    near = lax.ppermute(near_own, "yh", other)
    full_grad = lax.all_gather(grad_out, "dp", axis=0, tiled=True)
    local_shape = ((features, TOKENS_HERE), F32)
    slots, back, mine, local_query, local_key, local_value = call(
        local_kernel,
        [
            ((sources, SLOT, LANES), BF16),
            ((rows + GAP, LANES), BF16),
            ((heads * GAP, LANES), BF16),
            local_shape,
            local_shape,
            local_shape,
        ],
        1,
        (offsets, queries, keys, values, full_grad, out_weight, near),
    )
    back = lax.ppermute(back, "yh", other)
    slots = lax.all_to_all(slots, "xz", 0, 0, tiled=True)
    merged_rows = HEAD_DIM + sources * GAP // 2
    (merged,) = call(
        merge_kernel,
        [((PLANES, merged_rows, LANES), BF16)],
        0,
        (slots,),
        [pltpu.VMEM((sources * GAP // 2, LANES), F32)],
    )
    merged = lax.all_to_all(merged, "yh", 0, 0, tiled=True)
    plane = lax.axis_index("yh").reshape(1)
    far_count = PLANES * sources * 2
    (slots,) = call(
        far_kernel,
        [((sources, SLOT, LANES), BF16)],
        1,
        (plane, merged),
        [pltpu.VMEM((far_count, LANES), F32), pltpu.VMEM((far_count, LANES), F32)],
    )
    slots = lax.all_to_all(slots, "xz", 0, 0, tiled=True)
    grad_shape = ((features, TOKENS_HERE), BF16)
    return tuple(
        call(
            final_kernel,
            [grad_shape, grad_shape, grad_shape, ((features, model), F32)],
            1,
            (
                offsets,
                queries,
                keys,
                values,
                near,
                back,
                mine,
                local_query,
                local_key,
                local_value,
                slots,
            ),
        )
    )


def solution(mesh):
    devices = mesh.devices.reshape(-1, PLANES, mesh.devices.shape[1])
    split_mesh = Mesh(devices, ("xz", "yh", "dp"))
    wide = P("dp", ("xz", "yh"))
    return jax.shard_map(
        local,
        mesh=split_mesh,
        in_specs=(wide, wide, wide, wide, P("dp", None), P("dp")),
        out_specs=(wide, wide, wide, P("dp", None)),
        check_vma=False,
    )
```

time: 2250 us -> 101 us (0.04)
  waiting for transfers between devices: 1390 us -> 26.4 us
  blocking collectives: 755 us -> 34.4 us
  local copies, waits for them, and re-layouts: 43.5 us -> 3.11 us
    unnamed x2 -> x0, waiting for transfers between devices: 1390 us -> none
    all_gather x2 -> x0, blocking collectives: 748 us -> none  [the longest x1 374 us: local(): lax.all_gather(far_value[0], 'seq', axis=0, tiled=True)]
    all_to_all x0 -> x1, blocking collectives: none -> 28.2 us  [local(): slots = lax.all_to_all(slots, 'xz', 0, 0, tiled=True)]
    all_to_all x0 -> x2, waiting for transfers between devices: none -> 22.7 us  [the longest x1 13.9 us: local(): slots = lax.all_to_all(slots, 'xz', 0, 0, tiled=True)]
  transfers between devices with their start and end apart: 5 -> 4, of which waited for: 1 -> 3; matrix products, arithmetic and copies ran while one was open for 1% -> 0% of each run, Pallas kernels for 0% -> 0%
where the time goes in v2:
time: 101 us
  blocking collectives  34.4 us (34%)
  waiting for transfers between devices  26.4 us (26%)
  starting transfers between devices  25.5 us (25%)
  Pallas kernels  10.7 us (11%)
  local copies, waits for them, and re-layouts  3.11 us (3%)
    all_to_all x1, blocking collectives, local(): slots = lax.all_to_all(slots, 'xz', 0, 0, tiled=True)  28.2 us
    all_to_all x1, waiting for transfers between devices, local(): slots = lax.all_to_all(slots, 'xz', 0, 0, tiled=True)  13.9 us
    pallas_call x5, Pallas kernels, call(): pl.pallas_call(kernel, out_shape=shapes, in_specs=specs, out_specs=[pl.Bl...  10.7 us
    all_to_all x1, waiting for transfers between devices, local(): merged = lax.all_to_all(merged, 'yh', 0, 0, tiled=True)  8.83 us
    ppermute x1, starting transfers between devices, local(): near = lax.ppermute(near_own, 'yh', other)  7.76 us
    all_to_all x1, starting transfers between devices, local(): merged = lax.all_to_all(merged, 'yh', 0, 0, tiled=True)  7.49 us
    all_to_all x1, starting transfers between devices, local(): slots = lax.all_to_all(slots, 'xz', 0, 0, tiled=True)  7.4 us
    all_gather x1, blocking collectives, local(): full_grad = lax.all_gather(grad_out, 'dp', axis=0, tiled=True)  6.15 us
  transfers between devices with their start and end apart: 4, of which 3 were waited for; matrix products, arithmetic and copies ran while one was open for 0% of the time, Pallas kernels for 0%

profile of v2, /device:TPU:16, one launch (start us, length us, event | category | flops | bytes accessed | tf_op | source)
XLA Modules:
  0.0 100.8 jit_solution(5077416571426261490)
XLA Ops:
  0.6 0.0 copy-start
  0.6 0.9 copy-done
  1.5 0.0 copy-start.2
  1.5 0.9 copy-done.2
  2.4 0.0 copy-start.6
  2.4 0.7 copy-done.6
  3.1 0.0 copy-start.8
  3.1 0.7 near_kernel.1
  3.8 0.0 copy-start.4
  3.8 0.0 copy-start.5
  3.8 7.8 %collective-permute-start = (bf16[48,128]{1,0:T(8,128)(2,1)S(1)}, bf16[48,128]{1,0:T(8,128)(2,1)S(1)}, u32[]{:S(2)}, u32[]{:S(2)}) collective-permute-start(bf16[48,128]{1,0:T(8,128)(2,1)S(1)} %near_kernel.1), channel_id=1, source_target_pairs={{0,4},{4,0},{8,12},{12,8},{1,5},{5,1},{9,13},{13,9},{2,6},{6,2},{1... | collective-permute-start | bytes 36872 | tf_op jit(solution)/shard_map/ppermute | solution.py:376
  11.6 0.0 copy-done.8
  11.6 6.1 %all_gather.3.grad_ref = bf16[768,256]{1,0:T(8,128)(2,1)S(1)} all-gather(bf16[192,256]{1,0:T(8,128)(2,1)S(1)} %copy-done.8), channel_id=1, replica_groups=mesh['xz'=32,'yh'=4,'dp'=4] {'dp'}, dimensions={0}, use_global_device_ids=true | all-gather | bytes 491520 | tf_op jit(solution)/shard_map/all_gather | solution.py:377
  17.7 0.0 collective-permute-done.near_ref
  17.7 0.0 copy-done.4
  17.7 0.0 copy-done.5
  17.7 3.3 %local_kernel.1 = (bf16[32,80,128]{2,1,0:T(8,128)(2,1)S(1)}, bf16[64,128]{1,0:T(8,128)(2,1)S(1)}, bf16[48,128]{1,0:T(8,128)(2,1)S(1)}, f32[192,256]{1,0:T(8,128)...) custom-call(s32[3]{0:T(128)S(1)} %copy-done.6, bf16[192,256]{1,0:T(8,128)(2,1)S(1)} %copy-done.4, ...), custom_call_target="tpu_custom_call" | custom-call | tf_op jit(solution)/shard_map/local_kernel/pallas_call | solution.py:356
  21.0 28.2 %all_to_all.15.slots_ref = bf16[32,80,128]{2,1,0:T(8,128)(2,1)S(1)} all-to-all(bf16[32,80,128]{2,1,0:T(8,128)(2,1)S(1)} %get-tuple-element.15), channel_id=1, replica_groups=mesh['xz'=32,'yh'=4,'dp'=4] {'xz'}, dimensions={0} | all-to-all | bytes 1310720 | tf_op jit(solution)/shard_map/all_to_all | solution.py:393
  49.3 0.8 merge_kernel.1
  50.1 7.5 %all-to-all-start.1 = ((bf16[4,320,128]{2,1,0:T(8,128)(2,1)}), bf16[4,320,128]{2,1,0:T(8,128)(2,1)S(1)}, u32[]{:S(2)}, u32[]{:S(2)}) async-start(bf16[4,320,128]{2,1,0:T(8,128)(2,1)} %merge_kernel.1), calls=%async_computation.1 | async-start | bytes 655360 | tf_op jit(solution)/shard_map/all_to_all | solution.py:402
  57.6 8.8 %all-to-all-done.1.merged_ref = bf16[4,320,128]{2,1,0:T(8,128)(2,1)S(1)} async-done(((bf16[4,320,128]{2,1,0:T(8,128)(2,1)}), bf16[4,320,128]{2,1,0:T(8,128)(2,1)S(1)}, u32[]{:S(2)}, u32[]{:S(2)}) %all-to-all-start.1) | async-done | bytes 327712 | tf_op jit(solution)/shard_map/all_to_all | solution.py:402
  66.4 2.3 %far_kernel.1 = bf16[32,80,128]{2,1,0:T(8,128)(2,1)} custom-call(s32[1]{0:T(128)} %bitcast.plane_ref, bf16[4,320,128]{2,1,0:T(8,128)(2,1)S(1)} %all-to-all-done.1.merged_ref), custom_call_target="tpu_custom_call" | custom-call | tf_op jit(solution)/shard_map/far_kernel/pallas_call | solution.py:356
  68.7 0.0 copy-start.1
  68.7 0.0 copy-start.3
  68.7 7.4 %all-to-all-start.2 = ((bf16[32,80,128]{2,1,0:T(8,128)(2,1)}), bf16[32,80,128]{2,1,0:T(8,128)(2,1)S(1)}, u32[]{:S(2)}, u32[]{:S(2)}) async-start(bf16[32,80,128]{2,1,0:T(8,128)(2,1)} %far_kernel.1), calls=%async_computation.2 | async-start | bytes 1310720 | tf_op jit(solution)/shard_map/all_to_all | solution.py:412
  76.1 2.8 %collective-permute-start.1 = (bf16[64,128]{1,0:T(8,128)(2,1)S(1)}, bf16[64,128]{1,0:T(8,128)(2,1)S(1)}, u32[]{:S(2)}, u32[]{:S(2)}) collective-permute-start(bf16[64,128]{1,0:T(8,128)(2,1)S(1)} %get-tuple-element.10), channel_id=1, source_target_pairs={{0,4},{4,0},{8,12},{12,8},{1,5},{5,1},{9,13},{13,9},{2,6},{6,2},{1... | collective-permute-start | bytes 49160 | tf_op jit(solution)/shard_map/ppermute | solution.py:392
  79.0 3.7 %collective-permute-done.1.back_ref = bf16[64,128]{1,0:T(8,128)(2,1)S(1)} collective-permute-done((bf16[64,128]{1,0:T(8,128)(2,1)S(1)}, bf16[64,128]{1,0:T(8,128)(2,1)S(1)}, u32[]{:S(2)}, u32[]{:S(2)}) %collective-permute-start.1) | collective-permute-done | bytes 16416 | tf_op jit(solution)/shard_map/ppermute | solution.py:392
  82.6 13.9 %all-to-all-done.2.slots_ref = bf16[32,80,128]{2,1,0:T(8,128)(2,1)S(1)} async-done(((bf16[32,80,128]{2,1,0:T(8,128)(2,1)}), bf16[32,80,128]{2,1,0:T(8,128)(2,1)S(1)}, u32[]{:S(2)}, u32[]{:S(2)}) %all-to-all-start.2) | async-done | bytes 655392 | tf_op jit(solution)/shard_map/all_to_all | solution.py:412
  96.6 0.0 copy-start.7
  96.6 0.0 copy-done.1
  96.6 0.0 copy-done.3
  96.6 0.6 copy-done.7
  97.2 3.6 %final_kernel.1 = (bf16[192,256]{1,0:T(8,128)(2,1)}, bf16[192,256]{1,0:T(8,128)(2,1)}, bf16[192,256]{1,0:T(8,128)(2,1)}, f32[192,768]{1,0:T(8,128)}) custom-call(s32[3]{0:T(128)S(1)} %copy-done.7, bf16[192,256]{1,0:T(8,128)(2,1)S(1)} %copy-done.4, bf16[192,256]{1,0:T(8,128)(2,1)S(1)} %copy-done.1, bf16[192,256]{1,0:T(8,128)(2,1)S(1)} %copy-done.3, ...), custom_call_target="tpu_custom_call" | custom-call | tf_op jit(solution)/shard_map/final_kernel/pallas_call | solution.py:356
Async XLA Ops:
  0.6 0.9 copy-start
  1.5 0.9 copy-start.2
  2.4 0.7 copy-start.6
  3.1 8.5 %copy-start.8 = (bf16[192,256]{1,0:T(8,128)(2,1)S(1)}, bf16[192,256]{1,0:T(8,128)(2,1)}, u32[]{:S(2)}) copy-start(bf16[192,256]{1,0:T(8,128)(2,1)} %param.9) | copy-start | bytes 294916
  3.8 14.0 %copy-start.4 = (bf16[192,256]{1,0:T(8,128)(2,1)S(1)}, bf16[192,256]{1,0:T(8,128)(2,1)}, u32[]{:S(2)}) copy-start(bf16[192,256]{1,0:T(8,128)(2,1)} %query_ref.3) | copy-start | bytes 294916
  3.8 14.0 %copy-start.5 = (bf16[192,768]{1,0:T(8,128)(2,1)S(1)}, bf16[192,768]{1,0:T(8,128)(2,1)}, u32[]{:S(2)}) copy-start(bf16[192,768]{1,0:T(8,128)(2,1)} %weight_ref.1) | copy-start | bytes 884740
  3.8 13.9 %collective-permute-start = (bf16[48,128]{1,0:T(8,128)(2,1)S(1)}, bf16[48,128]{1,0:T(8,128)(2,1)S(1)}, u32[]{:S(2)}, u32[]{:S(2)}) collective-permute-start(bf16[48,128]{1,0:T(8,128)(2,1)S(1)} %near_kernel.1), channel_id=1, source_target_pairs={{0,4},{4,0},{8,12},{12,8},{1,5},{5,1},{9,13},{13,9},{2,6},{6,2},{1... | collective-permute-start | bytes 36872 | tf_op jit(solution)/shard_map/ppermute | solution.py:376
  50.1 16.3 %all-to-all-start.1 = ((bf16[4,320,128]{2,1,0:T(8,128)(2,1)}), bf16[4,320,128]{2,1,0:T(8,128)(2,1)S(1)}, u32[]{:S(2)}, u32[]{:S(2)}) async-start(bf16[4,320,128]{2,1,0:T(8,128)(2,1)} %merge_kernel.1), calls=%async_computation.1 | async-start | bytes 655360 | tf_op jit(solution)/shard_map/all_to_all | solution.py:402
  68.7 27.9 %copy-start.1 = (bf16[192,256]{1,0:T(8,128)(2,1)S(1)}, bf16[192,256]{1,0:T(8,128)(2,1)}, u32[]{:S(2)}) copy-start(bf16[192,256]{1,0:T(8,128)(2,1)} %key_ref.5) | copy-start | bytes 294916
  68.7 27.9 %copy-start.3 = (bf16[192,256]{1,0:T(8,128)(2,1)S(1)}, bf16[192,256]{1,0:T(8,128)(2,1)}, u32[]{:S(2)}) copy-start(bf16[192,256]{1,0:T(8,128)(2,1)} %value_ref.5) | copy-start | bytes 294916
  68.7 27.8 %all-to-all-start.2 = ((bf16[32,80,128]{2,1,0:T(8,128)(2,1)}), bf16[32,80,128]{2,1,0:T(8,128)(2,1)S(1)}, u32[]{:S(2)}, u32[]{:S(2)}) async-start(bf16[32,80,128]{2,1,0:T(8,128)(2,1)} %far_kernel.1), calls=%async_computation.2 | async-start | bytes 1310720 | tf_op jit(solution)/shard_map/all_to_all | solution.py:412
  76.1 6.5 %collective-permute-start.1 = (bf16[64,128]{1,0:T(8,128)(2,1)S(1)}, bf16[64,128]{1,0:T(8,128)(2,1)S(1)}, u32[]{:S(2)}, u32[]{:S(2)}) collective-permute-start(bf16[64,128]{1,0:T(8,128)(2,1)S(1)} %get-tuple-element.10), channel_id=1, source_target_pairs={{0,4},{4,0},{8,12},{12,8},{1,5},{5,1},{9,13},{13,9},{2,6},{6,2},{1... | collective-permute-start | bytes 49160 | tf_op jit(solution)/shard_map/ppermute | solution.py:392
  96.6 0.7 copy-start.7

commit v3 on v2

--- a/solution.py
+++ b/solution.py
@@ -18,7 +18,9 @@
 PLANES = 4
 LANES = 128
 GAP = 16
-SLOT = HEAD_DIM + GAP
+SMALL = 8
+CHUNK = 40
+SLOT = CHUNK + SMALL
 
 F32 = jnp.float32
 BF16 = jnp.bfloat16
@@ -81,6 +83,14 @@
 
 def right_half(rows):
     return jnp.where(iota(rows.shape, 1) >= HEAD_DIM, rows.astype(F32), 0.0).astype(BF16)
+
+
+def chunk_rows(folded, chunk):
+    rows = folded[chunk * CHUNK : (chunk + 1) * CHUNK]
+    short = CHUNK - rows.shape[0]
+    if short:
+        rows = jnp.concatenate([rows, jnp.zeros((short,) + rows.shape[1:], rows.dtype)], axis=0)
+    return rows
 
 
 def near_kernel(offset_ref, key_ref, value_ref, near_ref):
@@ -107,9 +117,18 @@
     grad_value_ref,
 ):
     heads = query_ref.shape[0] // HEAD_DIM
-    tiles = grad_ref.shape[0] // LANES
+    half = grad_ref.shape[0] // 2
+    chunks = pl.cdiv(half, CHUNK)
     grad = grad_ref[...]
     dout = mm(weight_ref[...], grad, 1, 0).astype(BF16)
+    choosers = [far_chooser(offset_ref[head], 3) for head in range(heads)]
+    choosers = jnp.concatenate(choosers, axis=0)
+    wide = grad.astype(F32)
+    filler = jnp.zeros((LANES - 2 * CHUNK, TOKENS_HERE), F32)
+    far_grads = []
+    for chunk in range(chunks):
+        both = [chunk_rows(wide[:half], chunk), chunk_rows(wide[half:], chunk), filler]
+        far_grads.append(mm(choosers, jnp.concatenate(both, axis=0).astype(BF16), 1, 1))
     blank = jnp.zeros((HEAD_DIM, TOKENS_HERE), BF16)
     key_pos = iota((TOKENS_HERE, TOKENS_HERE), 0)
     query_pos = iota((TOKENS_HERE, TOKENS_HERE), 1)
@@ -167,7 +186,10 @@
         back_ref[near_rows] = back.astype(BF16)
 
         attended_kept = jnp.where(in_far, 0.0, attended).astype(BF16)
-        weight_part = mm(attended_kept, grad, 1, 1) * WEIGHT_SCALE
+        over = jnp.concatenate([attended_kept, blank], axis=0)
+        under = jnp.concatenate([blank, attended_kept], axis=0)
+        weight_part = mm(grad[:half], over, 1, 1) + mm(grad[half:], under, 1, 1)
+        weight_part = weight_part * WEIGHT_SCALE
         query_key = jnp.concatenate([query, key], axis=0)
         value_dout = jnp.concatenate([value, dout_head], axis=0)
         stats = lay_stats((HEAD_DIM, TOKENS_HERE), 0, 0, (log_mass, delta))
@@ -176,28 +198,25 @@
         mine = mine + mm(far_chooser(offset, 1), value_dout, 1, 1)
         mine = mine + mm(far_chooser(offset, 2), attended_stats, 1, 1)
         mine_ref[head * GAP : (head + 1) * GAP] = mine.astype(BF16)
-        far_grad = mm(far_chooser(offset, 3), grad, 1, 1)
-        for tile in range(tiles):
-            lanes = slice(tile * LANES, (tile + 1) * LANES)
-            slots_ref[head * tiles + tile, :HEAD_DIM] = weight_part[:, lanes].astype(BF16)
-            slots_ref[head * tiles + tile, HEAD_DIM:] = (mine + far_grad[:, lanes]).astype(BF16)
+        for chunk in range(chunks):
+            far_grad = far_grads[chunk][head * GAP : head * GAP + SMALL]
+            parts = [chunk_rows(weight_part, chunk), mine[:SMALL] + far_grad]
+            slots_ref[head * chunks + chunk] = jnp.concatenate(parts, axis=0).astype(BF16)
         query_dout = jnp.concatenate([query, dout_head], axis=0)
         partner_far = partner_far + mm(far_chooser(offset, head), query_dout, 1, 1)
     back_ref[heads * NEAR :] = partner_far.astype(BF16)
-    rest = slots_ref.shape[0] - heads * tiles
-    slots_ref[heads * tiles :] = jnp.zeros((rest,) + slots_ref.shape[1:], BF16)
+    rest = slots_ref.shape[0] - heads * chunks
+    slots_ref[heads * chunks :] = jnp.zeros((rest,) + slots_ref.shape[1:], BF16)
 
 
 def merge_kernel(slots_ref, merged_ref, far_ref):
     sources = slots_ref.shape[0]
-    total = slots_ref[0, :HEAD_DIM].astype(F32)
-    for source in range(1, sources):
-        total = total + slots_ref[source, :HEAD_DIM].astype(F32)
-    half = GAP // 2
+    total = jnp.zeros((SLOT, LANES), F32)
     for source in range(sources):
-        block = slots_ref[source, HEAD_DIM:].astype(F32)
-        far_ref[source * half : (source + 1) * half] = block[:half]
-    pieces = [far_ref[pl.ds(kind, sources, stride=half), :] for kind in range(half)]
+        block = slots_ref[source].astype(F32)
+        total = total + block
+        far_ref[source * SMALL : (source + 1) * SMALL] = block[CHUNK:]
+    pieces = [far_ref[pl.ds(kind, sources, stride=SMALL), :] for kind in range(SMALL)]
     full = jnp.concatenate([total] + pieces, axis=0).astype(BF16)
     for plane in range(PLANES):
         merged_ref[plane] = full
@@ -209,7 +228,7 @@
     count = PLANES * width
 
     def kind(index):
-        start = HEAD_DIM + index * width
+        start = SLOT + index * width
         return merged_ref[:, start : start + width, :].reshape(count, LANES)
 
     query_key, value_dout, attended_stats, far_grad = (kind(index) for index in range(4))
@@ -237,9 +256,6 @@
     grad_query = mm(grad_scores, key, 1, 0).astype(BF16)
     grad_key = mm(grad_scores, query, 0, 0).astype(BF16)
     grad_value = mm(probs_low, dout, 0, 0).astype(BF16)
-    weight_part = mm(attended.astype(BF16), far_grad, 0, 0) * WEIGHT_SCALE
-    for plane in range(PLANES):
-        weight_part = weight_part + merged_ref[plane, :HEAD_DIM].astype(F32)
 
     def other_plane(column):
         blocks = [column[(p ^ 1) * width : ((p ^ 1) + 1) * width] for p in range(PLANES)]
@@ -248,24 +264,30 @@
     shape = (HEAD_DIM, LANES)
     to_left = one_hot(iota(shape, 0) == iota(shape, 1))
     to_right = one_hot(iota(shape, 0) + HEAD_DIM == iota(shape, 1))
+    attended_low = attended.astype(BF16)
+    over = mm(attended_low, to_left, 1, 0).astype(BF16)
+    under = mm(attended_low, to_right, 1, 0).astype(BF16)
+    weight_part = mm(far_grad, over, 0, 0)[:CHUNK] + mm(far_grad, under, 0, 0)[CHUNK : 2 * CHUNK]
+    weight_part = weight_part * WEIGHT_SCALE
+    for plane in range(PLANES):
+        weight_part = weight_part + merged_ref[plane, :SLOT].astype(F32)[:CHUNK]
     both_stats = (normalizer, delta, other_plane(normalizer), other_plane(delta))
     first_ref[...] = mm(grad_value, to_left, 1, 0) + lay_stats(
         (count, LANES), 1, HEAD_DIM, both_stats
     )
     second_ref[...] = mm(grad_query, to_left, 1, 0) + mm(grad_key, to_right, 1, 0)
     own = pl.ds(pl.multiple_of(plane_ref[0] * width, width), width)
-    shape = (sources * GAP, width)
+    shape = (sources * SMALL, width)
     row, column = iota(shape, 0), iota(shape, 1)
-    same = (row // GAP) == (column % sources)
-    slot_row, pair = row % GAP, column // sources
+    same = (row // SMALL) == (column % sources)
+    slot_row, pair = row % SMALL, column // sources
     placed = mm(one_hot(same & (slot_row == pair)), first_ref[own, :].astype(BF16), 1, 0)
     placed = placed + mm(
         one_hot(same & (slot_row == pair + 2)), second_ref[own, :].astype(BF16), 1, 0
     )
-    slots_ref[:, HEAD_DIM:, :] = placed.astype(BF16).reshape(sources, GAP, LANES)
-    weight_low = weight_part.astype(BF16)
     for source in range(sources):
-        slots_ref[source, :HEAD_DIM] = weight_low
+        parts = [weight_part, placed[source * SMALL : (source + 1) * SMALL]]
+        slots_ref[source] = jnp.concatenate(parts, axis=0).astype(BF16)
 
 
 def final_kernel(
@@ -286,7 +308,8 @@
     grad_weight_ref,
 ):
     heads = query_ref.shape[0] // HEAD_DIM
-    tiles = grad_weight_ref.shape[1] // LANES
+    half = grad_weight_ref.shape[1] // 2
+    chunks = pl.cdiv(half, CHUNK)
     blank = jnp.zeros((HEAD_DIM, TOKENS_HERE), BF16)
     key_row = iota((1, TOKENS_HERE), 1)
     shape = (GAP, GAP)
@@ -300,8 +323,11 @@
         query, key, value = query_ref[rows], key_ref[rows], value_ref[rows]
         near = near_ref[near_rows]
         mine = mine_ref[head * GAP : (head + 1) * GAP]
-        returned = slots_ref[head * tiles, HEAD_DIM:]
-        stats = returned.astype(F32)
+        blocks = [slots_ref[head * chunks + chunk].astype(F32) for chunk in range(chunks)]
+        stats = jnp.concatenate(
+            [blocks[0][CHUNK:], jnp.zeros((GAP - SMALL, LANES), F32)], axis=0
+        )
+        returned = stats.astype(BF16)
         normalizer, delta, far_normalizer, far_delta = (take_stat(stats, i) for i in range(4))
         key_over = jnp.concatenate([key, blank], axis=0)
         value_under = jnp.concatenate([blank, value], axis=0)
@@ -344,9 +370,10 @@
         grad_query_ref[rows] = (grad_query * SCORE_SCALE).astype(BF16)
         grad_key_ref[rows] = (grad_key * SCORE_SCALE).astype(BF16)
         grad_value_ref[rows] = grad_value.astype(BF16)
-        for tile in range(tiles):
-            lanes = slice(tile * LANES, (tile + 1) * LANES)
-            grad_weight_ref[rows, lanes] = slots_ref[head * tiles + tile, :HEAD_DIM].astype(F32)
+        folded = jnp.concatenate([block[:CHUNK] for block in blocks], axis=0)[:half]
+        unfolded = jnp.transpose(folded)
+        grad_weight_ref[rows, :half] = unfolded[:HEAD_DIM]
+        grad_weight_ref[rows, half:] = unfolded[HEAD_DIM:]
 
 
 def call(kernel, outs, scalars, arrays, scratch=()):
@@ -391,13 +418,13 @@
     )
     back = lax.ppermute(back, "yh", other)
     slots = lax.all_to_all(slots, "xz", 0, 0, tiled=True)
-    merged_rows = HEAD_DIM + sources * GAP // 2
+    merged_rows = SLOT + sources * SMALL
     (merged,) = call(
         merge_kernel,
         [((PLANES, merged_rows, LANES), BF16)],
         0,
         (slots,),
-        [pltpu.VMEM((sources * GAP // 2, LANES), F32)],
+        [pltpu.VMEM((sources * SMALL, LANES), F32)],
     )
     merged = lax.all_to_all(merged, "yh", 0, 0, tiled=True)
     plane = lax.axis_index("yh").reshape(1)

time: 101 us -> 89 us (0.88)
  waiting for transfers between devices: 26.4 us -> 19.1 us
  blocking collectives: 34.4 us -> 28.7 us
  starting transfers between devices: 25.5 us -> 26.6 us
    all_to_all x1, waiting for transfers between devices: 13.9 us -> 7.88 us  [local(): slots = lax.all_to_all(slots, 'xz', 0, 0, tiled=True)]
    all_to_all x1, blocking collectives: 28.2 us -> 22.6 us  [local(): slots = lax.all_to_all(slots, 'xz', 0, 0, tiled=True)]
    all_to_all x1, waiting for transfers between devices: 8.83 us -> 7.55 us  [local(): merged = lax.all_to_all(merged, 'yh', 0, 0, tiled=True)]
    all_to_all x1, starting transfers between devices: 7.4 us -> 8.51 us  [local(): slots = lax.all_to_all(slots, 'xz', 0, 0, tiled=True)]
where the time goes in v3:
time: 89 us; the launch traced here: 88.6 us
  blocking collectives  28.7 us (32%)
  starting transfers between devices  26.6 us (30%)
  waiting for transfers between devices  19.1 us (21%)
  Pallas kernels  10.3 us (12%)
  local copies, waits for them, and re-layouts  3.11 us (3%)
    all_to_all x1, blocking collectives, local(): slots = lax.all_to_all(slots, 'xz', 0, 0, tiled=True)  22.6 us
    pallas_call x5, Pallas kernels, call(): pl.pallas_call(kernel, out_shape=shapes, in_specs=specs, out_specs=[pl.Bl...  10.3 us
    all_to_all x1, starting transfers between devices, local(): slots = lax.all_to_all(slots, 'xz', 0, 0, tiled=True)  8.51 us
    all_to_all x1, waiting for transfers between devices, local(): slots = lax.all_to_all(slots, 'xz', 0, 0, tiled=True)  7.88 us
    ppermute x1, starting transfers between devices, local(): near = lax.ppermute(near_own, 'yh', other)  7.76 us
    all_to_all x1, waiting for transfers between devices, local(): merged = lax.all_to_all(merged, 'yh', 0, 0, tiled=True)  7.55 us
    all_to_all x1, starting transfers between devices, local(): merged = lax.all_to_all(merged, 'yh', 0, 0, tiled=True)  7.49 us
    all_gather x1, blocking collectives, local(): full_grad = lax.all_gather(grad_out, 'dp', axis=0, tiled=True)  6.15 us
  transfers between devices with their start and end apart: 4, of which 3 were waited for; matrix products, arithmetic and copies ran while one was open for 0% of the time, Pallas kernels for 0%

profile of v3, /device:TPU:16, one launch (start us, length us, event | category | flops | bytes accessed | tf_op | source)
XLA Modules:
  0.0 88.6 jit_solution(12691526612667649742)
XLA Ops:
  0.6 0.0 copy-start
  0.6 0.9 copy-done
  1.5 0.0 copy-start.2
  1.5 0.9 %copy-done.2 = bf16[192,256]{1,0:T(8,128)(2,1)S(1)} copy-done((bf16[192,256]{1,0:T(8,128)(2,1)S(1)}, bf16[192,256]{1,0:T(8,128)(2,1)}, u32[]{:S(2)}) %copy-start.2) | copy-done | bytes 98328
  2.4 0.0 copy-start.6
  2.4 0.7 copy-done.6
  3.1 0.0 copy-start.8
  3.1 0.7 near_kernel.1
  3.8 0.0 copy-start.4
  3.8 0.0 copy-start.5
  3.8 7.8 %collective-permute-start = (bf16[48,128]{1,0:T(8,128)(2,1)S(1)}, bf16[48,128]{1,0:T(8,128)(2,1)S(1)}, u32[]{:S(2)}, u32[]{:S(2)}) collective-permute-start(bf16[48,128]{1,0:T(8,128)(2,1)S(1)} %near_kernel.1), channel_id=1, source_target_pairs={{0,4},{4,0},{8,12},{12,8},{1,5},{5,1},{9,13},{13,9},{2,6},{6,2},{1... | collective-permute-start | bytes 36872 | tf_op jit(solution)/shard_map/ppermute | solution.py:403
  11.6 0.0 copy-done.8
  11.6 6.1 %all_gather.3.grad_ref = bf16[768,256]{1,0:T(8,128)(2,1)S(1)} all-gather(bf16[192,256]{1,0:T(8,128)(2,1)S(1)} %copy-done.8), channel_id=1, replica_groups=mesh['xz'=32,'yh'=4,'dp'=4] {'dp'}, dimensions={0}, use_global_device_ids=true | all-gather | bytes 491520 | tf_op jit(solution)/shard_map/all_gather | solution.py:404
  17.7 0.0 collective-permute-done.near_ref
  17.7 0.0 copy-done.4
  17.7 0.0 copy-done.5
  17.7 3.2 %local_kernel.1 = (bf16[32,48,128]{2,1,0:T(8,128)(2,1)S(1)}, bf16[64,128]{1,0:T(8,128)(2,1)S(1)}, bf16[48,128]{1,0:T(8,128)(2,1)S(1)}, f32[192,256]{1,0:T(8,128)...) custom-call(s32[3]{0:T(128)S(1)} %copy-done.6, bf16[192,256]{1,0:T(8,128)(2,1)S(1)} %copy-done.4, ...), custom_call_target="tpu_custom_call" | custom-call | tf_op jit(solution)/shard_map/local_kernel/pallas_call | solution.py:383
  20.9 22.6 %all_to_all.15.slots_ref = bf16[32,48,128]{2,1,0:T(8,128)(2,1)S(1)} all-to-all(bf16[32,48,128]{2,1,0:T(8,128)(2,1)S(1)} %get-tuple-element.15), channel_id=1, replica_groups=mesh['xz'=32,'yh'=4,'dp'=4] {'xz'}, dimensions={0} | all-to-all | bytes 786432 | tf_op jit(solution)/shard_map/all_to_all | solution.py:420
  43.5 0.8 merge_kernel.1
  44.3 7.5 %all-to-all-start.1 = ((bf16[4,304,128]{2,1,0:T(8,128)(2,1)}), bf16[4,304,128]{2,1,0:T(8,128)(2,1)S(1)}, u32[]{:S(2)}, u32[]{:S(2)}) async-start(bf16[4,304,128]{2,1,0:T(8,128)(2,1)} %merge_kernel.1), calls=%async_computation.1 | async-start | bytes 622592 | tf_op jit(solution)/shard_map/all_to_all | solution.py:429
  51.8 7.5 %all-to-all-done.1.merged_ref = bf16[4,304,128]{2,1,0:T(8,128)(2,1)S(1)} async-done(((bf16[4,304,128]{2,1,0:T(8,128)(2,1)}), bf16[4,304,128]{2,1,0:T(8,128)(2,1)S(1)}, u32[]{:S(2)}, u32[]{:S(2)}) %all-to-all-start.1) | async-done | bytes 311328 | tf_op jit(solution)/shard_map/all_to_all | solution.py:429
  59.3 2.2 %far_kernel.1 = bf16[32,48,128]{2,1,0:T(8,128)(2,1)} custom-call(s32[1]{0:T(128)} %bitcast.plane_ref, bf16[4,304,128]{2,1,0:T(8,128)(2,1)S(1)} %all-to-all-done.1.merged_ref), custom_call_target="tpu_custom_call" | custom-call | tf_op jit(solution)/shard_map/far_kernel/pallas_call | solution.py:383
  61.5 0.0 copy-start.1
  61.5 0.0 copy-start.3
  61.5 8.5 %all-to-all-start.2 = ((bf16[32,48,128]{2,1,0:T(8,128)(2,1)}), bf16[32,48,128]{2,1,0:T(8,128)(2,1)S(1)}, u32[]{:S(2)}, u32[]{:S(2)}) async-start(bf16[32,48,128]{2,1,0:T(8,128)(2,1)} %far_kernel.1), calls=%async_computation.2 | async-start | bytes 786432 | tf_op jit(solution)/shard_map/all_to_all | solution.py:439
  70.0 2.9 %collective-permute-start.1 = (bf16[64,128]{1,0:T(8,128)(2,1)S(1)}, bf16[64,128]{1,0:T(8,128)(2,1)S(1)}, u32[]{:S(2)}, u32[]{:S(2)}) collective-permute-start(bf16[64,128]{1,0:T(8,128)(2,1)S(1)} %get-tuple-element.10), channel_id=1, source_target_pairs={{0,4},{4,0},{8,12},{12,8},{1,5},{5,1},{9,13},{13,9},{2,6},{6,2},{1... | collective-permute-start | bytes 49160 | tf_op jit(solution)/shard_map/ppermute | solution.py:419
  72.9 3.6 %collective-permute-done.1.back_ref = bf16[64,128]{1,0:T(8,128)(2,1)S(1)} collective-permute-done((bf16[64,128]{1,0:T(8,128)(2,1)S(1)}, bf16[64,128]{1,0:T(8,128)(2,1)S(1)}, u32[]{:S(2)}, u32[]{:S(2)}) %collective-permute-start.1) | collective-permute-done | bytes 16416 | tf_op jit(solution)/shard_map/ppermute | solution.py:419
  76.6 7.9 %all-to-all-done.2.slots_ref = bf16[32,48,128]{2,1,0:T(8,128)(2,1)S(1)} async-done(((bf16[32,48,128]{2,1,0:T(8,128)(2,1)}), bf16[32,48,128]{2,1,0:T(8,128)(2,1)S(1)}, u32[]{:S(2)}, u32[]{:S(2)}) %all-to-all-start.2) | async-done | bytes 393248 | tf_op jit(solution)/shard_map/all_to_all | solution.py:439
  84.4 0.0 copy-start.7
  84.4 0.0 copy-done.1
  84.5 0.0 copy-done.3
  84.5 0.6 copy-done.7
  85.1 3.5 %final_kernel.1 = (bf16[192,256]{1,0:T(8,128)(2,1)}, bf16[192,256]{1,0:T(8,128)(2,1)}, bf16[192,256]{1,0:T(8,128)(2,1)}, f32[192,768]{1,0:T(8,128)}) custom-call(s32[3]{0:T(128)S(1)} %copy-done.7, bf16[192,256]{1,0:T(8,128)(2,1)S(1)} %copy-done.4, bf16[192,256]{1,0:T(8,128)(2,1)S(1)} %copy-done.1, bf16[192,256]{1,0:T(8,128)(2,1)S(1)} %copy-done.3, ...), custom_call_target="tpu_custom_call" | custom-call | tf_op jit(solution)/shard_map/final_kernel/pallas_call | solution.py:383
Async XLA Ops:
  0.6 0.9 %copy-start = (bf16[192,256]{1,0:T(8,128)(2,1)S(1)}, bf16[192,256]{1,0:T(8,128)(2,1)}, u32[]{:S(2)}) copy-start(bf16[192,256]{1,0:T(8,128)(2,1)} %key_ref.5) | copy-start | bytes 294916
  1.5 0.9 %copy-start.2 = (bf16[192,256]{1,0:T(8,128)(2,1)S(1)}, bf16[192,256]{1,0:T(8,128)(2,1)}, u32[]{:S(2)}) copy-start(bf16[192,256]{1,0:T(8,128)(2,1)} %value_ref.5) | copy-start | bytes 294916
  2.4 0.7 copy-start.6
  3.1 8.5 %copy-start.8 = (bf16[192,256]{1,0:T(8,128)(2,1)S(1)}, bf16[192,256]{1,0:T(8,128)(2,1)}, u32[]{:S(2)}) copy-start(bf16[192,256]{1,0:T(8,128)(2,1)} %param.9) | copy-start | bytes 294916
  3.8 14.0 %copy-start.4 = (bf16[192,256]{1,0:T(8,128)(2,1)S(1)}, bf16[192,256]{1,0:T(8,128)(2,1)}, u32[]{:S(2)}) copy-start(bf16[192,256]{1,0:T(8,128)(2,1)} %query_ref.3) | copy-start | bytes 294916
  3.8 14.0 %copy-start.5 = (bf16[192,768]{1,0:T(8,128)(2,1)S(1)}, bf16[192,768]{1,0:T(8,128)(2,1)}, u32[]{:S(2)}) copy-start(bf16[192,768]{1,0:T(8,128)(2,1)} %weight_ref.1) | copy-start | bytes 884740
  3.8 13.9 %collective-permute-start = (bf16[48,128]{1,0:T(8,128)(2,1)S(1)}, bf16[48,128]{1,0:T(8,128)(2,1)S(1)}, u32[]{:S(2)}, u32[]{:S(2)}) collective-permute-start(bf16[48,128]{1,0:T(8,128)(2,1)S(1)} %near_kernel.1), channel_id=1, source_target_pairs={{0,4},{4,0},{8,12},{12,8},{1,5},{5,1},{9,13},{13,9},{2,6},{6,2},{1... | collective-permute-start | bytes 36872 | tf_op jit(solution)/shard_map/ppermute | solution.py:403
  44.3 15.0 %all-to-all-start.1 = ((bf16[4,304,128]{2,1,0:T(8,128)(2,1)}), bf16[4,304,128]{2,1,0:T(8,128)(2,1)S(1)}, u32[]{:S(2)}, u32[]{:S(2)}) async-start(bf16[4,304,128]{2,1,0:T(8,128)(2,1)} %merge_kernel.1), calls=%async_computation.1 | async-start | bytes 622592 | tf_op jit(solution)/shard_map/all_to_all | solution.py:429
  61.5 22.9 %copy-start.1 = (bf16[192,256]{1,0:T(8,128)(2,1)S(1)}, bf16[192,256]{1,0:T(8,128)(2,1)}, u32[]{:S(2)}) copy-start(bf16[192,256]{1,0:T(8,128)(2,1)} %key_ref.5) | copy-start | bytes 294916
  61.5 22.9 %copy-start.3 = (bf16[192,256]{1,0:T(8,128)(2,1)S(1)}, bf16[192,256]{1,0:T(8,128)(2,1)}, u32[]{:S(2)}) copy-start(bf16[192,256]{1,0:T(8,128)(2,1)} %value_ref.5) | copy-start | bytes 294916
  61.5 22.9 %all-to-all-start.2 = ((bf16[32,48,128]{2,1,0:T(8,128)(2,1)}), bf16[32,48,128]{2,1,0:T(8,128)(2,1)S(1)}, u32[]{:S(2)}, u32[]{:S(2)}) async-start(bf16[32,48,128]{2,1,0:T(8,128)(2,1)} %far_kernel.1), calls=%async_computation.2 | async-start | bytes 786432 | tf_op jit(solution)/shard_map/all_to_all | solution.py:439
  70.0 6.5 %collective-permute-start.1 = (bf16[64,128]{1,0:T(8,128)(2,1)S(1)}, bf16[64,128]{1,0:T(8,128)(2,1)S(1)}, u32[]{:S(2)}, u32[]{:S(2)}) collective-permute-start(bf16[64,128]{1,0:T(8,128)(2,1)S(1)} %get-tuple-element.10), channel_id=1, source_target_pairs={{0,4},{4,0},{8,12},{12,8},{1,5},{5,1},{9,13},{13,9},{2,6},{6,2},{1... | collective-permute-start | bytes 49160 | tf_op jit(solution)/shard_map/ppermute | solution.py:419
  84.4 0.7 copy-start.7

commit v4 on v3

v4 whole, which is shorter than its diff:
```python
import jax
import jax.numpy as jnp
from jax import lax
from jax.experimental import pallas as pl
from jax.experimental.pallas import tpu as pltpu
from jax.sharding import Mesh
from jax.sharding import PartitionSpec as P

HEAD_DIM = 64
TOKENS_HERE = 256
RB = 2
RC = 16
RE = 128
NEAR = TOKENS_HERE // RC
SCORE_SCALE = HEAD_DIM ** (-0.5)
WEIGHT_SCALE = 0.03125

PLANES = 4
LANES = 128
GAP = 16
SMALL = 8
CHUNK = 40
SLOT = CHUNK + SMALL
ABSENT = -1e30
LIMIT = 63_400_000

F32 = jnp.float32
BF16 = jnp.bfloat16


def mm(left, right, left_dim, right_dim):
    return lax.dot_general(
        left, right, (((left_dim,), (right_dim,)), ((), ())), preferred_element_type=F32
    )


def iota(shape, dim):
    return lax.broadcasted_iota(jnp.int32, shape, dim)


def one_hot(condition):
    return jnp.where(condition, 1.0, 0.0).astype(BF16)


def same_class(position, offset, stride):
    return (position & (stride - 1)) == (offset & (stride - 1))


def near_chooser(offset):
    shape = (NEAR, TOKENS_HERE)
    return one_hot(iota(shape, 1) == RC * iota(shape, 0) + (offset & (RC - 1)))


def far_chooser(offset, pair):
    shape = (GAP, TOKENS_HERE)
    row = iota(shape, 0)
    hit = iota(shape, 1) == RE * (row & 1) + offset
    return one_hot(hit & ((row >> 1) == pair))


def split3(value):
    high = value.astype(BF16).astype(F32)
    rest = value - high
    middle = rest.astype(BF16).astype(F32)
    return high, middle, rest - middle


def lay_stats(shape, dim, start, values):
    place = iota(shape, dim) - start
    out = jnp.zeros(shape, F32)
    for index, value in enumerate(values):
        for part_index, part in enumerate(split3(value)):
            out = jnp.where(place == 3 * index + part_index, part, out)
    return out


def take_stat(rows, index):
    place = iota(rows.shape, 1) - HEAD_DIM - 3 * index
    return jnp.sum(jnp.where((place >= 0) & (place < 3), rows, 0.0), axis=1, keepdims=True)


def chunk_rows(folded, chunk):
    rows = folded[chunk * CHUNK : (chunk + 1) * CHUNK]
    short = CHUNK - rows.shape[0]
    if short:
        rows = jnp.concatenate([rows, jnp.zeros((short,) + rows.shape[1:], rows.dtype)], axis=0)
    return rows


def near_kernel(
    offset_hbm, key_hbm, value_hbm, near_ref, offset_ref, key_ref, value_ref, semaphores
):
    pairs = ((offset_hbm, offset_ref), (key_hbm, key_ref), (value_hbm, value_ref))
    copies = [
        pltpu.make_async_copy(source, target, semaphores.at[index])
        for index, (source, target) in enumerate(pairs)
    ]
    for copy in copies:
        copy.start()
    for copy in copies:
        copy.wait()
    for head in range(key_ref.shape[0] // HEAD_DIM):
        rows = slice(head * HEAD_DIM, (head + 1) * HEAD_DIM)
        both = jnp.concatenate([key_ref[rows], value_ref[rows]], axis=0)
        picked = mm(near_chooser(offset_ref[head]), both, 1, 1)
        near_ref[head * NEAR : (head + 1) * NEAR, :] = picked.astype(BF16)


def pair_count(key_pos, query_pos, offset):
    count = 1.0 + jnp.where(
        same_class(key_pos, offset, RB) & same_class(query_pos, offset, RB), 1.0, 0.0
    )
    return count + jnp.where(
        same_class(key_pos, offset, RC) & same_class(query_pos, offset, RC), 1.0, 0.0
    )


def local_kernel(
    offset_ref,
    query_ref,
    key_ref,
    value_ref,
    grad_ref,
    weight_ref,
    near_ref,
    slots_ref,
    dout_ref,
    stats_ref,
):
    heads = query_ref.shape[0] // HEAD_DIM
    half = grad_ref.shape[0] // 2
    chunks = pl.cdiv(half, CHUNK)
    grad = grad_ref[...]
    dout = mm(weight_ref[...], grad, 1, 0).astype(BF16)
    dout_ref[...] = dout
    choosers = [far_chooser(offset_ref[head], 3) for head in range(heads)]
    choosers = jnp.concatenate(choosers, axis=0)
    wide = grad.astype(F32)
    filler = jnp.zeros((LANES - 2 * CHUNK, TOKENS_HERE), F32)
    far_grads = []
    for chunk in range(chunks):
        both = [chunk_rows(wide[:half], chunk), chunk_rows(wide[half:], chunk), filler]
        far_grads.append(mm(choosers, jnp.concatenate(both, axis=0).astype(BF16), 1, 1))
    blank = jnp.zeros((HEAD_DIM, TOKENS_HERE), BF16)
    key_pos = iota((TOKENS_HERE, TOKENS_HERE), 0)
    query_pos = iota((TOKENS_HERE, TOKENS_HERE), 1)
    query_row = iota((1, TOKENS_HERE), 1)
    for head in range(heads):
        offset = offset_ref[head]
        rows = slice(head * HEAD_DIM, (head + 1) * HEAD_DIM)
        query, key, value = query_ref[rows], key_ref[rows], value_ref[rows]
        near = near_ref[head * NEAR : (head + 1) * NEAR]
        dout_head = dout[rows]
        query_over = jnp.concatenate([query, blank], axis=0)
        in_near = same_class(query_row, offset, RC)
        in_far = same_class(query_row, offset, RE)

        scores = mm(key, query, 0, 0) * SCORE_SCALE
        near_scores = mm(near, query_over, 1, 0) * SCORE_SCALE
        near_max = jnp.max(near_scores, axis=0, keepdims=True)
        peak = jnp.max(scores, axis=0, keepdims=True)
        peak = jnp.where(in_near, jnp.maximum(peak, near_max), peak)
        mass = pair_count(key_pos, query_pos, offset) * jnp.exp(scores - peak)
        near_mass = jnp.where(in_near, jnp.exp(near_scores - peak), 0.0)
        total = jnp.sum(mass, axis=0, keepdims=True) + jnp.sum(near_mass, axis=0, keepdims=True)
        log_mass = peak + jnp.log(total)
        inverse = 1.0 / total
        probs_low = (mass * inverse).astype(BF16)
        near_low = (near_mass * inverse).astype(BF16)
        attended = mm(value, probs_low, 1, 0) + mm(near, near_low, 0, 0)[HEAD_DIM:]
        delta = jnp.sum(dout_head.astype(F32) * attended, axis=0, keepdims=True)
        place = iota((SMALL, TOKENS_HERE), 0)
        stats_ref[head * SMALL : (head + 1) * SMALL] = jnp.where(place == 0, log_mass, delta)

        attended_kept = jnp.where(in_far, 0.0, attended).astype(BF16)
        over = jnp.concatenate([attended_kept, blank], axis=0)
        under = jnp.concatenate([blank, attended_kept], axis=0)
        weight_part = mm(grad[:half], over, 1, 1) + mm(grad[half:], under, 1, 1)
        weight_part = weight_part * WEIGHT_SCALE
        query_key = jnp.concatenate([query, key], axis=0)
        value_dout = jnp.concatenate([value, dout_head], axis=0)
        stats = lay_stats((HEAD_DIM, TOKENS_HERE), 0, 0, (log_mass, delta))
        attended_stats = jnp.concatenate([attended.astype(BF16), stats.astype(BF16)], axis=0)
        mine = mm(far_chooser(offset, 0), query_key, 1, 1)
        mine = mine + mm(far_chooser(offset, 1), value_dout, 1, 1)
        mine = mine + mm(far_chooser(offset, 2), attended_stats, 1, 1)
        for chunk in range(chunks):
            far_grad = far_grads[chunk][head * GAP : head * GAP + SMALL]
            parts = [chunk_rows(weight_part, chunk), mine[:SMALL] + far_grad]
            slots_ref[head * chunks + chunk] = jnp.concatenate(parts, axis=0).astype(BF16)
    rest = slots_ref.shape[0] - heads * chunks
    slots_ref[heads * chunks :] = jnp.zeros((rest,) + slots_ref.shape[1:], BF16)


def local_grad_kernel(
    offset_ref,
    query_ref,
    key_ref,
    value_ref,
    dout_ref,
    stats_ref,
    near_ref,
    back_ref,
    grad_query_ref,
    grad_key_ref,
    grad_value_ref,
):
    heads = query_ref.shape[0] // HEAD_DIM
    blank = jnp.zeros((HEAD_DIM, TOKENS_HERE), BF16)
    key_pos = iota((TOKENS_HERE, TOKENS_HERE), 0)
    query_pos = iota((TOKENS_HERE, TOKENS_HERE), 1)
    query_row = iota((1, TOKENS_HERE), 1)
    far_rows = jnp.zeros((GAP, LANES), F32)
    for head in range(heads):
        offset = offset_ref[head]
        rows = slice(head * HEAD_DIM, (head + 1) * HEAD_DIM)
        near_rows = slice(head * NEAR, (head + 1) * NEAR)
        query, key, value = query_ref[rows], key_ref[rows], value_ref[rows]
        near = near_ref[near_rows]
        dout_head = dout_ref[rows]
        log_mass = stats_ref[head * SMALL : head * SMALL + 1]
        delta = stats_ref[head * SMALL + 1 : head * SMALL + 2]
        query_over = jnp.concatenate([query, blank], axis=0)
        dout_under = jnp.concatenate([blank, dout_head], axis=0)
        in_near = same_class(query_row, offset, RC)
        in_far = same_class(query_row, offset, RE)
        near_only = in_near & jnp.logical_not(in_far)

        scores = mm(key, query, 0, 0) * SCORE_SCALE
        near_scores = mm(near, query_over, 1, 0) * SCORE_SCALE
        probs = pair_count(key_pos, query_pos, offset) * jnp.exp(scores - log_mass)
        probs = jnp.where(in_far, 0.0, probs)
        near_probs = jnp.where(near_only, jnp.exp(near_scores - log_mass), 0.0)
        grad_scores = (probs * (mm(value, dout_head, 0, 0) - delta)).astype(BF16)
        near_grad_scores = (near_probs * (mm(near, dout_under, 1, 0) - delta)).astype(BF16)
        grad_query_ref[rows] = (
            mm(key, grad_scores, 1, 0) + mm(near, near_grad_scores, 0, 0)[:HEAD_DIM]
        )
        grad_key_ref[rows] = mm(query, grad_scores, 1, 1)
        grad_value_ref[rows] = mm(dout_head, probs.astype(BF16), 1, 1)
        back = mm(near_grad_scores, query_over, 1, 1)
        back = back + mm(near_probs.astype(BF16), dout_under, 1, 1)
        back_ref[near_rows] = back.astype(BF16)
        query_dout = jnp.concatenate([query, dout_head], axis=0)
        far_rows = far_rows + mm(far_chooser(offset, head), query_dout, 1, 1)
    back_ref[heads * NEAR :] = far_rows.astype(BF16)


def merge_kernel(slots_ref, merged_ref, far_ref):
    sources = slots_ref.shape[0]
    total = jnp.zeros((SLOT, LANES), F32)
    for source in range(sources):
        block = slots_ref[source].astype(F32)
        total = total + block
        far_ref[source * SMALL : (source + 1) * SMALL] = block[CHUNK:]
    pieces = [far_ref[pl.ds(kind, sources, stride=SMALL), :] for kind in range(SMALL)]
    full = jnp.concatenate([total] + pieces, axis=0).astype(BF16)
    for plane in range(PLANES):
        merged_ref[plane] = full


def far_kernel(plane_ref, merged_ref, slots_ref, returned_ref):
    sources = slots_ref.shape[0]
    width = 2 * sources
    count = PLANES * width

    def kind(index):
        start = SLOT + index * width
        return merged_ref[:, start : start + width, :].reshape(count, LANES)

    query_key, value_dout, attended_stats, far_grad = (kind(index) for index in range(4))
    shape = (LANES, HEAD_DIM)
    lower = one_hot(iota(shape, 0) == iota(shape, 1) + HEAD_DIM)
    query, value = query_key[:, :HEAD_DIM], value_dout[:, :HEAD_DIM]
    key, dout = (mm(both, lower, 1, 0).astype(BF16) for both in (query_key, value_dout))
    local_attended = attended_stats[:, :HEAD_DIM].astype(F32)
    stats = attended_stats.astype(F32)
    local_mass = take_stat(stats, 0)

    scores = mm(query, key, 1, 1) * SCORE_SCALE
    peak = jnp.maximum(jnp.max(scores, axis=1, keepdims=True), local_mass)
    mass = jnp.exp(scores - peak)
    local_part = jnp.exp(local_mass - peak)
    total = jnp.sum(mass, axis=1, keepdims=True) + local_part
    normalizer = peak + jnp.log(total)
    inverse = 1.0 / total
    probs = mass * inverse
    probs_low = probs.astype(BF16)
    attended = local_part * inverse * local_attended + mm(probs_low, value, 1, 0)
    delta = jnp.sum(dout.astype(F32) * attended, axis=1, keepdims=True)
    grad_probs = mm(dout, value, 1, 1)
    grad_scores = (probs * (grad_probs - delta)).astype(BF16)
    grad_query = mm(grad_scores, key, 1, 0).astype(BF16)
    grad_key = mm(grad_scores, query, 0, 0).astype(BF16)
    grad_value = mm(probs_low, dout, 0, 0).astype(BF16)

    def other_plane(column):
        blocks = [column[(p ^ 1) * width : ((p ^ 1) + 1) * width] for p in range(PLANES)]
        return jnp.concatenate(blocks, axis=0)

    shape = (HEAD_DIM, LANES)
    to_left = one_hot(iota(shape, 0) == iota(shape, 1))
    to_right = one_hot(iota(shape, 0) + HEAD_DIM == iota(shape, 1))
    attended_low = attended.astype(BF16)
    over = mm(attended_low, to_left, 1, 0).astype(BF16)
    under = mm(attended_low, to_right, 1, 0).astype(BF16)
    weight_part = mm(far_grad, over, 0, 0)[:CHUNK] + mm(far_grad, under, 0, 0)[CHUNK : 2 * CHUNK]
    weight_part = weight_part * WEIGHT_SCALE
    for plane in range(PLANES):
        weight_part = weight_part + merged_ref[plane, :SLOT].astype(F32)[:CHUNK]
    own_stats = lay_stats((count, LANES), 1, HEAD_DIM, (normalizer, delta))
    other_stats = lay_stats(
        (count, LANES), 1, HEAD_DIM, (other_plane(normalizer), other_plane(delta))
    )
    returned_ref[0] = mm(grad_value, to_left, 1, 0) + other_stats
    returned_ref[1] = mm(grad_query, to_left, 1, 0) + own_stats
    returned_ref[2] = mm(grad_key, to_left, 1, 0)
    own = pl.ds(pl.multiple_of(plane_ref[0] * width, width), width)
    shape = (sources * SMALL, width)
    row, column = iota(shape, 0), iota(shape, 1)
    same = (row // SMALL) == (column % sources)
    slot_row, pair = row % SMALL, column // sources
    placed = jnp.zeros((sources * SMALL, LANES), F32)
    for index in range(returned_ref.shape[0]):
        chosen = one_hot(same & (slot_row == pair + 2 * index))
        placed = placed + mm(chosen, returned_ref[index, own, :].astype(BF16), 1, 0)
    for source in range(sources):
        parts = [weight_part, placed[source * SMALL : (source + 1) * SMALL]]
        slots_ref[source] = jnp.concatenate(parts, axis=0).astype(BF16)


def prepare_kernel(
    offset_ref,
    key_ref,
    value_ref,
    near_ref,
    own_ref,
    partner_ref,
    local_key_ref,
    local_value_ref,
    rows_ref,
    scores_ref,
    grad_probs_ref,
    keys_ref,
    chooser_ref,
    grad_key_ref,
    grad_value_ref,
):
    heads = key_ref.shape[0] // HEAD_DIM
    first_far = heads * NEAR
    blank = jnp.zeros((HEAD_DIM, TOKENS_HERE + LANES), BF16)
    shape = (GAP, GAP)
    row, column = iota(shape, 0), iota(shape, 1)
    widen = one_hot(iota((NEAR, LANES), 0) == iota((NEAR, LANES), 1))
    shape = (GAP, TOKENS_HERE + LANES)
    block_row, place = iota(shape, 0), iota(shape, 1)
    here = place < TOKENS_HERE
    from_partner, from_here = block_row < 2, (block_row >= 2) & (block_row < 4)
    for head in range(heads):
        offset = offset_ref[head]
        rows = slice(head * HEAD_DIM, (head + 1) * HEAD_DIM)
        block = slice(head * GAP, (head + 1) * GAP)
        key, value = key_ref[rows], value_ref[rows]
        near = mm(near_ref[block], widen, 0, 0).astype(BF16)
        keys = jnp.concatenate([key, near[:HEAD_DIM]], axis=1)
        values = jnp.concatenate([value, near[HEAD_DIM:]], axis=1)
        keys = jnp.concatenate([keys, blank], axis=0)
        values = jnp.concatenate([blank, values], axis=0)
        from_partner_far = one_hot((row < 2) & (column == row + 2 * head))
        from_own_far = one_hot((row >= 2) & (row < 4) & (column == row - 2 + 2 * head))
        chosen = mm(from_partner_far, partner_ref[first_far:], 1, 0)
        chosen = (chosen + mm(from_own_far, own_ref[first_far:], 1, 0)).astype(BF16)
        in_near = here & same_class(place, offset, RC)
        extra = jnp.where(here & same_class(place, offset, RB), 1.0, 0.0)
        extra = extra + jnp.where(in_near, 1.0, 0.0)
        mask_here = jnp.where(place < TOKENS_HERE + NEAR, jnp.log(1.0 + extra), ABSENT)
        mask = jnp.where(from_here, mask_here, ABSENT)
        mask = jnp.where(from_partner & in_near, 0.0, mask)
        rows_ref[block] = chosen
        scores_ref[block] = mm(chosen, keys, 1, 0) * SCORE_SCALE + mask
        grad_probs_ref[block] = mm(chosen, values, 1, 0)
        keys_ref[head] = keys
        for pair in range(3):
            chooser_ref[head, pair] = far_chooser(offset, pair)
        spread = mm(partner_ref[block], near_chooser(offset), 0, 0)
        grad_key_ref[rows] = local_key_ref[rows] + spread[:HEAD_DIM]
        grad_value_ref[rows] = local_value_ref[rows] + spread[HEAD_DIM:]


def final_kernel(
    rows_ref,
    scores_ref,
    grad_probs_ref,
    keys_ref,
    chooser_ref,
    local_query_ref,
    local_key_ref,
    local_value_ref,
    slots_ref,
    grad_query_ref,
    grad_key_ref,
    grad_value_ref,
    grad_weight_ref,
):
    heads = local_query_ref.shape[0] // HEAD_DIM
    half = grad_weight_ref.shape[1] // 2
    chunks = pl.cdiv(half, CHUNK)
    for head in range(heads):
        rows = slice(head * HEAD_DIM, (head + 1) * HEAD_DIM)
        block = slice(head * GAP, (head + 1) * GAP)
        pieces = [slots_ref[head * chunks + chunk].astype(F32) for chunk in range(chunks)]
        folded = jnp.concatenate([piece[:CHUNK] for piece in pieces], axis=0)[:half]
        unfolded = jnp.transpose(folded)
        grad_weight_ref[rows, :half] = unfolded[:HEAD_DIM]
        grad_weight_ref[rows, half:] = unfolded[HEAD_DIM:]

        returned = jnp.concatenate(
            [pieces[0][CHUNK:], jnp.zeros((GAP - SMALL, LANES), F32)], axis=0
        )
        chosen = rows_ref[block]
        probs = jnp.exp(scores_ref[block] - take_stat(returned, 0))
        grad_scores = (probs * (grad_probs_ref[block] - take_stat(returned, 1))).astype(BF16)
        probs_low = probs[:, :TOKENS_HERE].astype(BF16)
        far_query = (returned + mm(grad_scores, keys_ref[head], 1, 1)).astype(BF16)
        returned = returned.astype(BF16)
        grad_query = mm(far_query, chooser_ref[head, 1], 0, 0)[:HEAD_DIM]
        grad_key = mm(returned, chooser_ref[head, 2], 0, 0)[:HEAD_DIM]
        grad_key = grad_key + mm(chosen, grad_scores[:, :TOKENS_HERE], 0, 0)[:HEAD_DIM]
        grad_value = mm(returned, chooser_ref[head, 0], 0, 0)[:HEAD_DIM]
        grad_value = grad_value + mm(chosen, probs_low, 0, 0)[HEAD_DIM:]
        grad_query = (local_query_ref[rows] + grad_query) * SCORE_SCALE
        grad_key = (local_key_ref[rows] + grad_key) * SCORE_SCALE
        grad_query_ref[rows] = grad_query.astype(BF16)
        grad_key_ref[rows] = grad_key.astype(BF16)
        grad_value_ref[rows] = (local_value_ref[rows] + grad_value).astype(BF16)


def call(kernel, outs, arrays, scalars=0, scratch=(), space=pltpu.VMEM, limit=40 << 20):
    specs = [pl.BlockSpec(memory_space=pltpu.SMEM)] * scalars
    specs = specs + [pl.BlockSpec(memory_space=space)] * (len(arrays) - scalars)
    shapes = [jax.ShapeDtypeStruct(shape, dtype) for shape, dtype in outs]
    return pl.pallas_call(
        kernel,
        out_shape=shapes,
        in_specs=specs,
        out_specs=[pl.BlockSpec(memory_space=pltpu.VMEM)] * len(shapes),
        scratch_shapes=list(scratch),
        compiler_params=pltpu.CompilerParams(vmem_limit_bytes=limit),
        name=kernel.__name__,
    )(*arrays)


def local(queries, keys, values, grad_out, out_weight, offsets):
    features = queries.shape[0]
    model = out_weight.shape[1]
    heads = offsets.shape[0]
    sources = lax.axis_size("xz")
    near_shape = ((heads * NEAR, LANES), BF16)
    back_shape = ((heads * NEAR + GAP, LANES), BF16)
    slots_shape = ((sources, SLOT, LANES), BF16)
    merged_shape = ((PLANES, SLOT + sources * SMALL, LANES), BF16)
    wide_shape = ((features, TOKENS_HERE), F32)
    grad_shape = ((features, TOKENS_HERE), BF16)
    block_shape = ((heads * GAP, TOKENS_HERE + LANES), F32)
    other = [(i, i ^ 1) for i in range(PLANES)]

    scratch = [
        pltpu.SMEM(offsets.shape, offsets.dtype),
        pltpu.VMEM(keys.shape, keys.dtype),
        pltpu.VMEM(values.shape, values.dtype),
        pltpu.SemaphoreType.DMA((3,)),
    ]
    (near,) = call(
        near_kernel,
        [near_shape],
        (offsets, keys, values),
        scratch=scratch,
        space=pltpu.HBM,
        limit=LIMIT,
    )
    near = lax.ppermute(near, "yh", other)
    full_grad = lax.all_gather(grad_out, "dp", axis=0, tiled=True)
    slots, dout, stats = call(
        local_kernel,
        [slots_shape, grad_shape, ((heads * SMALL, TOKENS_HERE), F32)],
        (offsets, queries, keys, values, full_grad, out_weight, near),
        scalars=1,
    )
    slots = lax.all_to_all(slots, "xz", 0, 0, tiled=True)
    own, local_query, local_key, local_value = call(
        local_grad_kernel,
        [back_shape, wide_shape, wide_shape, wide_shape],
        (offsets, queries, keys, values, dout, stats, near),
        scalars=1,
    )
    (merged,) = call(
        merge_kernel,
        [merged_shape],
        (slots,),
        scratch=[pltpu.VMEM((sources * SMALL, LANES), F32)],
    )
    merged = lax.all_to_all(merged, "yh", 0, 0, tiled=True)
    partner = lax.ppermute(own, "yh", other)
    prepared = call(
        prepare_kernel,
        [
            near_shape,
            block_shape,
            block_shape,
            ((heads, LANES, TOKENS_HERE + LANES), BF16),
            ((heads, 3, GAP, TOKENS_HERE), BF16),
            wide_shape,
            wide_shape,
        ],
        (offsets, keys, values, near, own, partner, local_key, local_value),
        scalars=1,
    )
    merged, prepared, local_query = lax.optimization_barrier((merged, prepared, local_query))
    rows, scores, grad_probs, wide_keys, chooser, local_key, local_value = prepared
    plane = lax.axis_index("yh").reshape(1)
    (slots,) = call(
        far_kernel,
        [slots_shape],
        (plane, merged),
        scalars=1,
        scratch=[pltpu.VMEM((3, PLANES * sources * 2, LANES), F32)],
    )
    slots = lax.all_to_all(slots, "xz", 0, 0, tiled=True)
    return tuple(
        call(
            final_kernel,
            [grad_shape, grad_shape, grad_shape, ((features, model), F32)],
            (
                rows,
                scores,
                grad_probs,
                wide_keys,
                chooser,
                local_query,
                local_key,
                local_value,
                slots,
            ),
        )
    )


def solution(mesh):
    devices = mesh.devices.reshape(-1, PLANES, mesh.devices.shape[1])
    split_mesh = Mesh(devices, ("xz", "yh", "dp"))
    wide = P("dp", ("xz", "yh"))
    return jax.shard_map(
        local,
        mesh=split_mesh,
        in_specs=(wide, wide, wide, wide, P("dp", None), P("dp")),
        out_specs=(wide, wide, wide, P("dp", None)),
        check_vma=False,
    )
```

time: 89 us -> 83.7 us (0.940)
  the two profiles are of different devices: /device:TPU:16 before, /device:TPU:64 now
where the time goes in v4:
time: 83.7 us; the launch traced here: 83.3 us
  blocking collectives  53.2 us (64%)
  starting transfers between devices  14.4 us (17%)
  Pallas kernels  11.3 us (14%)
  waiting for transfers between devices  3.7 us (4%)
    all_to_all x2, blocking collectives, local(): slots = lax.all_to_all(slots, 'xz', 0, 0, tiled=True)  46.6 us
    pallas_call x7, Pallas kernels, call(): pl.pallas_call(kernel, out_shape=shapes, in_specs=specs, out_specs=[pl.Bl...  11.3 us
    all_gather x1, blocking collectives, local(): full_grad = lax.all_gather(grad_out, 'dp', axis=0, tiled=True)  6.54 us
    all_to_all x1, starting transfers between devices, local(): merged = lax.all_to_all(merged, 'yh', 0, 0, tiled=True)  4.89 us
    ppermute x1, starting transfers between devices, local(): partner = lax.ppermute(own, 'yh', other)  4.84 us
    ppermute x1, starting transfers between devices, local(): near = lax.ppermute(near, 'yh', other)  4.63 us
    ppermute x1, waiting for transfers between devices, local(): partner = lax.ppermute(own, 'yh', other)  2.22 us
  transfers between devices with their start and end apart: 3, of which 2 were waited for; matrix products, arithmetic and copies ran while one was open for 0% of the time, Pallas kernels for 4%

profile of v4, /device:TPU:64, one launch (start us, length us, event | category | flops | bytes accessed | tf_op | source)
XLA Modules:
  0.0 83.3 jit_solution(974345986661086197)
XLA Ops:
  0.6 0.0 copy-start.5
  0.6 0.0 copy-start.3
  0.7 1.8 %near_kernel.1 = bf16[48,128]{1,0:T(8,128)(2,1)} custom-call(s32[3]{0:T(128)} %offset_ref.5, bf16[192,256]{1,0:T(8,128)(2,1)} %key_ref.5, bf16[192,256]{1,0:T(8,128)(2,1)} %value_ref.5), custom_call_target="tpu_custom_call" | custom-call | tf_op jit(solution)/shard_map/near_kernel/pallas_call | solution.py:442
  2.5 0.0 copy-start
  2.5 0.0 copy-start.1
  2.5 0.0 copy-start.2
  2.5 0.0 copy-start.4
  2.5 4.6 %collective-permute-start = (bf16[48,128]{1,0:T(8,128)(2,1)}, bf16[48,128]{1,0:T(8,128)(2,1)S(1)}, u32[]{:S(2)}, u32[]{:S(2)}) collective-permute-start(bf16[48,128]{1,0:T(8,128)(2,1)} %near_kernel.1), channel_id=1, source_target_pairs={{0,4},{4,0},{8,12},{12,8},{1,5},{5,1},{9,13},{13,9},{2,6},{6,2},{1... | collective-permute-start | bytes 36872 | tf_op jit(solution)/shard_map/ppermute | solution.py:481
  7.1 0.0 copy-done.5
  7.2 6.5 %all_gather.3.grad_ref = bf16[768,256]{1,0:T(8,128)(2,1)S(1)} all-gather(bf16[192,256]{1,0:T(8,128)(2,1)S(1)} %copy-done.5), channel_id=1, replica_groups=mesh['xz'=32,'yh'=4,'dp'=4] {'dp'}, dimensions={0}, use_global_device_ids=true | all-gather | bytes 491520 | tf_op jit(solution)/shard_map/all_gather | solution.py:482
  13.7 0.0 collective-permute-done.near_ref
  13.7 0.0 copy-done.3
  13.7 0.0 copy-done
  13.7 0.0 copy-done.1
  13.7 0.0 copy-done.2
  13.7 0.0 copy-done.4
  13.7 2.5 %local_kernel.1 = (bf16[32,48,128]{2,1,0:T(8,128)(2,1)S(1)}, bf16[192,256]{1,0:T(8,128)(2,1)S(1)}, f32[24,256]{1,0:T(8,128)S(1)}) custom-call(s32[3]{0:T(128)S(1)} %copy-done.4, bf16[192,256]{1,0:T(8,128)(2,1)S(1)} %copy-done.2, bf16[192,256]{1,0:T(8,128)(2,1)S(1)} %copy-done, bf16[192,256]{1,0:T(8,128)(2,1)S(1)} %copy-done.1, ...), custom_call_target="tpu_custom_call" | custom-call | tf_op jit(solution)/shard_map/local_kernel/pallas_call | solution.py:442
  16.2 27.8 %all_to_all.15.slots_ref = bf16[32,48,128]{2,1,0:T(8,128)(2,1)S(1)} all-to-all(bf16[32,48,128]{2,1,0:T(8,128)(2,1)S(1)} %get-tuple-element.27), channel_id=1, replica_groups=mesh['xz'=32,'yh'=4,'dp'=4] {'xz'}, dimensions={0} | all-to-all | bytes 786432 | tf_op jit(solution)/shard_map/all_to_all | solution.py:489
  44.0 0.8 merge_kernel.1
  44.8 4.9 %all-to-all-start.1 = ((bf16[4,304,128]{2,1,0:T(8,128)(2,1)}), bf16[4,304,128]{2,1,0:T(8,128)(2,1)S(1)}, u32[]{:S(2)}, u32[]{:S(2)}) async-start(bf16[4,304,128]{2,1,0:T(8,128)(2,1)} %merge_kernel.1), calls=%async_computation.1 | async-start | bytes 622592 | tf_op jit(solution)/shard_map/all_to_all | solution.py:502
  49.7 1.7 %local_grad_kernel.1 = (bf16[64,128]{1,0:T(8,128)(2,1)S(1)}, f32[192,256]{1,0:T(8,128)S(1)}, f32[192,256]{1,0:T(8,128)S(1)}, f32[192,256]{1,0:T(8,128)S(1)}) custom-call(s32[3]{0:T(128)S(1)} %copy-done.4, bf16[192,256]{1,0:T(8,128)(2,1)S(1)} %copy-done.2, bf16[192,256]{1,0:T(8,128)(2,1)S(1)} %copy-done, bf16[192,256]{1,0:T(8,128)(2,1)S(1)} %copy-done.1, ...), custom_call_target="tpu_custom_call" | custom-call | tf_op jit(solution)/shard_map/local_grad_kernel/pallas_call | solution.py:442
  51.4 4.8 %collective-permute-start.1 = (bf16[64,128]{1,0:T(8,128)(2,1)S(1)}, bf16[64,128]{1,0:T(8,128)(2,1)S(1)}, u32[]{:S(2)}, u32[]{:S(2)}) collective-permute-start(bf16[64,128]{1,0:T(8,128)(2,1)S(1)} %get-tuple-element.30.own_ref), channel_id=1, source_target_pairs={{0,4},{4,0},{8,12},{12,8},{1,5},{5,1},{9,13},{13,9},{2,6},{6,2},{1... | collective-permute-start | bytes 49160 | tf_op jit(solution)/shard_map/ppermute | solution.py:503
  56.3 2.2 %collective-permute-done.1.partner_ref = bf16[64,128]{1,0:T(8,128)(2,1)S(1)} collective-permute-done((bf16[64,128]{1,0:T(8,128)(2,1)S(1)}, bf16[64,128]{1,0:T(8,128)(2,1)S(1)}, u32[]{:S(2)}, u32[]{:S(2)}) %collective-permute-start.1) | collective-permute-done | bytes 16416 | tf_op jit(solution)/shard_map/ppermute | solution.py:503
  58.5 1.2 %prepare_kernel.1 = (bf16[48,128]{1,0:T(8,128)(2,1)S(1)}, f32[48,384]{1,0:T(8,128)S(1)}, f32[48,384]{1,0:T(8,128)S(1)}, bf16[3,128,384]{2,1,0:T(8,128)(2,1)S(1)}...) custom-call(s32[3]{0:T(128)S(1)} %copy-done.4, ...), custom_call_target="tpu_custom_call" | custom-call | tf_op jit(solution)/shard_map/prepare_kernel/pallas_call | solution.py:442
  59.7 1.5 %all-to-all-done.1.merged_ref = bf16[4,304,128]{2,1,0:T(8,128)(2,1)S(1)} async-done(((bf16[4,304,128]{2,1,0:T(8,128)(2,1)}), bf16[4,304,128]{2,1,0:T(8,128)(2,1)S(1)}, u32[]{:S(2)}, u32[]{:S(2)}) %all-to-all-start.1) | async-done | bytes 311328 | tf_op jit(solution)/shard_map/all_to_all | solution.py:502
  61.2 1.5 %far_kernel.1 = bf16[32,48,128]{2,1,0:T(8,128)(2,1)S(1)} custom-call(s32[1]{0:T(128)} %bitcast.plane_ref, bf16[4,304,128]{2,1,0:T(8,128)(2,1)S(1)} %all-to-all-done.1.merged_ref), custom_call_target="tpu_custom_call" | custom-call | tf_op jit(solution)/shard_map/far_kernel/pallas_call | solution.py:442
  62.7 18.8 %all_to_all.16.slots_ref = bf16[32,48,128]{2,1,0:T(8,128)(2,1)S(1)} all-to-all(bf16[32,48,128]{2,1,0:T(8,128)(2,1)S(1)} %far_kernel.1), channel_id=1, replica_groups=mesh['xz'=32,'yh'=4,'dp'=4] {'xz'}, dimensions={0} | all-to-all | bytes 786432 | tf_op jit(solution)/shard_map/all_to_all | solution.py:528
  81.5 1.9 %final_kernel.1 = (bf16[192,256]{1,0:T(8,128)(2,1)}, bf16[192,256]{1,0:T(8,128)(2,1)}, bf16[192,256]{1,0:T(8,128)(2,1)}, f32[192,768]{1,0:T(8,128)}) custom-call(bf16[48,128]{1,0:T(8,128)(2,1)S(1)} %get-tuple-element.41.rows_ref, f32[48,384]{1,0:T(8,128)S(1)} %get-tuple-element.42.scores_ref, f32[48,384]{1,0:T(8,128)S(1)} %get-tuple-element.43.grad_probs_ref, ...), custom_call_target="tpu_custom_call" | custom-call | tf_op jit(solution)/shard_map/final_kernel/pallas_call | solution.py:442
Async XLA Ops:
  0.6 6.5 %copy-start.5 = (bf16[192,256]{1,0:T(8,128)(2,1)S(1)}, bf16[192,256]{1,0:T(8,128)(2,1)}, u32[]{:S(2)}) copy-start(bf16[192,256]{1,0:T(8,128)(2,1)} %param.9) | copy-start | bytes 294916
  0.6 13.1 %copy-start.3 = (bf16[192,768]{1,0:T(8,128)(2,1)S(1)}, bf16[192,768]{1,0:T(8,128)(2,1)}, u32[]{:S(2)}) copy-start(bf16[192,768]{1,0:T(8,128)(2,1)} %weight_ref.1) | copy-start | bytes 884740
  2.5 11.2 %copy-start = (bf16[192,256]{1,0:T(8,128)(2,1)S(1)}, bf16[192,256]{1,0:T(8,128)(2,1)}, u32[]{:S(2)}) copy-start(bf16[192,256]{1,0:T(8,128)(2,1)} %key_ref.5) | copy-start | bytes 294916
  2.5 11.2 %copy-start.1 = (bf16[192,256]{1,0:T(8,128)(2,1)S(1)}, bf16[192,256]{1,0:T(8,128)(2,1)}, u32[]{:S(2)}) copy-start(bf16[192,256]{1,0:T(8,128)(2,1)} %value_ref.5) | copy-start | bytes 294916
  2.5 11.2 %copy-start.2 = (bf16[192,256]{1,0:T(8,128)(2,1)S(1)}, bf16[192,256]{1,0:T(8,128)(2,1)}, u32[]{:S(2)}) copy-start(bf16[192,256]{1,0:T(8,128)(2,1)} %query_ref.3) | copy-start | bytes 294916
  2.5 11.2 %copy-start.4 = (s32[3]{0:T(128)S(1)}, s32[3]{0:T(128)}, u32[]{:S(2)}) copy-start(s32[3]{0:T(128)} %offset_ref.5) | copy-start | bytes 40
  2.5 11.2 %collective-permute-start = (bf16[48,128]{1,0:T(8,128)(2,1)}, bf16[48,128]{1,0:T(8,128)(2,1)S(1)}, u32[]{:S(2)}, u32[]{:S(2)}) collective-permute-start(bf16[48,128]{1,0:T(8,128)(2,1)} %near_kernel.1), channel_id=1, source_target_pairs={{0,4},{4,0},{8,12},{12,8},{1,5},{5,1},{9,13},{13,9},{2,6},{6,2},{1... | collective-permute-start | bytes 36872 | tf_op jit(solution)/shard_map/ppermute | solution.py:481
  44.8 16.4 %all-to-all-start.1 = ((bf16[4,304,128]{2,1,0:T(8,128)(2,1)}), bf16[4,304,128]{2,1,0:T(8,128)(2,1)S(1)}, u32[]{:S(2)}, u32[]{:S(2)}) async-start(bf16[4,304,128]{2,1,0:T(8,128)(2,1)} %merge_kernel.1), calls=%async_computation.1 | async-start | bytes 622592 | tf_op jit(solution)/shard_map/all_to_all | solution.py:502
  51.4 7.1 %collective-permute-start.1 = (bf16[64,128]{1,0:T(8,128)(2,1)S(1)}, bf16[64,128]{1,0:T(8,128)(2,1)S(1)}, u32[]{:S(2)}, u32[]{:S(2)}) collective-permute-start(bf16[64,128]{1,0:T(8,128)(2,1)S(1)} %get-tuple-element.30.own_ref), channel_id=1, source_target_pairs={{0,4},{4,0},{8,12},{12,8},{1,5},{5,1},{9,13},{13,9},{2,6},{6,2},{1... | collective-permute-start | bytes 49160 | tf_op jit(solution)/shard_map/ppermute | solution.py:503

commit v5 on v4

--- a/solution.py
+++ b/solution.py
@@ -145,49 +145,61 @@
     key_pos = iota((TOKENS_HERE, TOKENS_HERE), 0)
     query_pos = iota((TOKENS_HERE, TOKENS_HERE), 1)
     query_row = iota((1, TOKENS_HERE), 1)
-    for head in range(heads):
-        offset = offset_ref[head]
-        rows = slice(head * HEAD_DIM, (head + 1) * HEAD_DIM)
-        query, key, value = query_ref[rows], key_ref[rows], value_ref[rows]
-        near = near_ref[head * NEAR : (head + 1) * NEAR]
-        dout_head = dout[rows]
-        query_over = jnp.concatenate([query, blank], axis=0)
-        in_near = same_class(query_row, offset, RC)
-        in_far = same_class(query_row, offset, RE)
-
-        scores = mm(key, query, 0, 0) * SCORE_SCALE
-        near_scores = mm(near, query_over, 1, 0) * SCORE_SCALE
-        near_max = jnp.max(near_scores, axis=0, keepdims=True)
-        peak = jnp.max(scores, axis=0, keepdims=True)
-        peak = jnp.where(in_near, jnp.maximum(peak, near_max), peak)
-        mass = pair_count(key_pos, query_pos, offset) * jnp.exp(scores - peak)
-        near_mass = jnp.where(in_near, jnp.exp(near_scores - peak), 0.0)
-        total = jnp.sum(mass, axis=0, keepdims=True) + jnp.sum(near_mass, axis=0, keepdims=True)
-        log_mass = peak + jnp.log(total)
-        inverse = 1.0 / total
-        probs_low = (mass * inverse).astype(BF16)
-        near_low = (near_mass * inverse).astype(BF16)
-        attended = mm(value, probs_low, 1, 0) + mm(near, near_low, 0, 0)[HEAD_DIM:]
-        delta = jnp.sum(dout_head.astype(F32) * attended, axis=0, keepdims=True)
-        place = iota((SMALL, TOKENS_HERE), 0)
-        stats_ref[head * SMALL : (head + 1) * SMALL] = jnp.where(place == 0, log_mass, delta)
-
-        attended_kept = jnp.where(in_far, 0.0, attended).astype(BF16)
-        over = jnp.concatenate([attended_kept, blank], axis=0)
-        under = jnp.concatenate([blank, attended_kept], axis=0)
-        weight_part = mm(grad[:half], over, 1, 1) + mm(grad[half:], under, 1, 1)
-        weight_part = weight_part * WEIGHT_SCALE
-        query_key = jnp.concatenate([query, key], axis=0)
-        value_dout = jnp.concatenate([value, dout_head], axis=0)
-        stats = lay_stats((HEAD_DIM, TOKENS_HERE), 0, 0, (log_mass, delta))
-        attended_stats = jnp.concatenate([attended.astype(BF16), stats.astype(BF16)], axis=0)
-        mine = mm(far_chooser(offset, 0), query_key, 1, 1)
-        mine = mine + mm(far_chooser(offset, 1), value_dout, 1, 1)
-        mine = mine + mm(far_chooser(offset, 2), attended_stats, 1, 1)
+    heads = range(heads)
+    offsets = [offset_ref[head] for head in heads]
+    rows = [slice(head * HEAD_DIM, (head + 1) * HEAD_DIM) for head in heads]
+    near = [near_ref[head * NEAR : (head + 1) * NEAR] for head in heads]
+    in_near = [same_class(query_row, offset, RC) for offset in offsets]
+    in_far = [same_class(query_row, offset, RE) for offset in offsets]
+    scores = [mm(key_ref[rows[h]], query_ref[rows[h]], 0, 0) * SCORE_SCALE for h in heads]
+    near_scores = [
+        mm(near[h], jnp.concatenate([query_ref[rows[h]], blank], axis=0), 1, 0) * SCORE_SCALE
+        for h in heads
+    ]
+    peak = [jnp.max(scores[h], axis=0, keepdims=True) for h in heads]
+    near_max = [jnp.max(near_scores[h], axis=0, keepdims=True) for h in heads]
+    peak = [jnp.where(in_near[h], jnp.maximum(peak[h], near_max[h]), peak[h]) for h in heads]
+    mass = [
+        pair_count(key_pos, query_pos, offsets[h]) * jnp.exp(scores[h] - peak[h]) for h in heads
+    ]
+    near_mass = [jnp.where(in_near[h], jnp.exp(near_scores[h] - peak[h]), 0.0) for h in heads]
+    total = [
+        jnp.sum(mass[h], axis=0, keepdims=True) + jnp.sum(near_mass[h], axis=0, keepdims=True)
+        for h in heads
+    ]
+    log_mass = [peak[h] + jnp.log(total[h]) for h in heads]
+    inverse = [1.0 / total[h] for h in heads]
+    probs_low = [(mass[h] * inverse[h]).astype(BF16) for h in heads]
+    near_low = [(near_mass[h] * inverse[h]).astype(BF16) for h in heads]
+    attended = [
+        mm(value_ref[rows[h]], probs_low[h], 1, 0) + mm(near[h], near_low[h], 0, 0)[HEAD_DIM:]
+        for h in heads
+    ]
+    kept = [jnp.where(in_far[h], 0.0, attended[h]).astype(BF16) for h in heads]
+    over = [jnp.concatenate([kept[h], blank], axis=0) for h in heads]
+    under = [jnp.concatenate([blank, kept[h]], axis=0) for h in heads]
+    weight_part = [
+        (mm(grad[:half], over[h], 1, 1) + mm(grad[half:], under[h], 1, 1)) * WEIGHT_SCALE
+        for h in heads
+    ]
+    delta = [
+        jnp.sum(dout[rows[h]].astype(F32) * attended[h], axis=0, keepdims=True) for h in heads
+    ]
+    place = iota((SMALL, TOKENS_HERE), 0)
+    for h in heads:
+        query_key = jnp.concatenate([query_ref[rows[h]], key_ref[rows[h]]], axis=0)
+        value_dout = jnp.concatenate([value_ref[rows[h]], dout[rows[h]]], axis=0)
+        stats = lay_stats((HEAD_DIM, TOKENS_HERE), 0, 0, (log_mass[h], delta[h]))
+        attended_stats = jnp.concatenate([attended[h].astype(BF16), stats.astype(BF16)], axis=0)
+        mine = mm(far_chooser(offsets[h], 0), query_key, 1, 1)
+        mine = mine + mm(far_chooser(offsets[h], 1), value_dout, 1, 1)
+        mine = mine + mm(far_chooser(offsets[h], 2), attended_stats, 1, 1)
+        stats_ref[h * SMALL : (h + 1) * SMALL] = jnp.where(place == 0, log_mass[h], delta[h])
         for chunk in range(chunks):
-            far_grad = far_grads[chunk][head * GAP : head * GAP + SMALL]
-            parts = [chunk_rows(weight_part, chunk), mine[:SMALL] + far_grad]
-            slots_ref[head * chunks + chunk] = jnp.concatenate(parts, axis=0).astype(BF16)
+            far_grad = far_grads[chunk][h * GAP : h * GAP + SMALL]
+            parts = [chunk_rows(weight_part[h], chunk), mine[:SMALL] + far_grad]
+            slots_ref[h * chunks + chunk] = jnp.concatenate(parts, axis=0).astype(BF16)
+    heads = len(heads)
     rest = slots_ref.shape[0] - heads * chunks
     slots_ref[heads * chunks :] = jnp.zeros((rest,) + slots_ref.shape[1:], BF16)
 
@@ -493,13 +505,6 @@
         (offsets, queries, keys, values, dout, stats, near),
         scalars=1,
     )
-    (merged,) = call(
-        merge_kernel,
-        [merged_shape],
-        (slots,),
-        scratch=[pltpu.VMEM((sources * SMALL, LANES), F32)],
-    )
-    merged = lax.all_to_all(merged, "yh", 0, 0, tiled=True)
     partner = lax.ppermute(own, "yh", other)
     prepared = call(
         prepare_kernel,
@@ -515,9 +520,18 @@
         (offsets, keys, values, near, own, partner, local_key, local_value),
         scalars=1,
     )
-    merged, prepared, local_query = lax.optimization_barrier((merged, prepared, local_query))
+    plane = lax.axis_index("yh").reshape(1)
+    slots, prepared, local_query, plane = lax.optimization_barrier(
+        (slots, prepared, local_query, plane)
+    )
     rows, scores, grad_probs, wide_keys, chooser, local_key, local_value = prepared
-    plane = lax.axis_index("yh").reshape(1)
+    (merged,) = call(
+        merge_kernel,
+        [merged_shape],
+        (slots,),
+        scratch=[pltpu.VMEM((sources * SMALL, LANES), F32)],
+    )
+    merged = lax.all_to_all(merged, "yh", 0, 0, tiled=True)
     (slots,) = call(
         far_kernel,
         [slots_shape],

time: 83.7 us -> 82.8 us (0.989)
  the two profiles are of different devices: /device:TPU:64 before, /device:TPU:16 now
where the time goes in v5:
time: 82.8 us; the launch traced here: 82.4 us
  blocking collectives  43.2 us (52%)
  starting transfers between devices  20.4 us (25%)
  Pallas kernels  10.8 us (13%)
  waiting for transfers between devices  7.12 us (9%)
    all_to_all x1, blocking collectives, local(): slots = lax.all_to_all(slots, 'xz', 0, 0, tiled=True)  21.6 us
    all_to_all x1, blocking collectives, local(): merged = lax.all_to_all(merged, 'yh', 0, 0, tiled=True)  15.5 us
    pallas_call x7, Pallas kernels, call(): pl.pallas_call(kernel, out_shape=shapes, in_specs=specs, out_specs=[pl.Bl...  10.8 us
    all_to_all x1, starting transfers between devices, local(): slots = lax.all_to_all(slots, 'xz', 0, 0, tiled=True)  8.19 us
    ppermute x1, starting transfers between devices, local(): near = lax.ppermute(near, 'yh', other)  7.75 us
    all_gather x1, blocking collectives, local(): full_grad = lax.all_gather(grad_out, 'dp', axis=0, tiled=True)  6.15 us
    all_to_all x1, waiting for transfers between devices, local(): slots = lax.all_to_all(slots, 'xz', 0, 0, tiled=True)  5.06 us
    ppermute x1, starting transfers between devices, local(): partner = lax.ppermute(own, 'yh', other)  4.5 us
  transfers between devices with their start and end apart: 3, of which 2 were waited for; matrix products, arithmetic and copies ran while one was open for 0% of the time, Pallas kernels for 4%

profile of v5, /device:TPU:16, one launch (start us, length us, event | category | flops | bytes accessed | tf_op | source)
XLA Modules:
  0.0 82.4 jit_solution(2767039361388241244)
XLA Ops:
  0.6 0.0 copy-start.5
  0.6 0.0 copy-start.3
  0.7 1.8 %near_kernel.1 = bf16[48,128]{1,0:T(8,128)(2,1)} custom-call(s32[3]{0:T(128)} %offset_ref.5, bf16[192,256]{1,0:T(8,128)(2,1)} %key_ref.5, bf16[192,256]{1,0:T(8,128)(2,1)} %value_ref.5), custom_call_target="tpu_custom_call" | custom-call | tf_op jit(solution)/shard_map/near_kernel/pallas_call | solution.py:454
  2.5 0.0 copy-start
  2.5 0.0 copy-start.1
  2.5 0.0 copy-start.2
  2.5 0.0 copy-start.4
  2.5 7.7 %collective-permute-start = (bf16[48,128]{1,0:T(8,128)(2,1)}, bf16[48,128]{1,0:T(8,128)(2,1)S(1)}, u32[]{:S(2)}, u32[]{:S(2)}) collective-permute-start(bf16[48,128]{1,0:T(8,128)(2,1)} %near_kernel.1), channel_id=1, source_target_pairs={{0,4},{4,0},{8,12},{12,8},{1,5},{5,1},{9,13},{13,9},{2,6},{6,2},{1... | collective-permute-start | bytes 36872 | tf_op jit(solution)/shard_map/ppermute | solution.py:493
  10.3 0.0 copy-done.5
  10.3 6.1 %all_gather.3.grad_ref = bf16[768,256]{1,0:T(8,128)(2,1)S(1)} all-gather(bf16[192,256]{1,0:T(8,128)(2,1)S(1)} %copy-done.5), channel_id=1, replica_groups=mesh['xz'=32,'yh'=4,'dp'=4] {'dp'}, dimensions={0}, use_global_device_ids=true | all-gather | bytes 491520 | tf_op jit(solution)/shard_map/all_gather | solution.py:494
  16.4 0.0 collective-permute-done.near_ref
  16.4 0.0 copy-done.3
  16.4 0.0 copy-done
  16.4 0.0 copy-done.1
  16.4 0.0 copy-done.2
  16.4 0.0 copy-done.4
  16.5 2.7 %local_kernel.1 = (bf16[32,48,128]{2,1,0:T(8,128)(2,1)}, bf16[192,256]{1,0:T(8,128)(2,1)S(1)}, f32[24,256]{1,0:T(8,128)S(1)}) custom-call(s32[3]{0:T(128)S(1)} %copy-done.4, bf16[192,256]{1,0:T(8,128)(2,1)S(1)} %copy-done.2, bf16[192,256]{1,0:T(8,128)(2,1)S(1)} %copy-done, bf16[192,256]{1,0:T(8,128)(2,1)S(1)} %copy-done.1, ...), custom_call_target="tpu_custom_call" | custom-call | tf_op jit(solution)/shard_map/local_kernel/pallas_call | solution.py:454
  19.1 8.2 %all-to-all-start = ((bf16[32,48,128]{2,1,0:T(8,128)(2,1)}), bf16[32,48,128]{2,1,0:T(8,128)(2,1)S(1)}, u32[]{:S(2)}, u32[]{:S(2)}) async-start(bf16[32,48,128]{2,1,0:T(8,128)(2,1)} %get-tuple-element.28), calls=%async_computation | async-start | bytes 786432 | tf_op jit(solution)/shard_map/all_to_all | solution.py:501
  27.3 1.7 %local_grad_kernel.1 = (bf16[64,128]{1,0:T(8,128)(2,1)S(1)}, f32[192,256]{1,0:T(8,128)S(1)}, f32[192,256]{1,0:T(8,128)S(1)}, f32[192,256]{1,0:T(8,128)S(1)}) custom-call(s32[3]{0:T(128)S(1)} %copy-done.4, bf16[192,256]{1,0:T(8,128)(2,1)S(1)} %copy-done.2, bf16[192,256]{1,0:T(8,128)(2,1)S(1)} %copy-done, bf16[192,256]{1,0:T(8,128)(2,1)S(1)} %copy-done.1, ...), custom_call_target="tpu_custom_call" | custom-call | tf_op jit(solution)/shard_map/local_grad_kernel/pallas_call | solution.py:454
  29.1 4.5 %collective-permute-start.1 = (bf16[64,128]{1,0:T(8,128)(2,1)S(1)}, bf16[64,128]{1,0:T(8,128)(2,1)S(1)}, u32[]{:S(2)}, u32[]{:S(2)}) collective-permute-start(bf16[64,128]{1,0:T(8,128)(2,1)S(1)} %get-tuple-element.31.own_ref), channel_id=1, source_target_pairs={{0,4},{4,0},{8,12},{12,8},{1,5},{5,1},{9,13},{13,9},{2,6},{6,2},{1... | collective-permute-start | bytes 49160 | tf_op jit(solution)/shard_map/ppermute | solution.py:508
  33.6 2.1 %collective-permute-done.1.partner_ref = bf16[64,128]{1,0:T(8,128)(2,1)S(1)} collective-permute-done((bf16[64,128]{1,0:T(8,128)(2,1)S(1)}, bf16[64,128]{1,0:T(8,128)(2,1)S(1)}, u32[]{:S(2)}, u32[]{:S(2)}) %collective-permute-start.1) | collective-permute-done | bytes 16416 | tf_op jit(solution)/shard_map/ppermute | solution.py:508
  35.6 1.2 %prepare_kernel.1 = (bf16[48,128]{1,0:T(8,128)(2,1)S(1)}, f32[48,384]{1,0:T(8,128)S(1)}, f32[48,384]{1,0:T(8,128)S(1)}, bf16[3,128,384]{2,1,0:T(8,128)(2,1)S(1)}...) custom-call(s32[3]{0:T(128)S(1)} %copy-done.4, ...), custom_call_target="tpu_custom_call" | custom-call | tf_op jit(solution)/shard_map/prepare_kernel/pallas_call | solution.py:454
  36.9 5.1 %all-to-all-done.slots_ref = bf16[32,48,128]{2,1,0:T(8,128)(2,1)S(1)} async-done(((bf16[32,48,128]{2,1,0:T(8,128)(2,1)}), bf16[32,48,128]{2,1,0:T(8,128)(2,1)S(1)}, u32[]{:S(2)}, u32[]{:S(2)}) %all-to-all-start) | async-done | bytes 393248 | tf_op jit(solution)/shard_map/all_to_all | solution.py:501
  41.9 0.1 merge_kernel.1
  42.0 15.5 %all_to_all.15.merged_ref = bf16[4,304,128]{2,1,0:T(8,128)(2,1)S(1)} all-to-all(bf16[4,304,128]{2,1,0:T(8,128)(2,1)S(1)} %merge_kernel.1), channel_id=1, replica_groups=mesh['xz'=32,'yh'=4,'dp'=4] {'yh'}, dimensions={0} | all-to-all | bytes 622592 | tf_op jit(solution)/shard_map/all_to_all | solution.py:534
  57.5 1.5 %far_kernel.1 = bf16[32,48,128]{2,1,0:T(8,128)(2,1)S(1)} custom-call(s32[1]{0:T(128)} %bitcast.plane_ref, bf16[4,304,128]{2,1,0:T(8,128)(2,1)S(1)} %all_to_all.15.merged_ref), custom_call_target="tpu_custom_call" | custom-call | tf_op jit(solution)/shard_map/far_kernel/pallas_call | solution.py:454
  59.0 21.6 %all_to_all.16.slots_ref = bf16[32,48,128]{2,1,0:T(8,128)(2,1)S(1)} all-to-all(bf16[32,48,128]{2,1,0:T(8,128)(2,1)S(1)} %far_kernel.1), channel_id=1, replica_groups=mesh['xz'=32,'yh'=4,'dp'=4] {'xz'}, dimensions={0} | all-to-all | bytes 786432 | tf_op jit(solution)/shard_map/all_to_all | solution.py:542
  80.5 1.9 %final_kernel.1 = (bf16[192,256]{1,0:T(8,128)(2,1)}, bf16[192,256]{1,0:T(8,128)(2,1)}, bf16[192,256]{1,0:T(8,128)(2,1)}, f32[192,768]{1,0:T(8,128)}) custom-call(bf16[48,128]{1,0:T(8,128)(2,1)S(1)} %get-tuple-element.42.rows_ref, f32[48,384]{1,0:T(8,128)S(1)} %get-tuple-element.43.scores_ref, f32[48,384]{1,0:T(8,128)S(1)} %get-tuple-element.44.grad_probs_ref, ...), custom_call_target="tpu_custom_call" | custom-call | tf_op jit(solution)/shard_map/final_kernel/pallas_call | solution.py:454
Async XLA Ops:
  0.6 9.6 %copy-start.5 = (bf16[192,256]{1,0:T(8,128)(2,1)S(1)}, bf16[192,256]{1,0:T(8,128)(2,1)}, u32[]{:S(2)}) copy-start(bf16[192,256]{1,0:T(8,128)(2,1)} %param.9) | copy-start | bytes 294916
  0.6 15.8 %copy-start.3 = (bf16[192,768]{1,0:T(8,128)(2,1)S(1)}, bf16[192,768]{1,0:T(8,128)(2,1)}, u32[]{:S(2)}) copy-start(bf16[192,768]{1,0:T(8,128)(2,1)} %weight_ref.1) | copy-start | bytes 884740
  2.5 14.0 %copy-start = (bf16[192,256]{1,0:T(8,128)(2,1)S(1)}, bf16[192,256]{1,0:T(8,128)(2,1)}, u32[]{:S(2)}) copy-start(bf16[192,256]{1,0:T(8,128)(2,1)} %key_ref.5) | copy-start | bytes 294916
  2.5 14.0 %copy-start.1 = (bf16[192,256]{1,0:T(8,128)(2,1)S(1)}, bf16[192,256]{1,0:T(8,128)(2,1)}, u32[]{:S(2)}) copy-start(bf16[192,256]{1,0:T(8,128)(2,1)} %value_ref.5) | copy-start | bytes 294916
  2.5 14.0 %copy-start.2 = (bf16[192,256]{1,0:T(8,128)(2,1)S(1)}, bf16[192,256]{1,0:T(8,128)(2,1)}, u32[]{:S(2)}) copy-start(bf16[192,256]{1,0:T(8,128)(2,1)} %query_ref.3) | copy-start | bytes 294916
  2.5 14.0 %copy-start.4 = (s32[3]{0:T(128)S(1)}, s32[3]{0:T(128)}, u32[]{:S(2)}) copy-start(s32[3]{0:T(128)} %offset_ref.5) | copy-start | bytes 40
  2.5 13.9 %collective-permute-start = (bf16[48,128]{1,0:T(8,128)(2,1)}, bf16[48,128]{1,0:T(8,128)(2,1)S(1)}, u32[]{:S(2)}, u32[]{:S(2)}) collective-permute-start(bf16[48,128]{1,0:T(8,128)(2,1)} %near_kernel.1), channel_id=1, source_target_pairs={{0,4},{4,0},{8,12},{12,8},{1,5},{5,1},{9,13},{13,9},{2,6},{6,2},{1... | collective-permute-start | bytes 36872 | tf_op jit(solution)/shard_map/ppermute | solution.py:493
  19.1 22.8 %all-to-all-start = ((bf16[32,48,128]{2,1,0:T(8,128)(2,1)}), bf16[32,48,128]{2,1,0:T(8,128)(2,1)S(1)}, u32[]{:S(2)}, u32[]{:S(2)}) async-start(bf16[32,48,128]{2,1,0:T(8,128)(2,1)} %get-tuple-element.28), calls=%async_computation | async-start | bytes 786432 | tf_op jit(solution)/shard_map/all_to_all | solution.py:501
  29.1 6.6 %collective-permute-start.1 = (bf16[64,128]{1,0:T(8,128)(2,1)S(1)}, bf16[64,128]{1,0:T(8,128)(2,1)S(1)}, u32[]{:S(2)}, u32[]{:S(2)}) collective-permute-start(bf16[64,128]{1,0:T(8,128)(2,1)S(1)} %get-tuple-element.31.own_ref), channel_id=1, source_target_pairs={{0,4},{4,0},{8,12},{12,8},{1,5},{5,1},{9,13},{13,9},{2,6},{6,2},{1... | collective-permute-start | bytes 49160 | tf_op jit(solution)/shard_map/ppermute | solution.py:508

commit v6 on v5

--- a/solution.py
+++ b/solution.py
@@ -117,6 +117,7 @@
 
 def local_kernel(
     offset_ref,
+    side_ref,
     query_ref,
     key_ref,
     value_ref,
@@ -128,9 +129,11 @@
     stats_ref,
 ):
     heads = query_ref.shape[0] // HEAD_DIM
-    half = grad_ref.shape[0] // 2
+    side = side_ref[0]
+    blocks = [grad_ref[2 * core + (chip ^ side)] for chip in range(2) for core in range(2)]
+    grad = jnp.concatenate(blocks, axis=0)
+    half = grad.shape[0] // 2
     chunks = pl.cdiv(half, CHUNK)
-    grad = grad_ref[...]
     dout = mm(weight_ref[...], grad, 1, 0).astype(BF16)
     dout_ref[...] = dout
     choosers = [far_chooser(offset_ref[head], 3) for head in range(heads)]
@@ -482,6 +485,7 @@
         pltpu.VMEM(values.shape, values.dtype),
         pltpu.SemaphoreType.DMA((3,)),
     ]
+    other_grad = lax.ppermute(grad_out, "chip", [(0, 1), (1, 0)])
     (near,) = call(
         near_kernel,
         [near_shape],
@@ -491,12 +495,13 @@
         limit=LIMIT,
     )
     near = lax.ppermute(near, "yh", other)
-    full_grad = lax.all_gather(grad_out, "dp", axis=0, tiled=True)
+    pair_grads = lax.all_gather(jnp.stack([grad_out, other_grad]), "core", axis=0, tiled=True)
+    side = lax.axis_index("chip").reshape(1)
     slots, dout, stats = call(
         local_kernel,
         [slots_shape, grad_shape, ((heads * SMALL, TOKENS_HERE), F32)],
-        (offsets, queries, keys, values, full_grad, out_weight, near),
-        scalars=1,
+        (offsets, side, queries, keys, values, pair_grads, out_weight, near),
+        scalars=2,
     )
     slots = lax.all_to_all(slots, "xz", 0, 0, tiled=True)
     own, local_query, local_key, local_value = call(
@@ -560,13 +565,14 @@
 
 
 def solution(mesh):
-    devices = mesh.devices.reshape(-1, PLANES, mesh.devices.shape[1])
-    split_mesh = Mesh(devices, ("xz", "yh", "dp"))
-    wide = P("dp", ("xz", "yh"))
+    devices = mesh.devices.reshape(-1, PLANES, 2, mesh.devices.shape[1] // 2)
+    split_mesh = Mesh(devices, ("xz", "yh", "chip", "core"))
+    parts = ("chip", "core")
+    wide = P(parts, ("xz", "yh"))
     return jax.shard_map(
         local,
         mesh=split_mesh,
-        in_specs=(wide, wide, wide, wide, P("dp", None), P("dp")),
-        out_specs=(wide, wide, wide, P("dp", None)),
+        in_specs=(wide, wide, wide, wide, P(parts, None), P(parts)),
+        out_specs=(wide, wide, wide, P(parts, None)),
         check_vma=False,
     )

time: 82.8 us -> 81.3 us (0.982)
  the two profiles are of different devices: /device:TPU:16 before, /device:TPU:64 now
where the time goes in v6:
time: 81.3 us; the launch traced here: 80.9 us
  blocking collectives  35.6 us (44%)
  starting transfers between devices  24.5 us (30%)
  Pallas kernels  10.8 us (13%)
  waiting for transfers between devices  8.59 us (11%)
    all_to_all x1, blocking collectives, local(): slots = lax.all_to_all(slots, 'xz', 0, 0, tiled=True)  18.7 us
    all_to_all x1, blocking collectives, local(): merged = lax.all_to_all(merged, 'yh', 0, 0, tiled=True)  14.7 us
    all_to_all x1, starting transfers between devices, local(): slots = lax.all_to_all(slots, 'xz', 0, 0, tiled=True)  12.6 us
    pallas_call x7, Pallas kernels, call(): pl.pallas_call(kernel, out_shape=shapes, in_specs=specs, out_specs=[pl.Bl...  10.8 us
    all_to_all x1, waiting for transfers between devices, local(): slots = lax.all_to_all(slots, 'xz', 0, 0, tiled=True)  5.76 us
    ppermute x1, starting transfers between devices, local(): near = lax.ppermute(near, 'yh', other)  4.5 us
    ppermute x1, starting transfers between devices, local(): partner = lax.ppermute(own, 'yh', other)  3.75 us
    ppermute x1, starting transfers between devices, local(): other_grad = lax.ppermute(grad_out, 'chip', [(0, 1), (1, 0)])  3.62 us
  transfers between devices with their start and end apart: 4, of which 2 were waited for; matrix products, arithmetic and copies ran while one was open for 0% of the time, Pallas kernels for 6%

profile of v6, /device:TPU:64, one launch (start us, length us, event | category | flops | bytes accessed | tf_op | source)
XLA Modules:
  0.0 80.9 jit_solution(16754638459815154171)
XLA Ops:
  0.6 0.0 copy-start.5
  0.6 3.6 %collective-permute-start = (bf16[192,256]{1,0:T(8,128)(2,1)}, bf16[192,256]{1,0:T(8,128)(2,1)S(1)}, u32[]{:S(2)}, u32[]{:S(2)}) collective-permute-start(bf16[192,256]{1,0:T(8,128)(2,1)} %param.9), channel_id=1, source_target_pairs={{0,2},{2,0},{1,3},{3,1},{4,6},{6,4},{5,7},{7,5},{8,10},{10,8},{9,1... | collective-permute-start | bytes 294920 | tf_op jit(solution)/shard_map/ppermute | solution.py:488
  4.3 1.8 %near_kernel.1 = bf16[48,128]{1,0:T(8,128)(2,1)} custom-call(s32[3]{0:T(128)} %offset_ref.5, bf16[192,256]{1,0:T(8,128)(2,1)} %key_ref.5, bf16[192,256]{1,0:T(8,128)(2,1)} %value_ref.5), custom_call_target="tpu_custom_call" | custom-call | tf_op jit(solution)/shard_map/near_kernel/pallas_call | solution.py:457
  6.0 4.5 %collective-permute-start.1 = (bf16[48,128]{1,0:T(8,128)(2,1)}, bf16[48,128]{1,0:T(8,128)(2,1)S(1)}, u32[]{:S(2)}, u32[]{:S(2)}) collective-permute-start(bf16[48,128]{1,0:T(8,128)(2,1)} %near_kernel.1), channel_id=1, source_target_pairs={{0,4},{4,0},{8,12},{12,8},{1,5},{5,1},{9,13},{13,9},{2,6},{6,2},{1... | collective-permute-start | bytes 36872 | tf_op jit(solution)/shard_map/ppermute | solution.py:497
  10.5 0.0 collective-permute-done
  10.5 0.0 copy-done.5
  10.6 0.0 copy-start
  10.6 0.0 copy-start.1
  10.6 0.0 copy-start.2
  10.6 0.0 copy-start.3
  10.6 2.2 %all_gather.3.grad_ref = bf16[4,192,256]{2,1,0:T(8,128)(2,1)S(1)} all-gather(bf16[2,192,256]{2,1,0:T(8,128)(2,1)S(1)} %pad_maximum_fusion), channel_id=1, replica_groups=mesh['xz'=32,'yh'=4,'chip'=2,'core'=2] {'core'}, dimensions={0}, use_global_device_ids=true | all-gather | bytes 589824 | tf_op jit(solution)/shard_map/all_gather | solution.py:498
  12.9 0.0 copy-start.4
  12.9 0.0 collective-permute-done.1.near_ref
  12.9 0.0 copy-done
  12.9 0.0 copy-done.1
  12.9 0.0 copy-done.2
  12.9 0.0 copy-done.3
  12.9 0.6 copy-done.4
  13.5 2.7 %local_kernel.1 = (bf16[32,48,128]{2,1,0:T(8,128)(2,1)}, bf16[192,256]{1,0:T(8,128)(2,1)S(1)}, f32[24,256]{1,0:T(8,128)S(1)}) custom-call(s32[3]{0:T(128)S(1)} %copy-done.4, s32[1]{0:T(128)} %bitcast.side_ref, bf16[192,256]{1,0:T(8,128)(2,1)S(1)} %copy-done.2, bf16[192,256]{1,0:T(8,128)(2,1)S(1)} %copy-done, bf16[192,256]{1,0:T(8,128)(2,1)S(1)} %copy-done.1, ...), custom_call_target="tpu_custom_call" | custom-call | tf_op jit(solution)/shard_map/local_kernel/pallas_call | solution.py:457
  16.2 12.6 %all-to-all-start = ((bf16[32,48,128]{2,1,0:T(8,128)(2,1)}), bf16[32,48,128]{2,1,0:T(8,128)(2,1)S(1)}, u32[]{:S(2)}, u32[]{:S(2)}) async-start(bf16[32,48,128]{2,1,0:T(8,128)(2,1)} %get-tuple-element.28), calls=%async_computation | async-start | bytes 786432 | tf_op jit(solution)/shard_map/all_to_all | solution.py:506
  28.8 1.7 %local_grad_kernel.1 = (bf16[64,128]{1,0:T(8,128)(2,1)S(1)}, f32[192,256]{1,0:T(8,128)S(1)}, f32[192,256]{1,0:T(8,128)S(1)}, f32[192,256]{1,0:T(8,128)S(1)}) custom-call(s32[3]{0:T(128)S(1)} %copy-done.4, bf16[192,256]{1,0:T(8,128)(2,1)S(1)} %copy-done.2, bf16[192,256]{1,0:T(8,128)(2,1)S(1)} %copy-done, bf16[192,256]{1,0:T(8,128)(2,1)S(1)} %copy-done.1, ...), custom_call_target="tpu_custom_call" | custom-call | tf_op jit(solution)/shard_map/local_grad_kernel/pallas_call | solution.py:457
  30.5 3.8 %collective-permute-start.2 = (bf16[64,128]{1,0:T(8,128)(2,1)S(1)}, bf16[64,128]{1,0:T(8,128)(2,1)S(1)}, u32[]{:S(2)}, u32[]{:S(2)}) collective-permute-start(bf16[64,128]{1,0:T(8,128)(2,1)S(1)} %get-tuple-element.31.own_ref), channel_id=1, source_target_pairs={{0,4},{4,0},{8,12},{12,8},{1,5},{5,1},{9,13},{13,9},{2,6},{6,2},{1... | collective-permute-start | bytes 49160 | tf_op jit(solution)/shard_map/ppermute | solution.py:513
  34.3 2.8 %collective-permute-done.2.partner_ref = bf16[64,128]{1,0:T(8,128)(2,1)S(1)} collective-permute-done((bf16[64,128]{1,0:T(8,128)(2,1)S(1)}, bf16[64,128]{1,0:T(8,128)(2,1)S(1)}, u32[]{:S(2)}, u32[]{:S(2)}) %collective-permute-start.2) | collective-permute-done | bytes 16416 | tf_op jit(solution)/shard_map/ppermute | solution.py:513
  37.1 1.2 %prepare_kernel.1 = (bf16[48,128]{1,0:T(8,128)(2,1)S(1)}, f32[48,384]{1,0:T(8,128)S(1)}, f32[48,384]{1,0:T(8,128)S(1)}, bf16[3,128,384]{2,1,0:T(8,128)(2,1)S(1)}...) custom-call(s32[3]{0:T(128)S(1)} %copy-done.4, ...), custom_call_target="tpu_custom_call" | custom-call | tf_op jit(solution)/shard_map/prepare_kernel/pallas_call | solution.py:457
  38.3 5.8 %all-to-all-done.slots_ref = bf16[32,48,128]{2,1,0:T(8,128)(2,1)S(1)} async-done(((bf16[32,48,128]{2,1,0:T(8,128)(2,1)}), bf16[32,48,128]{2,1,0:T(8,128)(2,1)S(1)}, u32[]{:S(2)}, u32[]{:S(2)}) %all-to-all-start) | async-done | bytes 393248 | tf_op jit(solution)/shard_map/all_to_all | solution.py:506
  44.1 0.1 merge_kernel.1
  44.2 14.7 %all_to_all.15.merged_ref = bf16[4,304,128]{2,1,0:T(8,128)(2,1)S(1)} all-to-all(bf16[4,304,128]{2,1,0:T(8,128)(2,1)S(1)} %merge_kernel.1), channel_id=1, replica_groups=mesh['xz'=32,'yh'=4,'chip'=2,'core'=2] {'yh'}, dimensions={0} | all-to-all | bytes 622592 | tf_op jit(solution)/shard_map/all_to_all | solution.py:539
  58.9 1.5 %far_kernel.1 = bf16[32,48,128]{2,1,0:T(8,128)(2,1)S(1)} custom-call(s32[1]{0:T(128)} %bitcast.3.plane_ref, bf16[4,304,128]{2,1,0:T(8,128)(2,1)S(1)} %all_to_all.15.merged_ref), custom_call_target="tpu_custom_call" | custom-call | tf_op jit(solution)/shard_map/far_kernel/pallas_call | solution.py:457
  60.4 18.7 %all_to_all.16.slots_ref = bf16[32,48,128]{2,1,0:T(8,128)(2,1)S(1)} all-to-all(bf16[32,48,128]{2,1,0:T(8,128)(2,1)S(1)} %far_kernel.1), channel_id=1, replica_groups=mesh['xz'=32,'yh'=4,'chip'=2,'core'=2] {'xz'}, dimensions={0} | all-to-all | bytes 786432 | tf_op jit(solution)/shard_map/all_to_all | solution.py:547
  79.1 1.9 %final_kernel.1 = (bf16[192,256]{1,0:T(8,128)(2,1)}, bf16[192,256]{1,0:T(8,128)(2,1)}, bf16[192,256]{1,0:T(8,128)(2,1)}, f32[192,768]{1,0:T(8,128)}) custom-call(bf16[48,128]{1,0:T(8,128)(2,1)S(1)} %get-tuple-element.42.rows_ref, f32[48,384]{1,0:T(8,128)S(1)} %get-tuple-element.43.scores_ref, f32[48,384]{1,0:T(8,128)S(1)} %get-tuple-element.44.grad_probs_ref, ...), custom_call_target="tpu_custom_call" | custom-call | tf_op jit(solution)/shard_map/final_kernel/pallas_call | solution.py:457
  (1 shorter events, 0.0 us)
Async XLA Ops:
  0.6 9.9 %copy-start.5 = (bf16[192,256]{1,0:T(8,128)(2,1)S(1)}, bf16[192,256]{1,0:T(8,128)(2,1)}, u32[]{:S(2)}) copy-start(bf16[192,256]{1,0:T(8,128)(2,1)} %param.9) | copy-start | bytes 294916
  0.6 9.9 %collective-permute-start = (bf16[192,256]{1,0:T(8,128)(2,1)}, bf16[192,256]{1,0:T(8,128)(2,1)S(1)}, u32[]{:S(2)}, u32[]{:S(2)}) collective-permute-start(bf16[192,256]{1,0:T(8,128)(2,1)} %param.9), channel_id=1, source_target_pairs={{0,2},{2,0},{1,3},{3,1},{4,6},{6,4},{5,7},{7,5},{8,10},{10,8},{9,1... | collective-permute-start | bytes 294920 | tf_op jit(solution)/shard_map/ppermute | solution.py:488
  6.0 6.8 %collective-permute-start.1 = (bf16[48,128]{1,0:T(8,128)(2,1)}, bf16[48,128]{1,0:T(8,128)(2,1)S(1)}, u32[]{:S(2)}, u32[]{:S(2)}) collective-permute-start(bf16[48,128]{1,0:T(8,128)(2,1)} %near_kernel.1), channel_id=1, source_target_pairs={{0,4},{4,0},{8,12},{12,8},{1,5},{5,1},{9,13},{13,9},{2,6},{6,2},{1... | collective-permute-start | bytes 36872 | tf_op jit(solution)/shard_map/ppermute | solution.py:497
  10.6 2.3 %copy-start = (bf16[192,256]{1,0:T(8,128)(2,1)S(1)}, bf16[192,256]{1,0:T(8,128)(2,1)}, u32[]{:S(2)}) copy-start(bf16[192,256]{1,0:T(8,128)(2,1)} %key_ref.5) | copy-start | bytes 294916
  10.6 2.3 %copy-start.1 = (bf16[192,256]{1,0:T(8,128)(2,1)S(1)}, bf16[192,256]{1,0:T(8,128)(2,1)}, u32[]{:S(2)}) copy-start(bf16[192,256]{1,0:T(8,128)(2,1)} %value_ref.5) | copy-start | bytes 294916
  10.6 2.3 %copy-start.2 = (bf16[192,256]{1,0:T(8,128)(2,1)S(1)}, bf16[192,256]{1,0:T(8,128)(2,1)}, u32[]{:S(2)}) copy-start(bf16[192,256]{1,0:T(8,128)(2,1)} %query_ref.3) | copy-start | bytes 294916
  10.6 2.3 %copy-start.3 = (bf16[192,768]{1,0:T(8,128)(2,1)S(1)}, bf16[192,768]{1,0:T(8,128)(2,1)}, u32[]{:S(2)}) copy-start(bf16[192,768]{1,0:T(8,128)(2,1)} %weight_ref.1) | copy-start | bytes 884740
  12.9 0.7 copy-start.4
  16.2 27.9 %all-to-all-start = ((bf16[32,48,128]{2,1,0:T(8,128)(2,1)}), bf16[32,48,128]{2,1,0:T(8,128)(2,1)S(1)}, u32[]{:S(2)}, u32[]{:S(2)}) async-start(bf16[32,48,128]{2,1,0:T(8,128)(2,1)} %get-tuple-element.28), calls=%async_computation | async-start | bytes 786432 | tf_op jit(solution)/shard_map/all_to_all | solution.py:506
  30.5 6.6 %collective-permute-start.2 = (bf16[64,128]{1,0:T(8,128)(2,1)S(1)}, bf16[64,128]{1,0:T(8,128)(2,1)S(1)}, u32[]{:S(2)}, u32[]{:S(2)}) collective-permute-start(bf16[64,128]{1,0:T(8,128)(2,1)S(1)} %get-tuple-element.31.own_ref), channel_id=1, source_target_pairs={{0,4},{4,0},{8,12},{12,8},{1,5},{5,1},{9,13},{13,9},{2,6},{6,2},{1... | collective-permute-start | bytes 49160 | tf_op jit(solution)/shard_map/ppermute | solution.py:513

commit v7 on v6

--- a/solution.py
+++ b/solution.py
@@ -104,6 +104,17 @@
         both = jnp.concatenate([key_ref[rows], value_ref[rows]], axis=0)
         picked = mm(near_chooser(offset_ref[head]), both, 1, 1)
         near_ref[head * NEAR : (head + 1) * NEAR, :] = picked.astype(BF16)
+    heads = near_ref.shape[0] // NEAR - 1
+    row = iota((GAP, LANES), 0)
+    told = jnp.zeros((GAP, LANES), F32)
+    for head in range(heads):
+        told = jnp.where(row == head, offset_ref[head].astype(F32), told)
+    near_ref[heads * NEAR :] = told.astype(BF16)
+
+
+def told_offset(near_ref, head):
+    told = near_ref[near_ref.shape[0] - GAP :].astype(F32)
+    return told[head : head + 1, :1].astype(jnp.int32)
 
 
 def pair_count(key_pos, query_pos, offset):
@@ -116,7 +127,6 @@
 
 
 def local_kernel(
-    offset_ref,
     side_ref,
     query_ref,
     key_ref,
@@ -136,7 +146,8 @@
     chunks = pl.cdiv(half, CHUNK)
     dout = mm(weight_ref[...], grad, 1, 0).astype(BF16)
     dout_ref[...] = dout
-    choosers = [far_chooser(offset_ref[head], 3) for head in range(heads)]
+    offsets = [told_offset(near_ref, head) for head in range(heads)]
+    choosers = [far_chooser(offsets[head], 3) for head in range(heads)]
     choosers = jnp.concatenate(choosers, axis=0)
     wide = grad.astype(F32)
     filler = jnp.zeros((LANES - 2 * CHUNK, TOKENS_HERE), F32)
@@ -149,7 +160,6 @@
     query_pos = iota((TOKENS_HERE, TOKENS_HERE), 1)
     query_row = iota((1, TOKENS_HERE), 1)
     heads = range(heads)
-    offsets = [offset_ref[head] for head in heads]
     rows = [slice(head * HEAD_DIM, (head + 1) * HEAD_DIM) for head in heads]
     near = [near_ref[head * NEAR : (head + 1) * NEAR] for head in heads]
     in_near = [same_class(query_row, offset, RC) for offset in offsets]
@@ -208,7 +218,6 @@
 
 
 def local_grad_kernel(
-    offset_ref,
     query_ref,
     key_ref,
     value_ref,
@@ -227,7 +236,7 @@
     query_row = iota((1, TOKENS_HERE), 1)
     far_rows = jnp.zeros((GAP, LANES), F32)
     for head in range(heads):
-        offset = offset_ref[head]
+        offset = told_offset(near_ref, head)
         rows = slice(head * HEAD_DIM, (head + 1) * HEAD_DIM)
         near_rows = slice(head * NEAR, (head + 1) * NEAR)
         query, key, value = query_ref[rows], key_ref[rows], value_ref[rows]
@@ -345,7 +354,6 @@
 
 
 def prepare_kernel(
-    offset_ref,
     key_ref,
     value_ref,
     near_ref,
@@ -372,7 +380,7 @@
     here = place < TOKENS_HERE
     from_partner, from_here = block_row < 2, (block_row >= 2) & (block_row < 4)
     for head in range(heads):
-        offset = offset_ref[head]
+        offset = told_offset(near_ref, head)
         rows = slice(head * HEAD_DIM, (head + 1) * HEAD_DIM)
         block = slice(head * GAP, (head + 1) * GAP)
         key, value = key_ref[rows], value_ref[rows]
@@ -470,7 +478,7 @@
     model = out_weight.shape[1]
     heads = offsets.shape[0]
     sources = lax.axis_size("xz")
-    near_shape = ((heads * NEAR, LANES), BF16)
+    near_shape = ((heads * NEAR + GAP, LANES), BF16)
     back_shape = ((heads * NEAR + GAP, LANES), BF16)
     slots_shape = ((sources, SLOT, LANES), BF16)
     merged_shape = ((PLANES, SLOT + sources * SMALL, LANES), BF16)
@@ -500,21 +508,20 @@
     slots, dout, stats = call(
         local_kernel,
         [slots_shape, grad_shape, ((heads * SMALL, TOKENS_HERE), F32)],
-        (offsets, side, queries, keys, values, pair_grads, out_weight, near),
-        scalars=2,
+        (side, queries, keys, values, pair_grads, out_weight, near),
+        scalars=1,
     )
     slots = lax.all_to_all(slots, "xz", 0, 0, tiled=True)
     own, local_query, local_key, local_value = call(
         local_grad_kernel,
         [back_shape, wide_shape, wide_shape, wide_shape],
-        (offsets, queries, keys, values, dout, stats, near),
-        scalars=1,
+        (queries, keys, values, dout, stats, near),
     )
     partner = lax.ppermute(own, "yh", other)
     prepared = call(
         prepare_kernel,
         [
-            near_shape,
+            ((heads * GAP, LANES), BF16),
             block_shape,
             block_shape,
             ((heads, LANES, TOKENS_HERE + LANES), BF16),
@@ -522,8 +529,7 @@
             wide_shape,
             wide_shape,
         ],
-        (offsets, keys, values, near, own, partner, local_key, local_value),
-        scalars=1,
+        (keys, values, near, own, partner, local_key, local_value),
     )
     plane = lax.axis_index("yh").reshape(1)
     slots, prepared, local_query, plane = lax.optimization_barrier(

time: 81.3 us -> 80.4 us (0.989)
  the two profiles are of different devices: /device:TPU:64 before, /device:TPU:8 now
where the time goes in v7:
time: 80.4 us; the launch traced here: 80 us
  blocking collectives  37 us (46%)
  starting transfers between devices  22.1 us (27%)
  waiting for transfers between devices  10.6 us (13%)
  Pallas kernels  9.47 us (12%)
    all_to_all x1, blocking collectives, local(): slots = lax.all_to_all(slots, 'xz', 0, 0, tiled=True)  19 us
    all_to_all x1, blocking collectives, local(): merged = lax.all_to_all(merged, 'yh', 0, 0, tiled=True)  15.7 us
    pallas_call x7, Pallas kernels, call(): pl.pallas_call(kernel, out_shape=shapes, in_specs=specs, out_specs=[pl.Bl...  9.47 us
    all_to_all x1, starting transfers between devices, local(): slots = lax.all_to_all(slots, 'xz', 0, 0, tiled=True)  7.88 us
    ppermute x1, starting transfers between devices, local(): other_grad = lax.ppermute(grad_out, 'chip', [(0, 1), (1, 0)])  7.86 us
    all_to_all x1, waiting for transfers between devices, local(): slots = lax.all_to_all(slots, 'xz', 0, 0, tiled=True)  6.03 us
    ppermute x1, starting transfers between devices, local(): partner = lax.ppermute(own, 'yh', other)  4.41 us
    ppermute x1, waiting for transfers between devices, local(): near = lax.ppermute(near, 'yh', other)  2.49 us
  transfers between devices with their start and end apart: 4, of which 3 were waited for; matrix products, arithmetic and copies ran while one was open for 0% of the time, Pallas kernels for 5%

profile of v7, /device:TPU:8, one launch (start us, length us, event | category | flops | bytes accessed | tf_op | source)
XLA Modules:
  0.0 80.0 jit_solution(3849307272520166067)
XLA Ops:
  0.6 0.0 copy-start.4
  0.6 7.9 %collective-permute-start = (bf16[192,256]{1,0:T(8,128)(2,1)}, bf16[192,256]{1,0:T(8,128)(2,1)S(1)}, u32[]{:S(2)}, u32[]{:S(2)}) collective-permute-start(bf16[192,256]{1,0:T(8,128)(2,1)} %param.9), channel_id=1, source_target_pairs={{0,2},{2,0},{1,3},{3,1},{4,6},{6,4},{5,7},{7,5},{8,10},{10,8},{9,1... | collective-permute-start | bytes 294920 | tf_op jit(solution)/shard_map/ppermute | solution.py:496
  8.5 1.8 %near_kernel.1 = bf16[64,128]{1,0:T(8,128)(2,1)} custom-call(s32[3]{0:T(128)} %offset_hbm.1, bf16[192,256]{1,0:T(8,128)(2,1)} %key_ref.5, bf16[192,256]{1,0:T(8,128)(2,1)} %value_ref.5), custom_call_target="tpu_custom_call" | custom-call | tf_op jit(solution)/shard_map/near_kernel/pallas_call | solution.py:465
  10.3 1.9 %collective-permute-start.1 = (bf16[64,128]{1,0:T(8,128)(2,1)}, bf16[64,128]{1,0:T(8,128)(2,1)S(1)}, u32[]{:S(2)}, u32[]{:S(2)}) collective-permute-start(bf16[64,128]{1,0:T(8,128)(2,1)} %near_kernel.1), channel_id=1, source_target_pairs={{0,4},{4,0},{8,12},{12,8},{1,5},{5,1},{9,13},{13,9},{2,6},{6,2},{1... | collective-permute-start | bytes 49160 | tf_op jit(solution)/shard_map/ppermute | solution.py:505
  12.2 0.0 collective-permute-done
  12.2 0.0 copy-done.4
  12.3 0.0 copy-start
  12.3 0.0 copy-start.1
  12.3 0.0 copy-start.2
  12.3 0.0 copy-start.3
  12.3 2.2 %all_gather.3.grad_ref = bf16[4,192,256]{2,1,0:T(8,128)(2,1)S(1)} all-gather(bf16[2,192,256]{2,1,0:T(8,128)(2,1)S(1)} %pad_maximum_fusion), channel_id=1, replica_groups=mesh['xz'=32,'yh'=4,'chip'=2,'core'=2] {'core'}, dimensions={0}, use_global_device_ids=true | all-gather | bytes 589824 | tf_op jit(solution)/shard_map/all_gather | solution.py:506
  14.5 2.5 %collective-permute-done.1.near_ref = bf16[64,128]{1,0:T(8,128)(2,1)S(1)} collective-permute-done((bf16[64,128]{1,0:T(8,128)(2,1)}, bf16[64,128]{1,0:T(8,128)(2,1)S(1)}, u32[]{:S(2)}, u32[]{:S(2)}) %collective-permute-start.1) | collective-permute-done | bytes 16416 | tf_op jit(solution)/shard_map/ppermute | solution.py:505
  17.0 0.0 copy-done
  17.0 0.0 copy-done.1
  17.0 0.0 copy-done.2
  17.0 0.0 copy-done.3
  17.0 2.4 %local_kernel.1 = (bf16[32,48,128]{2,1,0:T(8,128)(2,1)}, bf16[192,256]{1,0:T(8,128)(2,1)S(1)}, f32[24,256]{1,0:T(8,128)S(1)}) custom-call(s32[1]{0:T(128)} %bitcast.side_ref, bf16[192,256]{1,0:T(8,128)(2,1)S(1)} %copy-done.2, bf16[192,256]{1,0:T(8,128)(2,1)S(1)} %copy-done, bf16[192,256]{1,0:T(8,128)(2,1)S(1)} %copy-done.1, ...), custom_call_target="tpu_custom_call" | custom-call | tf_op jit(solution)/shard_map/local_kernel/pallas_call | solution.py:465
  19.4 7.9 %all-to-all-start = ((bf16[32,48,128]{2,1,0:T(8,128)(2,1)}), bf16[32,48,128]{2,1,0:T(8,128)(2,1)S(1)}, u32[]{:S(2)}, u32[]{:S(2)}) async-start(bf16[32,48,128]{2,1,0:T(8,128)(2,1)} %get-tuple-element.28), calls=%async_computation | async-start | bytes 786432 | tf_op jit(solution)/shard_map/all_to_all | solution.py:514
  27.3 1.2 %local_grad_kernel.1 = (bf16[64,128]{1,0:T(8,128)(2,1)S(1)}, f32[192,256]{1,0:T(8,128)S(1)}, f32[192,256]{1,0:T(8,128)S(1)}, f32[192,256]{1,0:T(8,128)S(1)}) custom-call(bf16[192,256]{1,0:T(8,128)(2,1)S(1)} %copy-done.2, bf16[192,256]{1,0:T(8,128)(2,1)S(1)} %copy-done, bf16[192,256]{1,0:T(8,128)(2,1)S(1)} %copy-done.1, ...), custom_call_target="tpu_custom_call" | custom-call | tf_op jit(solution)/shard_map/local_grad_kernel/pallas_call | solution.py:465
  28.5 4.4 %collective-permute-start.2 = (bf16[64,128]{1,0:T(8,128)(2,1)S(1)}, bf16[64,128]{1,0:T(8,128)(2,1)S(1)}, u32[]{:S(2)}, u32[]{:S(2)}) collective-permute-start(bf16[64,128]{1,0:T(8,128)(2,1)S(1)} %get-tuple-element.31.own_ref), channel_id=1, source_target_pairs={{0,4},{4,0},{8,12},{12,8},{1,5},{5,1},{9,13},{13,9},{2,6},{6,2},{1... | collective-permute-start | bytes 49160 | tf_op jit(solution)/shard_map/ppermute | solution.py:520
  33.0 2.1 %collective-permute-done.2.partner_ref = bf16[64,128]{1,0:T(8,128)(2,1)S(1)} collective-permute-done((bf16[64,128]{1,0:T(8,128)(2,1)S(1)}, bf16[64,128]{1,0:T(8,128)(2,1)S(1)}, u32[]{:S(2)}, u32[]{:S(2)}) %collective-permute-start.2) | collective-permute-done | bytes 16416 | tf_op jit(solution)/shard_map/ppermute | solution.py:520
  35.1 0.7 prepare_kernel.1
  35.8 6.0 %all-to-all-done.slots_ref = bf16[32,48,128]{2,1,0:T(8,128)(2,1)S(1)} async-done(((bf16[32,48,128]{2,1,0:T(8,128)(2,1)}), bf16[32,48,128]{2,1,0:T(8,128)(2,1)S(1)}, u32[]{:S(2)}, u32[]{:S(2)}) %all-to-all-start) | async-done | bytes 393248 | tf_op jit(solution)/shard_map/all_to_all | solution.py:514
  41.8 0.1 merge_kernel.1
  41.9 15.7 %all_to_all.15.merged_ref = bf16[4,304,128]{2,1,0:T(8,128)(2,1)S(1)} all-to-all(bf16[4,304,128]{2,1,0:T(8,128)(2,1)S(1)} %merge_kernel.1), channel_id=1, replica_groups=mesh['xz'=32,'yh'=4,'chip'=2,'core'=2] {'yh'}, dimensions={0} | all-to-all | bytes 622592 | tf_op jit(solution)/shard_map/all_to_all | solution.py:545
  57.6 1.5 %far_kernel.1 = bf16[32,48,128]{2,1,0:T(8,128)(2,1)S(1)} custom-call(s32[1]{0:T(128)} %bitcast.3.plane_ref, bf16[4,304,128]{2,1,0:T(8,128)(2,1)S(1)} %all_to_all.15.merged_ref), custom_call_target="tpu_custom_call" | custom-call | tf_op jit(solution)/shard_map/far_kernel/pallas_call | solution.py:465
  59.1 19.0 %all_to_all.16.slots_ref = bf16[32,48,128]{2,1,0:T(8,128)(2,1)S(1)} all-to-all(bf16[32,48,128]{2,1,0:T(8,128)(2,1)S(1)} %far_kernel.1), channel_id=1, replica_groups=mesh['xz'=32,'yh'=4,'chip'=2,'core'=2] {'xz'}, dimensions={0} | all-to-all | bytes 786432 | tf_op jit(solution)/shard_map/all_to_all | solution.py:553
  78.1 1.8 %final_kernel.1 = (bf16[192,256]{1,0:T(8,128)(2,1)}, bf16[192,256]{1,0:T(8,128)(2,1)}, bf16[192,256]{1,0:T(8,128)(2,1)}, f32[192,768]{1,0:T(8,128)}) custom-call(bf16[48,128]{1,0:T(8,128)(2,1)S(1)} %get-tuple-element.42.rows_ref, f32[48,384]{1,0:T(8,128)S(1)} %get-tuple-element.43.scores_ref, f32[48,384]{1,0:T(8,128)S(1)} %get-tuple-element.44.grad_probs_ref, ...), custom_call_target="tpu_custom_call" | custom-call | tf_op jit(solution)/shard_map/final_kernel/pallas_call | solution.py:465
  (1 shorter events, 0.0 us)
Async XLA Ops:
  0.6 11.6 %copy-start.4 = (bf16[192,256]{1,0:T(8,128)(2,1)S(1)}, bf16[192,256]{1,0:T(8,128)(2,1)}, u32[]{:S(2)}) copy-start(bf16[192,256]{1,0:T(8,128)(2,1)} %param.9) | copy-start | bytes 294916
  0.6 11.6 %collective-permute-start = (bf16[192,256]{1,0:T(8,128)(2,1)}, bf16[192,256]{1,0:T(8,128)(2,1)S(1)}, u32[]{:S(2)}, u32[]{:S(2)}) collective-permute-start(bf16[192,256]{1,0:T(8,128)(2,1)} %param.9), channel_id=1, source_target_pairs={{0,2},{2,0},{1,3},{3,1},{4,6},{6,4},{5,7},{7,5},{8,10},{10,8},{9,1... | collective-permute-start | bytes 294920 | tf_op jit(solution)/shard_map/ppermute | solution.py:496
  10.3 6.7 %collective-permute-start.1 = (bf16[64,128]{1,0:T(8,128)(2,1)}, bf16[64,128]{1,0:T(8,128)(2,1)S(1)}, u32[]{:S(2)}, u32[]{:S(2)}) collective-permute-start(bf16[64,128]{1,0:T(8,128)(2,1)} %near_kernel.1), channel_id=1, source_target_pairs={{0,4},{4,0},{8,12},{12,8},{1,5},{5,1},{9,13},{13,9},{2,6},{6,2},{1... | collective-permute-start | bytes 49160 | tf_op jit(solution)/shard_map/ppermute | solution.py:505
  12.3 4.8 %copy-start = (bf16[192,256]{1,0:T(8,128)(2,1)S(1)}, bf16[192,256]{1,0:T(8,128)(2,1)}, u32[]{:S(2)}) copy-start(bf16[192,256]{1,0:T(8,128)(2,1)} %key_ref.5) | copy-start | bytes 294916
  12.3 4.8 %copy-start.1 = (bf16[192,256]{1,0:T(8,128)(2,1)S(1)}, bf16[192,256]{1,0:T(8,128)(2,1)}, u32[]{:S(2)}) copy-start(bf16[192,256]{1,0:T(8,128)(2,1)} %value_ref.5) | copy-start | bytes 294916
  12.3 4.7 %copy-start.2 = (bf16[192,256]{1,0:T(8,128)(2,1)S(1)}, bf16[192,256]{1,0:T(8,128)(2,1)}, u32[]{:S(2)}) copy-start(bf16[192,256]{1,0:T(8,128)(2,1)} %query_ref.3) | copy-start | bytes 294916
  12.3 4.7 %copy-start.3 = (bf16[192,768]{1,0:T(8,128)(2,1)S(1)}, bf16[192,768]{1,0:T(8,128)(2,1)}, u32[]{:S(2)}) copy-start(bf16[192,768]{1,0:T(8,128)(2,1)} %weight_ref.1) | copy-start | bytes 884740
  19.4 22.3 %all-to-all-start = ((bf16[32,48,128]{2,1,0:T(8,128)(2,1)}), bf16[32,48,128]{2,1,0:T(8,128)(2,1)S(1)}, u32[]{:S(2)}, u32[]{:S(2)}) async-start(bf16[32,48,128]{2,1,0:T(8,128)(2,1)} %get-tuple-element.28), calls=%async_computation | async-start | bytes 786432 | tf_op jit(solution)/shard_map/all_to_all | solution.py:514
  28.5 6.5 %collective-permute-start.2 = (bf16[64,128]{1,0:T(8,128)(2,1)S(1)}, bf16[64,128]{1,0:T(8,128)(2,1)S(1)}, u32[]{:S(2)}, u32[]{:S(2)}) collective-permute-start(bf16[64,128]{1,0:T(8,128)(2,1)S(1)} %get-tuple-element.31.own_ref), channel_id=1, source_target_pairs={{0,4},{4,0},{8,12},{12,8},{1,5},{5,1},{9,13},{13,9},{2,6},{6,2},{1... | collective-permute-start | bytes 49160 | tf_op jit(solution)/shard_map/ppermute | solution.py:520

commit v8 on v7

--- a/solution.py
+++ b/solution.py
@@ -74,8 +74,8 @@
     return out
 
 
-def take_stat(rows, index):
-    place = iota(rows.shape, 1) - HEAD_DIM - 3 * index
+def take_stat(rows, start, index):
+    place = iota(rows.shape, 1) - start - 3 * index
     return jnp.sum(jnp.where((place >= 0) & (place < 3), rows, 0.0), axis=1, keepdims=True)
 
 
@@ -200,13 +200,13 @@
     ]
     place = iota((SMALL, TOKENS_HERE), 0)
     for h in heads:
-        query_key = jnp.concatenate([query_ref[rows[h]], key_ref[rows[h]]], axis=0)
-        value_dout = jnp.concatenate([value_ref[rows[h]], dout[rows[h]]], axis=0)
+        query_dout = jnp.concatenate([query_ref[rows[h]], dout[rows[h]]], axis=0)
+        key_value = jnp.concatenate([key_ref[rows[h]], value_ref[rows[h]]], axis=0)
         stats = lay_stats((HEAD_DIM, TOKENS_HERE), 0, 0, (log_mass[h], delta[h]))
-        attended_stats = jnp.concatenate([attended[h].astype(BF16), stats.astype(BF16)], axis=0)
-        mine = mm(far_chooser(offsets[h], 0), query_key, 1, 1)
-        mine = mine + mm(far_chooser(offsets[h], 1), value_dout, 1, 1)
-        mine = mine + mm(far_chooser(offsets[h], 2), attended_stats, 1, 1)
+        stats_attended = jnp.concatenate([stats.astype(BF16), attended[h].astype(BF16)], axis=0)
+        mine = mm(far_chooser(offsets[h], 0), query_dout, 1, 1)
+        mine = mine + mm(far_chooser(offsets[h], 1), key_value, 1, 1)
+        mine = mine + mm(far_chooser(offsets[h], 2), stats_attended, 1, 1)
         stats_ref[h * SMALL : (h + 1) * SMALL] = jnp.where(place == 0, log_mass[h], delta[h])
         for chunk in range(chunks):
             far_grad = far_grads[chunk][h * GAP : h * GAP + SMALL]
@@ -292,53 +292,49 @@
         start = SLOT + index * width
         return merged_ref[:, start : start + width, :].reshape(count, LANES)
 
-    query_key, value_dout, attended_stats, far_grad = (kind(index) for index in range(4))
-    shape = (LANES, HEAD_DIM)
-    lower = one_hot(iota(shape, 0) == iota(shape, 1) + HEAD_DIM)
-    query, value = query_key[:, :HEAD_DIM], value_dout[:, :HEAD_DIM]
-    key, dout = (mm(both, lower, 1, 0).astype(BF16) for both in (query_key, value_dout))
-    local_attended = attended_stats[:, :HEAD_DIM].astype(F32)
-    stats = attended_stats.astype(F32)
-    local_mass = take_stat(stats, 0)
-
-    scores = mm(query, key, 1, 1) * SCORE_SCALE
+    query_dout, key_value, stats_attended, far_grad = (kind(index) for index in range(4))
+    left = iota((count, LANES), 1) < HEAD_DIM
+    shape = (LANES, LANES)
+    swap = one_hot(iota(shape, 0) == (iota(shape, 1) ^ HEAD_DIM))
+    value_key = mm(key_value, swap, 1, 0).astype(BF16)
+    stats = stats_attended.astype(F32)
+    attended_stats = mm(stats_attended, swap, 1, 0)
+    wide = query_dout.astype(F32)
+    query = jnp.where(left, wide, 0.0).astype(BF16)
+    dout_wide = jnp.where(left, 0.0, wide)
+    local_mass = take_stat(stats, 0, 0)
+
+    scores = mm(query, key_value, 1, 1) * SCORE_SCALE
+    grad_probs = mm(dout_wide.astype(BF16), key_value, 1, 1)
     peak = jnp.maximum(jnp.max(scores, axis=1, keepdims=True), local_mass)
     mass = jnp.exp(scores - peak)
     local_part = jnp.exp(local_mass - peak)
     total = jnp.sum(mass, axis=1, keepdims=True) + local_part
     normalizer = peak + jnp.log(total)
     inverse = 1.0 / total
+    local_part = local_part * inverse
     probs = mass * inverse
     probs_low = probs.astype(BF16)
-    attended = local_part * inverse * local_attended + mm(probs_low, value, 1, 0)
-    delta = jnp.sum(dout.astype(F32) * attended, axis=1, keepdims=True)
-    grad_probs = mm(dout, value, 1, 1)
+    under = local_part * stats + mm(probs_low, key_value, 1, 0)
+    delta = jnp.sum(dout_wide * under, axis=1, keepdims=True)
+    over = local_part * attended_stats + mm(probs_low, value_key, 1, 0)
+    over = jnp.where(left, over, 0.0).astype(BF16)
+    under = jnp.where(left, 0.0, under).astype(BF16)
     grad_scores = (probs * (grad_probs - delta)).astype(BF16)
-    grad_query = mm(grad_scores, key, 1, 0).astype(BF16)
-    grad_key = mm(grad_scores, query, 0, 0).astype(BF16)
-    grad_value = mm(probs_low, dout, 0, 0).astype(BF16)
 
     def other_plane(column):
         blocks = [column[(p ^ 1) * width : ((p ^ 1) + 1) * width] for p in range(PLANES)]
         return jnp.concatenate(blocks, axis=0)
 
-    shape = (HEAD_DIM, LANES)
-    to_left = one_hot(iota(shape, 0) == iota(shape, 1))
-    to_right = one_hot(iota(shape, 0) + HEAD_DIM == iota(shape, 1))
-    attended_low = attended.astype(BF16)
-    over = mm(attended_low, to_left, 1, 0).astype(BF16)
-    under = mm(attended_low, to_right, 1, 0).astype(BF16)
     weight_part = mm(far_grad, over, 0, 0)[:CHUNK] + mm(far_grad, under, 0, 0)[CHUNK : 2 * CHUNK]
     weight_part = weight_part * WEIGHT_SCALE
     for plane in range(PLANES):
         weight_part = weight_part + merged_ref[plane, :SLOT].astype(F32)[:CHUNK]
     own_stats = lay_stats((count, LANES), 1, HEAD_DIM, (normalizer, delta))
-    other_stats = lay_stats(
-        (count, LANES), 1, HEAD_DIM, (other_plane(normalizer), other_plane(delta))
-    )
-    returned_ref[0] = mm(grad_value, to_left, 1, 0) + other_stats
-    returned_ref[1] = mm(grad_query, to_left, 1, 0) + own_stats
-    returned_ref[2] = mm(grad_key, to_left, 1, 0)
+    other_stats = lay_stats((count, LANES), 1, 0, (other_plane(normalizer), other_plane(delta)))
+    returned_ref[0] = jnp.where(left, other_stats, mm(probs_low, query_dout, 0, 0))
+    returned_ref[1] = jnp.where(left, mm(grad_scores, key_value, 1, 0), own_stats)
+    returned_ref[2] = jnp.where(left, mm(grad_scores, query_dout, 0, 0), 0.0)
     own = pl.ds(pl.multiple_of(plane_ref[0] * width, width), width)
     shape = (sources * SMALL, width)
     row, column = iota(shape, 0), iota(shape, 1)
@@ -441,15 +437,17 @@
             [pieces[0][CHUNK:], jnp.zeros((GAP - SMALL, LANES), F32)], axis=0
         )
         chosen = rows_ref[block]
-        probs = jnp.exp(scores_ref[block] - take_stat(returned, 0))
-        grad_scores = (probs * (grad_probs_ref[block] - take_stat(returned, 1))).astype(BF16)
+        start = jnp.where(iota(returned.shape, 0) < 2, 0, HEAD_DIM)
+        normalizer, delta = (take_stat(returned, start, index) for index in range(2))
+        probs = jnp.exp(scores_ref[block] - normalizer)
+        grad_scores = (probs * (grad_probs_ref[block] - delta)).astype(BF16)
         probs_low = probs[:, :TOKENS_HERE].astype(BF16)
         far_query = (returned + mm(grad_scores, keys_ref[head], 1, 1)).astype(BF16)
         returned = returned.astype(BF16)
         grad_query = mm(far_query, chooser_ref[head, 1], 0, 0)[:HEAD_DIM]
         grad_key = mm(returned, chooser_ref[head, 2], 0, 0)[:HEAD_DIM]
         grad_key = grad_key + mm(chosen, grad_scores[:, :TOKENS_HERE], 0, 0)[:HEAD_DIM]
-        grad_value = mm(returned, chooser_ref[head, 0], 0, 0)[:HEAD_DIM]
+        grad_value = mm(returned, chooser_ref[head, 0], 0, 0)[HEAD_DIM:]
         grad_value = grad_value + mm(chosen, probs_low, 0, 0)[HEAD_DIM:]
         grad_query = (local_query_ref[rows] + grad_query) * SCORE_SCALE
         grad_key = (local_key_ref[rows] + grad_key) * SCORE_SCALE

time: 80.4 us -> 80.1 us (level)
  no operation moved by 1% of the time
where the time goes in v8:
time: 80.1 us; the launch traced here: 79.7 us
  blocking collectives  37 us (46%)
  starting transfers between devices  22.1 us (28%)
  waiting for transfers between devices  10.6 us (13%)
  Pallas kernels  9.16 us (11%)
    all_to_all x1, blocking collectives, local(): slots = lax.all_to_all(slots, 'xz', 0, 0, tiled=True)  19 us
    all_to_all x1, blocking collectives, local(): merged = lax.all_to_all(merged, 'yh', 0, 0, tiled=True)  15.7 us
    pallas_call x7, Pallas kernels, call(): pl.pallas_call(kernel, out_shape=shapes, in_specs=specs, out_specs=[pl.Bl...  9.16 us
    all_to_all x1, starting transfers between devices, local(): slots = lax.all_to_all(slots, 'xz', 0, 0, tiled=True)  7.88 us
    ppermute x1, starting transfers between devices, local(): other_grad = lax.ppermute(grad_out, 'chip', [(0, 1), (1, 0)])  7.86 us
    all_to_all x1, waiting for transfers between devices, local(): slots = lax.all_to_all(slots, 'xz', 0, 0, tiled=True)  6.02 us
    ppermute x1, starting transfers between devices, local(): partner = lax.ppermute(own, 'yh', other)  4.41 us
    ppermute x1, waiting for transfers between devices, local(): near = lax.ppermute(near, 'yh', other)  2.49 us
  transfers between devices with their start and end apart: 4, of which 3 were waited for; matrix products, arithmetic and copies ran while one was open for 0% of the time, Pallas kernels for 5%

profile of v8, /device:TPU:8, one launch (start us, length us, event | category | flops | bytes accessed | tf_op | source)
XLA Modules:
  0.0 79.7 jit_solution(6365493410722293835)
XLA Ops:
  0.6 0.0 copy-start.4
  0.6 7.9 %collective-permute-start = (bf16[192,256]{1,0:T(8,128)(2,1)}, bf16[192,256]{1,0:T(8,128)(2,1)S(1)}, u32[]{:S(2)}, u32[]{:S(2)}) collective-permute-start(bf16[192,256]{1,0:T(8,128)(2,1)} %param.9), channel_id=1, source_target_pairs={{0,2},{2,0},{1,3},{3,1},{4,6},{6,4},{5,7},{7,5},{8,10},{10,8},{9,1... | collective-permute-start | bytes 294920 | tf_op jit(solution)/shard_map/ppermute | solution.py:494
  8.5 1.8 %near_kernel.1 = bf16[64,128]{1,0:T(8,128)(2,1)} custom-call(s32[3]{0:T(128)} %offset_hbm.1, bf16[192,256]{1,0:T(8,128)(2,1)} %key_ref.5, bf16[192,256]{1,0:T(8,128)(2,1)} %value_ref.5), custom_call_target="tpu_custom_call" | custom-call | tf_op jit(solution)/shard_map/near_kernel/pallas_call | solution.py:463
  10.3 1.9 %collective-permute-start.1 = (bf16[64,128]{1,0:T(8,128)(2,1)}, bf16[64,128]{1,0:T(8,128)(2,1)S(1)}, u32[]{:S(2)}, u32[]{:S(2)}) collective-permute-start(bf16[64,128]{1,0:T(8,128)(2,1)} %near_kernel.1), channel_id=1, source_target_pairs={{0,4},{4,0},{8,12},{12,8},{1,5},{5,1},{9,13},{13,9},{2,6},{6,2},{1... | collective-permute-start | bytes 49160 | tf_op jit(solution)/shard_map/ppermute | solution.py:503
  12.2 0.0 collective-permute-done
  12.2 0.0 copy-done.4
  12.3 0.0 copy-start
  12.3 0.0 copy-start.1
  12.3 0.0 copy-start.2
  12.3 0.0 copy-start.3
  12.3 2.2 %all_gather.3.grad_ref = bf16[4,192,256]{2,1,0:T(8,128)(2,1)S(1)} all-gather(bf16[2,192,256]{2,1,0:T(8,128)(2,1)S(1)} %pad_maximum_fusion), channel_id=1, replica_groups=mesh['xz'=32,'yh'=4,'chip'=2,'core'=2] {'core'}, dimensions={0}, use_global_device_ids=true | all-gather | bytes 589824 | tf_op jit(solution)/shard_map/all_gather | solution.py:504
  14.5 2.5 %collective-permute-done.1.near_ref = bf16[64,128]{1,0:T(8,128)(2,1)S(1)} collective-permute-done((bf16[64,128]{1,0:T(8,128)(2,1)}, bf16[64,128]{1,0:T(8,128)(2,1)S(1)}, u32[]{:S(2)}, u32[]{:S(2)}) %collective-permute-start.1) | collective-permute-done | bytes 16416 | tf_op jit(solution)/shard_map/ppermute | solution.py:503
  17.0 0.0 copy-done
  17.0 0.0 copy-done.1
  17.0 0.0 copy-done.2
  17.0 0.0 copy-done.3
  17.0 2.4 %local_kernel.1 = (bf16[32,48,128]{2,1,0:T(8,128)(2,1)}, bf16[192,256]{1,0:T(8,128)(2,1)S(1)}, f32[24,256]{1,0:T(8,128)S(1)}) custom-call(s32[1]{0:T(128)} %bitcast.side_ref, bf16[192,256]{1,0:T(8,128)(2,1)S(1)} %copy-done.2, bf16[192,256]{1,0:T(8,128)(2,1)S(1)} %copy-done, bf16[192,256]{1,0:T(8,128)(2,1)S(1)} %copy-done.1, ...), custom_call_target="tpu_custom_call" | custom-call | tf_op jit(solution)/shard_map/local_kernel/pallas_call | solution.py:463
  19.5 7.9 %all-to-all-start = ((bf16[32,48,128]{2,1,0:T(8,128)(2,1)}), bf16[32,48,128]{2,1,0:T(8,128)(2,1)S(1)}, u32[]{:S(2)}, u32[]{:S(2)}) async-start(bf16[32,48,128]{2,1,0:T(8,128)(2,1)} %get-tuple-element.28), calls=%async_computation | async-start | bytes 786432 | tf_op jit(solution)/shard_map/all_to_all | solution.py:512
  27.4 1.2 %local_grad_kernel.1 = (bf16[64,128]{1,0:T(8,128)(2,1)S(1)}, f32[192,256]{1,0:T(8,128)S(1)}, f32[192,256]{1,0:T(8,128)S(1)}, f32[192,256]{1,0:T(8,128)S(1)}) custom-call(bf16[192,256]{1,0:T(8,128)(2,1)S(1)} %copy-done.2, bf16[192,256]{1,0:T(8,128)(2,1)S(1)} %copy-done, bf16[192,256]{1,0:T(8,128)(2,1)S(1)} %copy-done.1, ...), custom_call_target="tpu_custom_call" | custom-call | tf_op jit(solution)/shard_map/local_grad_kernel/pallas_call | solution.py:463
  28.6 4.4 %collective-permute-start.2 = (bf16[64,128]{1,0:T(8,128)(2,1)S(1)}, bf16[64,128]{1,0:T(8,128)(2,1)S(1)}, u32[]{:S(2)}, u32[]{:S(2)}) collective-permute-start(bf16[64,128]{1,0:T(8,128)(2,1)S(1)} %get-tuple-element.31.own_ref), channel_id=1, source_target_pairs={{0,4},{4,0},{8,12},{12,8},{1,5},{5,1},{9,13},{13,9},{2,6},{6,2},{1... | collective-permute-start | bytes 49160 | tf_op jit(solution)/shard_map/ppermute | solution.py:518
  33.0 2.1 %collective-permute-done.2.partner_ref = bf16[64,128]{1,0:T(8,128)(2,1)S(1)} collective-permute-done((bf16[64,128]{1,0:T(8,128)(2,1)S(1)}, bf16[64,128]{1,0:T(8,128)(2,1)S(1)}, u32[]{:S(2)}, u32[]{:S(2)}) %collective-permute-start.2) | collective-permute-done | bytes 16416 | tf_op jit(solution)/shard_map/ppermute | solution.py:518
  35.1 0.7 prepare_kernel.1
  35.8 6.0 %all-to-all-done.slots_ref = bf16[32,48,128]{2,1,0:T(8,128)(2,1)S(1)} async-done(((bf16[32,48,128]{2,1,0:T(8,128)(2,1)}), bf16[32,48,128]{2,1,0:T(8,128)(2,1)S(1)}, u32[]{:S(2)}, u32[]{:S(2)}) %all-to-all-start) | async-done | bytes 393248 | tf_op jit(solution)/shard_map/all_to_all | solution.py:512
  41.8 0.1 merge_kernel.1
  41.9 15.7 %all_to_all.15.merged_ref = bf16[4,304,128]{2,1,0:T(8,128)(2,1)S(1)} all-to-all(bf16[4,304,128]{2,1,0:T(8,128)(2,1)S(1)} %merge_kernel.1), channel_id=1, replica_groups=mesh['xz'=32,'yh'=4,'chip'=2,'core'=2] {'yh'}, dimensions={0} | all-to-all | bytes 622592 | tf_op jit(solution)/shard_map/all_to_all | solution.py:543
  57.6 1.2 %far_kernel.1 = bf16[32,48,128]{2,1,0:T(8,128)(2,1)S(1)} custom-call(s32[1]{0:T(128)} %bitcast.3.plane_ref, bf16[4,304,128]{2,1,0:T(8,128)(2,1)S(1)} %all_to_all.15.merged_ref), custom_call_target="tpu_custom_call" | custom-call | tf_op jit(solution)/shard_map/far_kernel/pallas_call | solution.py:463
  58.8 19.0 %all_to_all.16.slots_ref = bf16[32,48,128]{2,1,0:T(8,128)(2,1)S(1)} all-to-all(bf16[32,48,128]{2,1,0:T(8,128)(2,1)S(1)} %far_kernel.1), channel_id=1, replica_groups=mesh['xz'=32,'yh'=4,'chip'=2,'core'=2] {'xz'}, dimensions={0} | all-to-all | bytes 786432 | tf_op jit(solution)/shard_map/all_to_all | solution.py:551
  77.8 1.8 %final_kernel.1 = (bf16[192,256]{1,0:T(8,128)(2,1)}, bf16[192,256]{1,0:T(8,128)(2,1)}, bf16[192,256]{1,0:T(8,128)(2,1)}, f32[192,768]{1,0:T(8,128)}) custom-call(bf16[48,128]{1,0:T(8,128)(2,1)S(1)} %get-tuple-element.42.rows_ref, f32[48,384]{1,0:T(8,128)S(1)} %get-tuple-element.43.scores_ref, f32[48,384]{1,0:T(8,128)S(1)} %get-tuple-element.44.grad_probs_ref, ...), custom_call_target="tpu_custom_call" | custom-call | tf_op jit(solution)/shard_map/final_kernel/pallas_call | solution.py:463
  (1 shorter events, 0.0 us)
Async XLA Ops:
  0.6 11.6 %copy-start.4 = (bf16[192,256]{1,0:T(8,128)(2,1)S(1)}, bf16[192,256]{1,0:T(8,128)(2,1)}, u32[]{:S(2)}) copy-start(bf16[192,256]{1,0:T(8,128)(2,1)} %param.9) | copy-start | bytes 294916
  0.6 11.6 %collective-permute-start = (bf16[192,256]{1,0:T(8,128)(2,1)}, bf16[192,256]{1,0:T(8,128)(2,1)S(1)}, u32[]{:S(2)}, u32[]{:S(2)}) collective-permute-start(bf16[192,256]{1,0:T(8,128)(2,1)} %param.9), channel_id=1, source_target_pairs={{0,2},{2,0},{1,3},{3,1},{4,6},{6,4},{5,7},{7,5},{8,10},{10,8},{9,1... | collective-permute-start | bytes 294920 | tf_op jit(solution)/shard_map/ppermute | solution.py:494
  10.3 6.7 %collective-permute-start.1 = (bf16[64,128]{1,0:T(8,128)(2,1)}, bf16[64,128]{1,0:T(8,128)(2,1)S(1)}, u32[]{:S(2)}, u32[]{:S(2)}) collective-permute-start(bf16[64,128]{1,0:T(8,128)(2,1)} %near_kernel.1), channel_id=1, source_target_pairs={{0,4},{4,0},{8,12},{12,8},{1,5},{5,1},{9,13},{13,9},{2,6},{6,2},{1... | collective-permute-start | bytes 49160 | tf_op jit(solution)/shard_map/ppermute | solution.py:503
  12.3 4.8 %copy-start = (bf16[192,256]{1,0:T(8,128)(2,1)S(1)}, bf16[192,256]{1,0:T(8,128)(2,1)}, u32[]{:S(2)}) copy-start(bf16[192,256]{1,0:T(8,128)(2,1)} %key_ref.5) | copy-start | bytes 294916
  12.3 4.8 %copy-start.1 = (bf16[192,256]{1,0:T(8,128)(2,1)S(1)}, bf16[192,256]{1,0:T(8,128)(2,1)}, u32[]{:S(2)}) copy-start(bf16[192,256]{1,0:T(8,128)(2,1)} %value_ref.5) | copy-start | bytes 294916
  12.3 4.7 %copy-start.2 = (bf16[192,256]{1,0:T(8,128)(2,1)S(1)}, bf16[192,256]{1,0:T(8,128)(2,1)}, u32[]{:S(2)}) copy-start(bf16[192,256]{1,0:T(8,128)(2,1)} %query_ref.3) | copy-start | bytes 294916
  12.3 4.7 %copy-start.3 = (bf16[192,768]{1,0:T(8,128)(2,1)S(1)}, bf16[192,768]{1,0:T(8,128)(2,1)}, u32[]{:S(2)}) copy-start(bf16[192,768]{1,0:T(8,128)(2,1)} %weight_ref.1) | copy-start | bytes 884740
  19.5 22.3 %all-to-all-start = ((bf16[32,48,128]{2,1,0:T(8,128)(2,1)}), bf16[32,48,128]{2,1,0:T(8,128)(2,1)S(1)}, u32[]{:S(2)}, u32[]{:S(2)}) async-start(bf16[32,48,128]{2,1,0:T(8,128)(2,1)} %get-tuple-element.28), calls=%async_computation | async-start | bytes 786432 | tf_op jit(solution)/shard_map/all_to_all | solution.py:512
  28.6 6.5 %collective-permute-start.2 = (bf16[64,128]{1,0:T(8,128)(2,1)S(1)}, bf16[64,128]{1,0:T(8,128)(2,1)S(1)}, u32[]{:S(2)}, u32[]{:S(2)}) collective-permute-start(bf16[64,128]{1,0:T(8,128)(2,1)S(1)} %get-tuple-element.31.own_ref), channel_id=1, source_target_pairs={{0,4},{4,0},{8,12},{12,8},{1,5},{5,1},{9,13},{13,9},{2,6},{6,2},{1... | collective-permute-start | bytes 49160 | tf_op jit(solution)/shard_map/ppermute | solution.py:518

commit v9 on v8

--- a/solution.py
+++ b/solution.py
@@ -118,12 +118,11 @@
 
 
 def pair_count(key_pos, query_pos, offset):
-    count = 1.0 + jnp.where(
-        same_class(key_pos, offset, RB) & same_class(query_pos, offset, RB), 1.0, 0.0
-    )
-    return count + jnp.where(
-        same_class(key_pos, offset, RC) & same_class(query_pos, offset, RC), 1.0, 0.0
-    )
+    count = 1.0
+    for stride in (RB, RC):
+        keys = jnp.where(same_class(key_pos, offset, stride), 1.0, 0.0)
+        count = count + keys * jnp.where(same_class(query_pos, offset, stride), 1.0, 0.0)
+    return count
 
 
 def local_kernel(
@@ -156,9 +155,9 @@
         both = [chunk_rows(wide[:half], chunk), chunk_rows(wide[half:], chunk), filler]
         far_grads.append(mm(choosers, jnp.concatenate(both, axis=0).astype(BF16), 1, 1))
     blank = jnp.zeros((HEAD_DIM, TOKENS_HERE), BF16)
-    key_pos = iota((TOKENS_HERE, TOKENS_HERE), 0)
-    query_pos = iota((TOKENS_HERE, TOKENS_HERE), 1)
+    key_pos = iota((TOKENS_HERE, 1), 0)
     query_row = iota((1, TOKENS_HERE), 1)
+    query_pos = query_row
     heads = range(heads)
     rows = [slice(head * HEAD_DIM, (head + 1) * HEAD_DIM) for head in heads]
     near = [near_ref[head * NEAR : (head + 1) * NEAR] for head in heads]
@@ -231,9 +230,9 @@
 ):
     heads = query_ref.shape[0] // HEAD_DIM
     blank = jnp.zeros((HEAD_DIM, TOKENS_HERE), BF16)
-    key_pos = iota((TOKENS_HERE, TOKENS_HERE), 0)
-    query_pos = iota((TOKENS_HERE, TOKENS_HERE), 1)
+    key_pos = iota((TOKENS_HERE, 1), 0)
     query_row = iota((1, TOKENS_HERE), 1)
+    query_pos = query_row
     far_rows = jnp.zeros((GAP, LANES), F32)
     for head in range(heads):
         offset = told_offset(near_ref, head)
@@ -424,12 +423,13 @@
     heads = local_query_ref.shape[0] // HEAD_DIM
     half = grad_weight_ref.shape[1] // 2
     chunks = pl.cdiv(half, CHUNK)
+    eye = one_hot(iota((LANES, LANES), 0) == iota((LANES, LANES), 1))
     for head in range(heads):
         rows = slice(head * HEAD_DIM, (head + 1) * HEAD_DIM)
         block = slice(head * GAP, (head + 1) * GAP)
         pieces = [slots_ref[head * chunks + chunk].astype(F32) for chunk in range(chunks)]
         folded = jnp.concatenate([piece[:CHUNK] for piece in pieces], axis=0)[:half]
-        unfolded = jnp.transpose(folded)
+        unfolded = mm(eye, folded.astype(BF16), 1, 1)
         grad_weight_ref[rows, :half] = unfolded[:HEAD_DIM]
         grad_weight_ref[rows, half:] = unfolded[HEAD_DIM:]
 

time: 80.1 us -> 79.8 us (level)
  no operation moved by 1% of the time
where the time goes in v9:
time: 79.8 us; the launch traced here: 79.4 us
  blocking collectives  37 us (46%)
  starting transfers between devices  22.1 us (28%)
  waiting for transfers between devices  10.6 us (13%)
  Pallas kernels  8.85 us (11%)
    all_to_all x1, blocking collectives, local(): slots = lax.all_to_all(slots, 'xz', 0, 0, tiled=True)  19 us
    all_to_all x1, blocking collectives, local(): merged = lax.all_to_all(merged, 'yh', 0, 0, tiled=True)  15.7 us
    pallas_call x7, Pallas kernels, call(): pl.pallas_call(kernel, out_shape=shapes, in_specs=specs, out_specs=[pl.Bl...  8.85 us
    all_to_all x1, starting transfers between devices, local(): slots = lax.all_to_all(slots, 'xz', 0, 0, tiled=True)  7.89 us
    ppermute x1, starting transfers between devices, local(): other_grad = lax.ppermute(grad_out, 'chip', [(0, 1), (1, 0)])  7.86 us
    all_to_all x1, waiting for transfers between devices, local(): slots = lax.all_to_all(slots, 'xz', 0, 0, tiled=True)  5.99 us
    ppermute x1, starting transfers between devices, local(): partner = lax.ppermute(own, 'yh', other)  4.4 us
    ppermute x1, waiting for transfers between devices, local(): near = lax.ppermute(near, 'yh', other)  2.49 us
  transfers between devices with their start and end apart: 4, of which 3 were waited for; matrix products, arithmetic and copies ran while one was open for 0% of the time, Pallas kernels for 5%

profile of v9, /device:TPU:8, one launch (start us, length us, event | category | flops | bytes accessed | tf_op | source)
XLA Modules:
  0.0 79.4 jit_solution(3673436014257764182)
XLA Ops:
  0.6 0.0 copy-start.4
  0.6 7.9 %collective-permute-start = (bf16[192,256]{1,0:T(8,128)(2,1)}, bf16[192,256]{1,0:T(8,128)(2,1)S(1)}, u32[]{:S(2)}, u32[]{:S(2)}) collective-permute-start(bf16[192,256]{1,0:T(8,128)(2,1)} %param.9), channel_id=1, source_target_pairs={{0,2},{2,0},{1,3},{3,1},{4,6},{6,4},{5,7},{7,5},{8,10},{10,8},{9,1... | collective-permute-start | bytes 294920 | tf_op jit(solution)/shard_map/ppermute | solution.py:494
  8.5 1.8 %near_kernel.1 = bf16[64,128]{1,0:T(8,128)(2,1)} custom-call(s32[3]{0:T(128)} %offset_hbm.1, bf16[192,256]{1,0:T(8,128)(2,1)} %key_ref.5, bf16[192,256]{1,0:T(8,128)(2,1)} %value_ref.5), custom_call_target="tpu_custom_call" | custom-call | tf_op jit(solution)/shard_map/near_kernel/pallas_call | solution.py:463
  10.3 1.9 %collective-permute-start.1 = (bf16[64,128]{1,0:T(8,128)(2,1)}, bf16[64,128]{1,0:T(8,128)(2,1)S(1)}, u32[]{:S(2)}, u32[]{:S(2)}) collective-permute-start(bf16[64,128]{1,0:T(8,128)(2,1)} %near_kernel.1), channel_id=1, source_target_pairs={{0,4},{4,0},{8,12},{12,8},{1,5},{5,1},{9,13},{13,9},{2,6},{6,2},{1... | collective-permute-start | bytes 49160 | tf_op jit(solution)/shard_map/ppermute | solution.py:503
  12.2 0.0 collective-permute-done
  12.2 0.0 copy-done.4
  12.3 0.0 copy-start
  12.3 0.0 copy-start.1
  12.3 0.0 copy-start.2
  12.3 0.0 copy-start.3
  12.3 2.2 %all_gather.3.grad_ref = bf16[4,192,256]{2,1,0:T(8,128)(2,1)S(1)} all-gather(bf16[2,192,256]{2,1,0:T(8,128)(2,1)S(1)} %pad_maximum_fusion), channel_id=1, replica_groups=mesh['xz'=32,'yh'=4,'chip'=2,'core'=2] {'core'}, dimensions={0}, use_global_device_ids=true | all-gather | bytes 589824 | tf_op jit(solution)/shard_map/all_gather | solution.py:504
  14.5 2.5 %collective-permute-done.1.near_ref = bf16[64,128]{1,0:T(8,128)(2,1)S(1)} collective-permute-done((bf16[64,128]{1,0:T(8,128)(2,1)}, bf16[64,128]{1,0:T(8,128)(2,1)S(1)}, u32[]{:S(2)}, u32[]{:S(2)}) %collective-permute-start.1) | collective-permute-done | bytes 16416 | tf_op jit(solution)/shard_map/ppermute | solution.py:503
  17.0 0.0 copy-done
  17.0 0.0 copy-done.1
  17.0 0.0 copy-done.2
  17.0 0.0 copy-done.3
  17.0 2.2 %local_kernel.1 = (bf16[32,48,128]{2,1,0:T(8,128)(2,1)}, bf16[192,256]{1,0:T(8,128)(2,1)S(1)}, f32[24,256]{1,0:T(8,128)S(1)}) custom-call(s32[1]{0:T(128)} %bitcast.side_ref, bf16[192,256]{1,0:T(8,128)(2,1)S(1)} %copy-done.2, bf16[192,256]{1,0:T(8,128)(2,1)S(1)} %copy-done, bf16[192,256]{1,0:T(8,128)(2,1)S(1)} %copy-done.1, ...), custom_call_target="tpu_custom_call" | custom-call | tf_op jit(solution)/shard_map/local_kernel/pallas_call | solution.py:463
  19.2 7.9 %all-to-all-start = ((bf16[32,48,128]{2,1,0:T(8,128)(2,1)}), bf16[32,48,128]{2,1,0:T(8,128)(2,1)S(1)}, u32[]{:S(2)}, u32[]{:S(2)}) async-start(bf16[32,48,128]{2,1,0:T(8,128)(2,1)} %get-tuple-element.28), calls=%async_computation | async-start | bytes 786432 | tf_op jit(solution)/shard_map/all_to_all | solution.py:512
  27.1 1.2 %local_grad_kernel.1 = (bf16[64,128]{1,0:T(8,128)(2,1)S(1)}, f32[192,256]{1,0:T(8,128)S(1)}, f32[192,256]{1,0:T(8,128)S(1)}, f32[192,256]{1,0:T(8,128)S(1)}) custom-call(bf16[192,256]{1,0:T(8,128)(2,1)S(1)} %copy-done.2, bf16[192,256]{1,0:T(8,128)(2,1)S(1)} %copy-done, bf16[192,256]{1,0:T(8,128)(2,1)S(1)} %copy-done.1, ...), custom_call_target="tpu_custom_call" | custom-call | tf_op jit(solution)/shard_map/local_grad_kernel/pallas_call | solution.py:463
  28.4 4.4 %collective-permute-start.2 = (bf16[64,128]{1,0:T(8,128)(2,1)S(1)}, bf16[64,128]{1,0:T(8,128)(2,1)S(1)}, u32[]{:S(2)}, u32[]{:S(2)}) collective-permute-start(bf16[64,128]{1,0:T(8,128)(2,1)S(1)} %get-tuple-element.31.own_ref), channel_id=1, source_target_pairs={{0,4},{4,0},{8,12},{12,8},{1,5},{5,1},{9,13},{13,9},{2,6},{6,2},{1... | collective-permute-start | bytes 49160 | tf_op jit(solution)/shard_map/ppermute | solution.py:518
  32.8 2.1 %collective-permute-done.2.partner_ref = bf16[64,128]{1,0:T(8,128)(2,1)S(1)} collective-permute-done((bf16[64,128]{1,0:T(8,128)(2,1)S(1)}, bf16[64,128]{1,0:T(8,128)(2,1)S(1)}, u32[]{:S(2)}, u32[]{:S(2)}) %collective-permute-start.2) | collective-permute-done | bytes 16416 | tf_op jit(solution)/shard_map/ppermute | solution.py:518
  34.9 0.7 prepare_kernel.1
  35.6 6.0 %all-to-all-done.slots_ref = bf16[32,48,128]{2,1,0:T(8,128)(2,1)S(1)} async-done(((bf16[32,48,128]{2,1,0:T(8,128)(2,1)}), bf16[32,48,128]{2,1,0:T(8,128)(2,1)S(1)}, u32[]{:S(2)}, u32[]{:S(2)}) %all-to-all-start) | async-done | bytes 393248 | tf_op jit(solution)/shard_map/all_to_all | solution.py:512
  41.6 0.1 merge_kernel.1
  41.6 15.7 %all_to_all.15.merged_ref = bf16[4,304,128]{2,1,0:T(8,128)(2,1)S(1)} all-to-all(bf16[4,304,128]{2,1,0:T(8,128)(2,1)S(1)} %merge_kernel.1), channel_id=1, replica_groups=mesh['xz'=32,'yh'=4,'chip'=2,'core'=2] {'yh'}, dimensions={0} | all-to-all | bytes 622592 | tf_op jit(solution)/shard_map/all_to_all | solution.py:543
  57.4 1.2 %far_kernel.1 = bf16[32,48,128]{2,1,0:T(8,128)(2,1)S(1)} custom-call(s32[1]{0:T(128)} %bitcast.3.plane_ref, bf16[4,304,128]{2,1,0:T(8,128)(2,1)S(1)} %all_to_all.15.merged_ref), custom_call_target="tpu_custom_call" | custom-call | tf_op jit(solution)/shard_map/far_kernel/pallas_call | solution.py:463
  58.6 19.0 %all_to_all.16.slots_ref = bf16[32,48,128]{2,1,0:T(8,128)(2,1)S(1)} all-to-all(bf16[32,48,128]{2,1,0:T(8,128)(2,1)S(1)} %far_kernel.1), channel_id=1, replica_groups=mesh['xz'=32,'yh'=4,'chip'=2,'core'=2] {'xz'}, dimensions={0} | all-to-all | bytes 786432 | tf_op jit(solution)/shard_map/all_to_all | solution.py:551
  77.6 1.8 %final_kernel.1 = (bf16[192,256]{1,0:T(8,128)(2,1)}, bf16[192,256]{1,0:T(8,128)(2,1)}, bf16[192,256]{1,0:T(8,128)(2,1)}, f32[192,768]{1,0:T(8,128)}) custom-call(bf16[48,128]{1,0:T(8,128)(2,1)S(1)} %get-tuple-element.42.rows_ref, f32[48,384]{1,0:T(8,128)S(1)} %get-tuple-element.43.scores_ref, f32[48,384]{1,0:T(8,128)S(1)} %get-tuple-element.44.grad_probs_ref, ...), custom_call_target="tpu_custom_call" | custom-call | tf_op jit(solution)/shard_map/final_kernel/pallas_call | solution.py:463
  (1 shorter events, 0.0 us)
Async XLA Ops:
  0.6 11.6 %copy-start.4 = (bf16[192,256]{1,0:T(8,128)(2,1)S(1)}, bf16[192,256]{1,0:T(8,128)(2,1)}, u32[]{:S(2)}) copy-start(bf16[192,256]{1,0:T(8,128)(2,1)} %param.9) | copy-start | bytes 294916
  0.6 11.6 %collective-permute-start = (bf16[192,256]{1,0:T(8,128)(2,1)}, bf16[192,256]{1,0:T(8,128)(2,1)S(1)}, u32[]{:S(2)}, u32[]{:S(2)}) collective-permute-start(bf16[192,256]{1,0:T(8,128)(2,1)} %param.9), channel_id=1, source_target_pairs={{0,2},{2,0},{1,3},{3,1},{4,6},{6,4},{5,7},{7,5},{8,10},{10,8},{9,1... | collective-permute-start | bytes 294920 | tf_op jit(solution)/shard_map/ppermute | solution.py:494
  10.3 6.7 %collective-permute-start.1 = (bf16[64,128]{1,0:T(8,128)(2,1)}, bf16[64,128]{1,0:T(8,128)(2,1)S(1)}, u32[]{:S(2)}, u32[]{:S(2)}) collective-permute-start(bf16[64,128]{1,0:T(8,128)(2,1)} %near_kernel.1), channel_id=1, source_target_pairs={{0,4},{4,0},{8,12},{12,8},{1,5},{5,1},{9,13},{13,9},{2,6},{6,2},{1... | collective-permute-start | bytes 49160 | tf_op jit(solution)/shard_map/ppermute | solution.py:503
  12.3 4.8 %copy-start = (bf16[192,256]{1,0:T(8,128)(2,1)S(1)}, bf16[192,256]{1,0:T(8,128)(2,1)}, u32[]{:S(2)}) copy-start(bf16[192,256]{1,0:T(8,128)(2,1)} %key_ref.5) | copy-start | bytes 294916
  12.3 4.8 %copy-start.1 = (bf16[192,256]{1,0:T(8,128)(2,1)S(1)}, bf16[192,256]{1,0:T(8,128)(2,1)}, u32[]{:S(2)}) copy-start(bf16[192,256]{1,0:T(8,128)(2,1)} %value_ref.5) | copy-start | bytes 294916
  12.3 4.7 %copy-start.2 = (bf16[192,256]{1,0:T(8,128)(2,1)S(1)}, bf16[192,256]{1,0:T(8,128)(2,1)}, u32[]{:S(2)}) copy-start(bf16[192,256]{1,0:T(8,128)(2,1)} %query_ref.3) | copy-start | bytes 294916
  12.3 4.7 %copy-start.3 = (bf16[192,768]{1,0:T(8,128)(2,1)S(1)}, bf16[192,768]{1,0:T(8,128)(2,1)}, u32[]{:S(2)}) copy-start(bf16[192,768]{1,0:T(8,128)(2,1)} %weight_ref.1) | copy-start | bytes 884740
  19.2 22.3 %all-to-all-start = ((bf16[32,48,128]{2,1,0:T(8,128)(2,1)}), bf16[32,48,128]{2,1,0:T(8,128)(2,1)S(1)}, u32[]{:S(2)}, u32[]{:S(2)}) async-start(bf16[32,48,128]{2,1,0:T(8,128)(2,1)} %get-tuple-element.28), calls=%async_computation | async-start | bytes 786432 | tf_op jit(solution)/shard_map/all_to_all | solution.py:512
  28.4 6.5 %collective-permute-start.2 = (bf16[64,128]{1,0:T(8,128)(2,1)S(1)}, bf16[64,128]{1,0:T(8,128)(2,1)S(1)}, u32[]{:S(2)}, u32[]{:S(2)}) collective-permute-start(bf16[64,128]{1,0:T(8,128)(2,1)S(1)} %get-tuple-element.31.own_ref), channel_id=1, source_target_pairs={{0,4},{4,0},{8,12},{12,8},{1,5},{5,1},{9,13},{13,9},{2,6},{6,2},{1... | collective-permute-start | bytes 49160 | tf_op jit(solution)/shard_map/ppermute | solution.py:518

commit v10 on v9

--- a/solution.py
+++ b/solution.py
@@ -22,7 +22,7 @@
 CHUNK = 40
 SLOT = CHUNK + SMALL
 ABSENT = -1e30
-LIMIT = 63_400_000
+LIMIT = 40 << 20
 
 F32 = jnp.float32
 BF16 = jnp.bfloat16
@@ -495,7 +495,7 @@
     (near,) = call(
         near_kernel,
         [near_shape],
-        (offsets, keys, values),
+        tuple(pltpu.with_memory_space_constraint(x, pltpu.HBM) for x in (offsets, keys, values)),
         scratch=scratch,
         space=pltpu.HBM,
         limit=LIMIT,

time: 79.8 us -> 79.6 us (level)
  transfers between devices with their start and end apart: 4 -> 4, of which waited for: 3 -> 3; matrix products, arithmetic and copies ran while one was open for 0% -> 0% of each run, Pallas kernels for 5% -> 4%
where the time goes in v10:
time: 79.6 us; the launch traced here: 79.2 us
  blocking collectives  37.4 us (47%)
  starting transfers between devices  22.1 us (28%)
  waiting for transfers between devices  10.6 us (13%)
  Pallas kernels  8.27 us (10%)
    all_to_all x1, blocking collectives, local(): slots = lax.all_to_all(slots, 'xz', 0, 0, tiled=True)  19.3 us
    all_to_all x1, blocking collectives, local(): merged = lax.all_to_all(merged, 'yh', 0, 0, tiled=True)  15.9 us
    pallas_call x7, Pallas kernels, call(): pl.pallas_call(kernel, out_shape=shapes, in_specs=specs, out_specs=[pl.Bl...  8.27 us
    all_to_all x1, starting transfers between devices, local(): slots = lax.all_to_all(slots, 'xz', 0, 0, tiled=True)  8.11 us
    ppermute x1, starting transfers between devices, local(): other_grad = lax.ppermute(grad_out, 'chip', [(0, 1), (1, 0)])  7.86 us
    all_to_all x1, waiting for transfers between devices, local(): slots = lax.all_to_all(slots, 'xz', 0, 0, tiled=True)  5.99 us
    ppermute x1, starting transfers between devices, local(): partner = lax.ppermute(own, 'yh', other)  4.19 us
    ppermute x1, waiting for transfers between devices, local(): partner = lax.ppermute(own, 'yh', other)  2.34 us
  transfers between devices with their start and end apart: 4, of which 3 were waited for; matrix products, arithmetic and copies ran while one was open for 0% of the time, Pallas kernels for 4%

profile of v10, /device:TPU:8, one launch (start us, length us, event | category | flops | bytes accessed | tf_op | source)
XLA Modules:
  0.0 79.2 jit_solution(1352802264920349602)
XLA Ops:
  0.6 0.0 copy-start.4
  0.6 7.9 %collective-permute-start = (bf16[192,256]{1,0:T(8,128)(2,1)}, bf16[192,256]{1,0:T(8,128)(2,1)S(1)}, u32[]{:S(2)}, u32[]{:S(2)}) collective-permute-start(bf16[192,256]{1,0:T(8,128)(2,1)} %param.9), channel_id=1, source_target_pairs={{0,2},{2,0},{1,3},{3,1},{4,6},{6,4},{5,7},{7,5},{8,10},{10,8},{9,1... | collective-permute-start | bytes 294920 | tf_op jit(solution)/shard_map/ppermute | solution.py:494
  8.5 1.2 %near_kernel.1 = bf16[64,128]{1,0:T(8,128)(2,1)S(1)} custom-call(s32[3]{0:T(128)} %offset_hbm.1, bf16[192,256]{1,0:T(8,128)(2,1)} %key_ref.5, bf16[192,256]{1,0:T(8,128)(2,1)} %value_ref.5), custom_call_target="tpu_custom_call" | custom-call | tf_op jit(solution)/shard_map/near_kernel/pallas_call | solution.py:463
  9.7 1.9 %collective-permute-start.1 = (bf16[64,128]{1,0:T(8,128)(2,1)S(1)}, bf16[64,128]{1,0:T(8,128)(2,1)S(1)}, u32[]{:S(2)}, u32[]{:S(2)}) collective-permute-start(bf16[64,128]{1,0:T(8,128)(2,1)S(1)} %near_kernel.1), channel_id=1, source_target_pairs={{0,4},{4,0},{8,12},{12,8},{1,5},{5,1},{9,13},{13,9},{2,6},{6,2},{1... | collective-permute-start | bytes 49160 | tf_op jit(solution)/shard_map/ppermute | solution.py:503
  11.6 0.0 collective-permute-done
  11.6 0.0 copy-done.4
  11.7 0.0 copy-start
  11.7 0.0 copy-start.1
  11.7 0.0 copy-start.2
  11.7 0.0 copy-start.3
  11.7 2.2 %all_gather.3.grad_ref = bf16[4,192,256]{2,1,0:T(8,128)(2,1)S(1)} all-gather(bf16[2,192,256]{2,1,0:T(8,128)(2,1)S(1)} %pad_maximum_fusion), channel_id=1, replica_groups=mesh['xz'=32,'yh'=4,'chip'=2,'core'=2] {'core'}, dimensions={0}, use_global_device_ids=true | all-gather | bytes 589824 | tf_op jit(solution)/shard_map/all_gather | solution.py:504
  13.9 2.3 %collective-permute-done.1.near_ref = bf16[64,128]{1,0:T(8,128)(2,1)S(1)} collective-permute-done((bf16[64,128]{1,0:T(8,128)(2,1)S(1)}, bf16[64,128]{1,0:T(8,128)(2,1)S(1)}, u32[]{:S(2)}, u32[]{:S(2)}) %collective-permute-start.1) | collective-permute-done | bytes 16416 | tf_op jit(solution)/shard_map/ppermute | solution.py:503
  16.2 0.0 copy-done
  16.2 0.0 copy-done.1
  16.2 0.0 copy-done.2
  16.2 0.0 copy-done.3
  16.2 2.2 %local_kernel.1 = (bf16[32,48,128]{2,1,0:T(8,128)(2,1)}, bf16[192,256]{1,0:T(8,128)(2,1)S(1)}, f32[24,256]{1,0:T(8,128)S(1)}) custom-call(s32[1]{0:T(128)} %bitcast.side_ref, bf16[192,256]{1,0:T(8,128)(2,1)S(1)} %copy-done.2, bf16[192,256]{1,0:T(8,128)(2,1)S(1)} %copy-done, bf16[192,256]{1,0:T(8,128)(2,1)S(1)} %copy-done.1, ...), custom_call_target="tpu_custom_call" | custom-call | tf_op jit(solution)/shard_map/local_kernel/pallas_call | solution.py:463
  18.4 8.1 %all-to-all-start = ((bf16[32,48,128]{2,1,0:T(8,128)(2,1)}), bf16[32,48,128]{2,1,0:T(8,128)(2,1)S(1)}, u32[]{:S(2)}, u32[]{:S(2)}) async-start(bf16[32,48,128]{2,1,0:T(8,128)(2,1)} %get-tuple-element.28), calls=%async_computation | async-start | bytes 786432 | tf_op jit(solution)/shard_map/all_to_all | solution.py:512
  26.5 1.2 %local_grad_kernel.1 = (bf16[64,128]{1,0:T(8,128)(2,1)S(1)}, f32[192,256]{1,0:T(8,128)S(1)}, f32[192,256]{1,0:T(8,128)S(1)}, f32[192,256]{1,0:T(8,128)S(1)}) custom-call(bf16[192,256]{1,0:T(8,128)(2,1)S(1)} %copy-done.2, bf16[192,256]{1,0:T(8,128)(2,1)S(1)} %copy-done, bf16[192,256]{1,0:T(8,128)(2,1)S(1)} %copy-done.1, ...), custom_call_target="tpu_custom_call" | custom-call | tf_op jit(solution)/shard_map/local_grad_kernel/pallas_call | solution.py:463
  27.8 4.2 %collective-permute-start.2 = (bf16[64,128]{1,0:T(8,128)(2,1)S(1)}, bf16[64,128]{1,0:T(8,128)(2,1)S(1)}, u32[]{:S(2)}, u32[]{:S(2)}) collective-permute-start(bf16[64,128]{1,0:T(8,128)(2,1)S(1)} %get-tuple-element.31.own_ref), channel_id=1, source_target_pairs={{0,4},{4,0},{8,12},{12,8},{1,5},{5,1},{9,13},{13,9},{2,6},{6,2},{1... | collective-permute-start | bytes 49160 | tf_op jit(solution)/shard_map/ppermute | solution.py:518
  32.0 2.3 %collective-permute-done.2.partner_ref = bf16[64,128]{1,0:T(8,128)(2,1)S(1)} collective-permute-done((bf16[64,128]{1,0:T(8,128)(2,1)S(1)}, bf16[64,128]{1,0:T(8,128)(2,1)S(1)}, u32[]{:S(2)}, u32[]{:S(2)}) %collective-permute-start.2) | collective-permute-done | bytes 16416 | tf_op jit(solution)/shard_map/ppermute | solution.py:518
  34.3 0.7 prepare_kernel.1
  35.0 6.0 %all-to-all-done.slots_ref = bf16[32,48,128]{2,1,0:T(8,128)(2,1)S(1)} async-done(((bf16[32,48,128]{2,1,0:T(8,128)(2,1)}), bf16[32,48,128]{2,1,0:T(8,128)(2,1)S(1)}, u32[]{:S(2)}, u32[]{:S(2)}) %all-to-all-start) | async-done | bytes 393248 | tf_op jit(solution)/shard_map/all_to_all | solution.py:512
  41.0 0.1 merge_kernel.1
  41.1 15.9 %all_to_all.15.merged_ref = bf16[4,304,128]{2,1,0:T(8,128)(2,1)S(1)} all-to-all(bf16[4,304,128]{2,1,0:T(8,128)(2,1)S(1)} %merge_kernel.1), channel_id=1, replica_groups=mesh['xz'=32,'yh'=4,'chip'=2,'core'=2] {'yh'}, dimensions={0} | all-to-all | bytes 622592 | tf_op jit(solution)/shard_map/all_to_all | solution.py:543
  57.0 1.2 %far_kernel.1 = bf16[32,48,128]{2,1,0:T(8,128)(2,1)S(1)} custom-call(s32[1]{0:T(128)} %bitcast.3.plane_ref, bf16[4,304,128]{2,1,0:T(8,128)(2,1)S(1)} %all_to_all.15.merged_ref), custom_call_target="tpu_custom_call" | custom-call | tf_op jit(solution)/shard_map/far_kernel/pallas_call | solution.py:463
  58.2 19.3 %all_to_all.16.slots_ref = bf16[32,48,128]{2,1,0:T(8,128)(2,1)S(1)} all-to-all(bf16[32,48,128]{2,1,0:T(8,128)(2,1)S(1)} %far_kernel.1), channel_id=1, replica_groups=mesh['xz'=32,'yh'=4,'chip'=2,'core'=2] {'xz'}, dimensions={0} | all-to-all | bytes 786432 | tf_op jit(solution)/shard_map/all_to_all | solution.py:551
  77.4 1.8 %final_kernel.1 = (bf16[192,256]{1,0:T(8,128)(2,1)}, bf16[192,256]{1,0:T(8,128)(2,1)}, bf16[192,256]{1,0:T(8,128)(2,1)}, f32[192,768]{1,0:T(8,128)}) custom-call(bf16[48,128]{1,0:T(8,128)(2,1)S(1)} %get-tuple-element.42.rows_ref, f32[48,384]{1,0:T(8,128)S(1)} %get-tuple-element.43.scores_ref, f32[48,384]{1,0:T(8,128)S(1)} %get-tuple-element.44.grad_probs_ref, ...), custom_call_target="tpu_custom_call" | custom-call | tf_op jit(solution)/shard_map/final_kernel/pallas_call | solution.py:463
  (1 shorter events, 0.0 us)
Async XLA Ops:
  0.6 11.0 %copy-start.4 = (bf16[192,256]{1,0:T(8,128)(2,1)S(1)}, bf16[192,256]{1,0:T(8,128)(2,1)}, u32[]{:S(2)}) copy-start(bf16[192,256]{1,0:T(8,128)(2,1)} %param.9) | copy-start | bytes 294916
  0.6 11.0 %collective-permute-start = (bf16[192,256]{1,0:T(8,128)(2,1)}, bf16[192,256]{1,0:T(8,128)(2,1)S(1)}, u32[]{:S(2)}, u32[]{:S(2)}) collective-permute-start(bf16[192,256]{1,0:T(8,128)(2,1)} %param.9), channel_id=1, source_target_pairs={{0,2},{2,0},{1,3},{3,1},{4,6},{6,4},{5,7},{7,5},{8,10},{10,8},{9,1... | collective-permute-start | bytes 294920 | tf_op jit(solution)/shard_map/ppermute | solution.py:494
  9.7 6.5 %collective-permute-start.1 = (bf16[64,128]{1,0:T(8,128)(2,1)S(1)}, bf16[64,128]{1,0:T(8,128)(2,1)S(1)}, u32[]{:S(2)}, u32[]{:S(2)}) collective-permute-start(bf16[64,128]{1,0:T(8,128)(2,1)S(1)} %near_kernel.1), channel_id=1, source_target_pairs={{0,4},{4,0},{8,12},{12,8},{1,5},{5,1},{9,13},{13,9},{2,6},{6,2},{1... | collective-permute-start | bytes 49160 | tf_op jit(solution)/shard_map/ppermute | solution.py:503
  11.7 4.5 %copy-start = (bf16[192,256]{1,0:T(8,128)(2,1)S(1)}, bf16[192,256]{1,0:T(8,128)(2,1)}, u32[]{:S(2)}) copy-start(bf16[192,256]{1,0:T(8,128)(2,1)} %key_ref.5) | copy-start | bytes 294916
  11.7 4.5 %copy-start.1 = (bf16[192,256]{1,0:T(8,128)(2,1)S(1)}, bf16[192,256]{1,0:T(8,128)(2,1)}, u32[]{:S(2)}) copy-start(bf16[192,256]{1,0:T(8,128)(2,1)} %value_ref.5) | copy-start | bytes 294916
  11.7 4.5 %copy-start.2 = (bf16[192,256]{1,0:T(8,128)(2,1)S(1)}, bf16[192,256]{1,0:T(8,128)(2,1)}, u32[]{:S(2)}) copy-start(bf16[192,256]{1,0:T(8,128)(2,1)} %query_ref.3) | copy-start | bytes 294916
  11.7 4.5 %copy-start.3 = (bf16[192,768]{1,0:T(8,128)(2,1)S(1)}, bf16[192,768]{1,0:T(8,128)(2,1)}, u32[]{:S(2)}) copy-start(bf16[192,768]{1,0:T(8,128)(2,1)} %weight_ref.1) | copy-start | bytes 884740
  18.4 22.6 %all-to-all-start = ((bf16[32,48,128]{2,1,0:T(8,128)(2,1)}), bf16[32,48,128]{2,1,0:T(8,128)(2,1)S(1)}, u32[]{:S(2)}, u32[]{:S(2)}) async-start(bf16[32,48,128]{2,1,0:T(8,128)(2,1)} %get-tuple-element.28), calls=%async_computation | async-start | bytes 786432 | tf_op jit(solution)/shard_map/all_to_all | solution.py:512
  27.8 6.5 %collective-permute-start.2 = (bf16[64,128]{1,0:T(8,128)(2,1)S(1)}, bf16[64,128]{1,0:T(8,128)(2,1)S(1)}, u32[]{:S(2)}, u32[]{:S(2)}) collective-permute-start(bf16[64,128]{1,0:T(8,128)(2,1)S(1)} %get-tuple-element.31.own_ref), channel_id=1, source_target_pairs={{0,4},{4,0},{8,12},{12,8},{1,5},{5,1},{9,13},{13,9},{2,6},{6,2},{1... | collective-permute-start | bytes 49160 | tf_op jit(solution)/shard_map/ppermute | solution.py:518

commit v11 on v10

--- a/solution.py
+++ b/solution.py
@@ -181,17 +181,17 @@
     ]
     log_mass = [peak[h] + jnp.log(total[h]) for h in heads]
     inverse = [1.0 / total[h] for h in heads]
-    probs_low = [(mass[h] * inverse[h]).astype(BF16) for h in heads]
-    near_low = [(near_mass[h] * inverse[h]).astype(BF16) for h in heads]
     attended = [
-        mm(value_ref[rows[h]], probs_low[h], 1, 0) + mm(near[h], near_low[h], 0, 0)[HEAD_DIM:]
+        mm(value_ref[rows[h]], mass[h].astype(BF16), 1, 0)
+        + mm(near[h], near_mass[h].astype(BF16), 0, 0)[HEAD_DIM:]
         for h in heads
     ]
-    kept = [jnp.where(in_far[h], 0.0, attended[h]).astype(BF16) for h in heads]
+    attended = [attended[h] * inverse[h] for h in heads]
+    kept = [jnp.where(in_far[h], 0.0, attended[h]).astype(BF16) * WEIGHT_SCALE for h in heads]
     over = [jnp.concatenate([kept[h], blank], axis=0) for h in heads]
     under = [jnp.concatenate([blank, kept[h]], axis=0) for h in heads]
     weight_part = [
-        (mm(grad[:half], over[h], 1, 1) + mm(grad[half:], under[h], 1, 1)) * WEIGHT_SCALE
+        mm(grad[:half], over[h], 1, 1) + mm(grad[half:], under[h], 1, 1)
         for h in heads
     ]
     delta = [
@@ -314,9 +314,10 @@
     local_part = local_part * inverse
     probs = mass * inverse
     probs_low = probs.astype(BF16)
-    under = local_part * stats + mm(probs_low, key_value, 1, 0)
+    mass_low = mass.astype(BF16)
+    under = local_part * stats + mm(mass_low, key_value, 1, 0) * inverse
     delta = jnp.sum(dout_wide * under, axis=1, keepdims=True)
-    over = local_part * attended_stats + mm(probs_low, value_key, 1, 0)
+    over = local_part * attended_stats + mm(mass_low, value_key, 1, 0) * inverse
     over = jnp.where(left, over, 0.0).astype(BF16)
     under = jnp.where(left, 0.0, under).astype(BF16)
     grad_scores = (probs * (grad_probs - delta)).astype(BF16)

time: 79.6 us -> 79.4 us (level)
  no operation moved by 1% of the time
where the time goes in v11:
time: 79.4 us; the launch traced here: 79 us
  blocking collectives  37.4 us (47%)
  starting transfers between devices  22.1 us (28%)
  waiting for transfers between devices  10.6 us (13%)
  Pallas kernels  8.08 us (10%)
    all_to_all x1, blocking collectives, local(): slots = lax.all_to_all(slots, 'xz', 0, 0, tiled=True)  19.2 us
    all_to_all x1, blocking collectives, local(): merged = lax.all_to_all(merged, 'yh', 0, 0, tiled=True)  15.9 us
    all_to_all x1, starting transfers between devices, local(): slots = lax.all_to_all(slots, 'xz', 0, 0, tiled=True)  8.11 us
    pallas_call x7, Pallas kernels, call(): pl.pallas_call(kernel, out_shape=shapes, in_specs=specs, out_specs=[pl.Bl...  8.08 us
    ppermute x1, starting transfers between devices, local(): other_grad = lax.ppermute(grad_out, 'chip', [(0, 1), (1, 0)])  7.86 us
    all_to_all x1, waiting for transfers between devices, local(): slots = lax.all_to_all(slots, 'xz', 0, 0, tiled=True)  5.99 us
    ppermute x1, starting transfers between devices, local(): partner = lax.ppermute(own, 'yh', other)  4.2 us
    ppermute x1, waiting for transfers between devices, local(): partner = lax.ppermute(own, 'yh', other)  2.33 us
  transfers between devices with their start and end apart: 4, of which 3 were waited for; matrix products, arithmetic and copies ran while one was open for 0% of the time, Pallas kernels for 4%

profile of v11, /device:TPU:8, one launch (start us, length us, event | category | flops | bytes accessed | tf_op | source)
XLA Modules:
  0.0 79.0 jit_solution(15865752247987030340)
XLA Ops:
  0.6 0.0 copy-start.4
  0.6 7.9 %collective-permute-start = (bf16[192,256]{1,0:T(8,128)(2,1)}, bf16[192,256]{1,0:T(8,128)(2,1)S(1)}, u32[]{:S(2)}, u32[]{:S(2)}) collective-permute-start(bf16[192,256]{1,0:T(8,128)(2,1)} %param.9), channel_id=1, source_target_pairs={{0,2},{2,0},{1,3},{3,1},{4,6},{6,4},{5,7},{7,5},{8,10},{10,8},{9,1... | collective-permute-start | bytes 294920 | tf_op jit(solution)/shard_map/ppermute | solution.py:495
  8.5 1.2 %near_kernel.1 = bf16[64,128]{1,0:T(8,128)(2,1)S(1)} custom-call(s32[3]{0:T(128)} %offset_hbm.1, bf16[192,256]{1,0:T(8,128)(2,1)} %key_ref.5, bf16[192,256]{1,0:T(8,128)(2,1)} %value_ref.5), custom_call_target="tpu_custom_call" | custom-call | tf_op jit(solution)/shard_map/near_kernel/pallas_call | solution.py:464
  9.7 1.9 %collective-permute-start.1 = (bf16[64,128]{1,0:T(8,128)(2,1)S(1)}, bf16[64,128]{1,0:T(8,128)(2,1)S(1)}, u32[]{:S(2)}, u32[]{:S(2)}) collective-permute-start(bf16[64,128]{1,0:T(8,128)(2,1)S(1)} %near_kernel.1), channel_id=1, source_target_pairs={{0,4},{4,0},{8,12},{12,8},{1,5},{5,1},{9,13},{13,9},{2,6},{6,2},{1... | collective-permute-start | bytes 49160 | tf_op jit(solution)/shard_map/ppermute | solution.py:504
  11.6 0.0 collective-permute-done
  11.6 0.0 copy-done.4
  11.7 0.0 copy-start
  11.7 0.0 copy-start.1
  11.7 0.0 copy-start.2
  11.7 0.0 copy-start.3
  11.7 2.2 %all_gather.3.grad_ref = bf16[4,192,256]{2,1,0:T(8,128)(2,1)S(1)} all-gather(bf16[2,192,256]{2,1,0:T(8,128)(2,1)S(1)} %pad_maximum_fusion), channel_id=1, replica_groups=mesh['xz'=32,'yh'=4,'chip'=2,'core'=2] {'core'}, dimensions={0}, use_global_device_ids=true | all-gather | bytes 589824 | tf_op jit(solution)/shard_map/all_gather | solution.py:505
  13.9 2.3 %collective-permute-done.1.near_ref = bf16[64,128]{1,0:T(8,128)(2,1)S(1)} collective-permute-done((bf16[64,128]{1,0:T(8,128)(2,1)S(1)}, bf16[64,128]{1,0:T(8,128)(2,1)S(1)}, u32[]{:S(2)}, u32[]{:S(2)}) %collective-permute-start.1) | collective-permute-done | bytes 16416 | tf_op jit(solution)/shard_map/ppermute | solution.py:504
  16.2 0.0 copy-done
  16.2 0.0 copy-done.1
  16.2 0.0 copy-done.2
  16.2 0.0 copy-done.3
  16.2 2.1 %local_kernel.1 = (bf16[32,48,128]{2,1,0:T(8,128)(2,1)}, bf16[192,256]{1,0:T(8,128)(2,1)S(1)}, f32[24,256]{1,0:T(8,128)S(1)}) custom-call(s32[1]{0:T(128)} %bitcast.side_ref, bf16[192,256]{1,0:T(8,128)(2,1)S(1)} %copy-done.2, bf16[192,256]{1,0:T(8,128)(2,1)S(1)} %copy-done, bf16[192,256]{1,0:T(8,128)(2,1)S(1)} %copy-done.1, ...), custom_call_target="tpu_custom_call" | custom-call | tf_op jit(solution)/shard_map/local_kernel/pallas_call | solution.py:464
  18.3 8.1 %all-to-all-start = ((bf16[32,48,128]{2,1,0:T(8,128)(2,1)}), bf16[32,48,128]{2,1,0:T(8,128)(2,1)S(1)}, u32[]{:S(2)}, u32[]{:S(2)}) async-start(bf16[32,48,128]{2,1,0:T(8,128)(2,1)} %get-tuple-element.28), calls=%async_computation | async-start | bytes 786432 | tf_op jit(solution)/shard_map/all_to_all | solution.py:513
  26.4 1.2 %local_grad_kernel.1 = (bf16[64,128]{1,0:T(8,128)(2,1)S(1)}, f32[192,256]{1,0:T(8,128)S(1)}, f32[192,256]{1,0:T(8,128)S(1)}, f32[192,256]{1,0:T(8,128)S(1)}) custom-call(bf16[192,256]{1,0:T(8,128)(2,1)S(1)} %copy-done.2, bf16[192,256]{1,0:T(8,128)(2,1)S(1)} %copy-done, bf16[192,256]{1,0:T(8,128)(2,1)S(1)} %copy-done.1, ...), custom_call_target="tpu_custom_call" | custom-call | tf_op jit(solution)/shard_map/local_grad_kernel/pallas_call | solution.py:464
  27.7 4.2 %collective-permute-start.2 = (bf16[64,128]{1,0:T(8,128)(2,1)S(1)}, bf16[64,128]{1,0:T(8,128)(2,1)S(1)}, u32[]{:S(2)}, u32[]{:S(2)}) collective-permute-start(bf16[64,128]{1,0:T(8,128)(2,1)S(1)} %get-tuple-element.31.own_ref), channel_id=1, source_target_pairs={{0,4},{4,0},{8,12},{12,8},{1,5},{5,1},{9,13},{13,9},{2,6},{6,2},{1... | collective-permute-start | bytes 49160 | tf_op jit(solution)/shard_map/ppermute | solution.py:519
  31.9 2.3 %collective-permute-done.2.partner_ref = bf16[64,128]{1,0:T(8,128)(2,1)S(1)} collective-permute-done((bf16[64,128]{1,0:T(8,128)(2,1)S(1)}, bf16[64,128]{1,0:T(8,128)(2,1)S(1)}, u32[]{:S(2)}, u32[]{:S(2)}) %collective-permute-start.2) | collective-permute-done | bytes 16416 | tf_op jit(solution)/shard_map/ppermute | solution.py:519
  34.2 0.7 prepare_kernel.1
  34.9 6.0 %all-to-all-done.slots_ref = bf16[32,48,128]{2,1,0:T(8,128)(2,1)S(1)} async-done(((bf16[32,48,128]{2,1,0:T(8,128)(2,1)}), bf16[32,48,128]{2,1,0:T(8,128)(2,1)S(1)}, u32[]{:S(2)}, u32[]{:S(2)}) %all-to-all-start) | async-done | bytes 393248 | tf_op jit(solution)/shard_map/all_to_all | solution.py:513
  40.9 0.1 merge_kernel.1
  40.9 15.9 %all_to_all.15.merged_ref = bf16[4,304,128]{2,1,0:T(8,128)(2,1)S(1)} all-to-all(bf16[4,304,128]{2,1,0:T(8,128)(2,1)S(1)} %merge_kernel.1), channel_id=1, replica_groups=mesh['xz'=32,'yh'=4,'chip'=2,'core'=2] {'yh'}, dimensions={0} | all-to-all | bytes 622592 | tf_op jit(solution)/shard_map/all_to_all | solution.py:544
  56.9 1.1 %far_kernel.1 = bf16[32,48,128]{2,1,0:T(8,128)(2,1)S(1)} custom-call(s32[1]{0:T(128)} %bitcast.3.plane_ref, bf16[4,304,128]{2,1,0:T(8,128)(2,1)S(1)} %all_to_all.15.merged_ref), custom_call_target="tpu_custom_call" | custom-call | tf_op jit(solution)/shard_map/far_kernel/pallas_call | solution.py:464
  58.0 19.2 %all_to_all.16.slots_ref = bf16[32,48,128]{2,1,0:T(8,128)(2,1)S(1)} all-to-all(bf16[32,48,128]{2,1,0:T(8,128)(2,1)S(1)} %far_kernel.1), channel_id=1, replica_groups=mesh['xz'=32,'yh'=4,'chip'=2,'core'=2] {'xz'}, dimensions={0} | all-to-all | bytes 786432 | tf_op jit(solution)/shard_map/all_to_all | solution.py:552
  77.2 1.8 %final_kernel.1 = (bf16[192,256]{1,0:T(8,128)(2,1)}, bf16[192,256]{1,0:T(8,128)(2,1)}, bf16[192,256]{1,0:T(8,128)(2,1)}, f32[192,768]{1,0:T(8,128)}) custom-call(bf16[48,128]{1,0:T(8,128)(2,1)S(1)} %get-tuple-element.42.rows_ref, f32[48,384]{1,0:T(8,128)S(1)} %get-tuple-element.43.scores_ref, f32[48,384]{1,0:T(8,128)S(1)} %get-tuple-element.44.grad_probs_ref, ...), custom_call_target="tpu_custom_call" | custom-call | tf_op jit(solution)/shard_map/final_kernel/pallas_call | solution.py:464
  (1 shorter events, 0.0 us)
Async XLA Ops:
  0.6 11.0 %copy-start.4 = (bf16[192,256]{1,0:T(8,128)(2,1)S(1)}, bf16[192,256]{1,0:T(8,128)(2,1)}, u32[]{:S(2)}) copy-start(bf16[192,256]{1,0:T(8,128)(2,1)} %param.9) | copy-start | bytes 294916
  0.6 11.0 %collective-permute-start = (bf16[192,256]{1,0:T(8,128)(2,1)}, bf16[192,256]{1,0:T(8,128)(2,1)S(1)}, u32[]{:S(2)}, u32[]{:S(2)}) collective-permute-start(bf16[192,256]{1,0:T(8,128)(2,1)} %param.9), channel_id=1, source_target_pairs={{0,2},{2,0},{1,3},{3,1},{4,6},{6,4},{5,7},{7,5},{8,10},{10,8},{9,1... | collective-permute-start | bytes 294920 | tf_op jit(solution)/shard_map/ppermute | solution.py:495
  9.7 6.5 %collective-permute-start.1 = (bf16[64,128]{1,0:T(8,128)(2,1)S(1)}, bf16[64,128]{1,0:T(8,128)(2,1)S(1)}, u32[]{:S(2)}, u32[]{:S(2)}) collective-permute-start(bf16[64,128]{1,0:T(8,128)(2,1)S(1)} %near_kernel.1), channel_id=1, source_target_pairs={{0,4},{4,0},{8,12},{12,8},{1,5},{5,1},{9,13},{13,9},{2,6},{6,2},{1... | collective-permute-start | bytes 49160 | tf_op jit(solution)/shard_map/ppermute | solution.py:504
  11.7 4.5 %copy-start = (bf16[192,256]{1,0:T(8,128)(2,1)S(1)}, bf16[192,256]{1,0:T(8,128)(2,1)}, u32[]{:S(2)}) copy-start(bf16[192,256]{1,0:T(8,128)(2,1)} %key_ref.5) | copy-start | bytes 294916
  11.7 4.5 %copy-start.1 = (bf16[192,256]{1,0:T(8,128)(2,1)S(1)}, bf16[192,256]{1,0:T(8,128)(2,1)}, u32[]{:S(2)}) copy-start(bf16[192,256]{1,0:T(8,128)(2,1)} %value_ref.5) | copy-start | bytes 294916
  11.7 4.5 %copy-start.2 = (bf16[192,256]{1,0:T(8,128)(2,1)S(1)}, bf16[192,256]{1,0:T(8,128)(2,1)}, u32[]{:S(2)}) copy-start(bf16[192,256]{1,0:T(8,128)(2,1)} %query_ref.3) | copy-start | bytes 294916
  11.7 4.5 %copy-start.3 = (bf16[192,768]{1,0:T(8,128)(2,1)S(1)}, bf16[192,768]{1,0:T(8,128)(2,1)}, u32[]{:S(2)}) copy-start(bf16[192,768]{1,0:T(8,128)(2,1)} %weight_ref.1) | copy-start | bytes 884740
  18.3 22.6 %all-to-all-start = ((bf16[32,48,128]{2,1,0:T(8,128)(2,1)}), bf16[32,48,128]{2,1,0:T(8,128)(2,1)S(1)}, u32[]{:S(2)}, u32[]{:S(2)}) async-start(bf16[32,48,128]{2,1,0:T(8,128)(2,1)} %get-tuple-element.28), calls=%async_computation | async-start | bytes 786432 | tf_op jit(solution)/shard_map/all_to_all | solution.py:513
  27.7 6.5 %collective-permute-start.2 = (bf16[64,128]{1,0:T(8,128)(2,1)S(1)}, bf16[64,128]{1,0:T(8,128)(2,1)S(1)}, u32[]{:S(2)}, u32[]{:S(2)}) collective-permute-start(bf16[64,128]{1,0:T(8,128)(2,1)S(1)} %get-tuple-element.31.own_ref), channel_id=1, source_target_pairs={{0,4},{4,0},{8,12},{12,8},{1,5},{5,1},{9,13},{13,9},{2,6},{6,2},{1... | collective-permute-start | bytes 49160 | tf_op jit(solution)/shard_map/ppermute | solution.py:519

commit v12 on v11

--- a/solution.py
+++ b/solution.py
@@ -163,10 +163,10 @@
     near = [near_ref[head * NEAR : (head + 1) * NEAR] for head in heads]
     in_near = [same_class(query_row, offset, RC) for offset in offsets]
     in_far = [same_class(query_row, offset, RE) for offset in offsets]
-    scores = [mm(key_ref[rows[h]], query_ref[rows[h]], 0, 0) * SCORE_SCALE for h in heads]
+    scaled = [query_ref[rows[h]] * SCORE_SCALE for h in heads]
+    scores = [mm(key_ref[rows[h]], scaled[h], 0, 0) for h in heads]
     near_scores = [
-        mm(near[h], jnp.concatenate([query_ref[rows[h]], blank], axis=0), 1, 0) * SCORE_SCALE
-        for h in heads
+        mm(near[h], jnp.concatenate([scaled[h], blank], axis=0), 1, 0) for h in heads
     ]
     peak = [jnp.max(scores[h], axis=0, keepdims=True) for h in heads]
     near_max = [jnp.max(near_scores[h], axis=0, keepdims=True) for h in heads]
@@ -299,11 +299,11 @@
     stats = stats_attended.astype(F32)
     attended_stats = mm(stats_attended, swap, 1, 0)
     wide = query_dout.astype(F32)
-    query = jnp.where(left, wide, 0.0).astype(BF16)
+    query = jnp.where(left, wide * SCORE_SCALE, 0.0).astype(BF16)
     dout_wide = jnp.where(left, 0.0, wide)
     local_mass = take_stat(stats, 0, 0)
 
-    scores = mm(query, key_value, 1, 1) * SCORE_SCALE
+    scores = mm(query, key_value, 1, 1)
     grad_probs = mm(dout_wide.astype(BF16), key_value, 1, 1)
     peak = jnp.maximum(jnp.max(scores, axis=1, keepdims=True), local_mass)
     mass = jnp.exp(scores - peak)

time: 79.4 us -> 79.4 us (level)
  no operation moved by 1% of the time
where the time goes in v12:
time: 79.4 us; the launch traced here: 79 us
  blocking collectives  37.4 us (47%)
  starting transfers between devices  22.1 us (28%)
  waiting for transfers between devices  10.6 us (13%)
  Pallas kernels  8.06 us (10%)
    all_to_all x1, blocking collectives, local(): slots = lax.all_to_all(slots, 'xz', 0, 0, tiled=True)  19.2 us
    all_to_all x1, blocking collectives, local(): merged = lax.all_to_all(merged, 'yh', 0, 0, tiled=True)  15.9 us
    all_to_all x1, starting transfers between devices, local(): slots = lax.all_to_all(slots, 'xz', 0, 0, tiled=True)  8.11 us
    pallas_call x7, Pallas kernels, call(): pl.pallas_call(kernel, out_shape=shapes, in_specs=specs, out_specs=[pl.Bl...  8.06 us
    ppermute x1, starting transfers between devices, local(): other_grad = lax.ppermute(grad_out, 'chip', [(0, 1), (1, 0)])  7.86 us
    all_to_all x1, waiting for transfers between devices, local(): slots = lax.all_to_all(slots, 'xz', 0, 0, tiled=True)  6 us
    ppermute x1, starting transfers between devices, local(): partner = lax.ppermute(own, 'yh', other)  4.19 us
    ppermute x1, waiting for transfers between devices, local(): partner = lax.ppermute(own, 'yh', other)  2.32 us
  transfers between devices with their start and end apart: 4, of which 3 were waited for; matrix products, arithmetic and copies ran while one was open for 0% of the time, Pallas kernels for 4%

profile of v12, /device:TPU:8, one launch (start us, length us, event | category | flops | bytes accessed | tf_op | source)
XLA Modules:
  0.0 79.0 jit_solution(17360018120845502768)
XLA Ops:
  0.6 0.0 copy-start.4
  0.6 7.9 %collective-permute-start = (bf16[192,256]{1,0:T(8,128)(2,1)}, bf16[192,256]{1,0:T(8,128)(2,1)S(1)}, u32[]{:S(2)}, u32[]{:S(2)}) collective-permute-start(bf16[192,256]{1,0:T(8,128)(2,1)} %param.9), channel_id=1, source_target_pairs={{0,2},{2,0},{1,3},{3,1},{4,6},{6,4},{5,7},{7,5},{8,10},{10,8},{9,1... | collective-permute-start | bytes 294920 | tf_op jit(solution)/shard_map/ppermute | solution.py:495
  8.5 1.2 %near_kernel.1 = bf16[64,128]{1,0:T(8,128)(2,1)S(1)} custom-call(s32[3]{0:T(128)} %offset_hbm.1, bf16[192,256]{1,0:T(8,128)(2,1)} %key_ref.5, bf16[192,256]{1,0:T(8,128)(2,1)} %value_ref.5), custom_call_target="tpu_custom_call" | custom-call | tf_op jit(solution)/shard_map/near_kernel/pallas_call | solution.py:464
  9.7 1.9 %collective-permute-start.1 = (bf16[64,128]{1,0:T(8,128)(2,1)S(1)}, bf16[64,128]{1,0:T(8,128)(2,1)S(1)}, u32[]{:S(2)}, u32[]{:S(2)}) collective-permute-start(bf16[64,128]{1,0:T(8,128)(2,1)S(1)} %near_kernel.1), channel_id=1, source_target_pairs={{0,4},{4,0},{8,12},{12,8},{1,5},{5,1},{9,13},{13,9},{2,6},{6,2},{1... | collective-permute-start | bytes 49160 | tf_op jit(solution)/shard_map/ppermute | solution.py:504
  11.6 0.0 collective-permute-done
  11.6 0.0 copy-done.4
  11.7 0.0 copy-start
  11.7 0.0 copy-start.1
  11.7 0.0 copy-start.2
  11.7 0.0 copy-start.3
  11.7 2.2 %all_gather.3.grad_ref = bf16[4,192,256]{2,1,0:T(8,128)(2,1)S(1)} all-gather(bf16[2,192,256]{2,1,0:T(8,128)(2,1)S(1)} %pad_maximum_fusion), channel_id=1, replica_groups=mesh['xz'=32,'yh'=4,'chip'=2,'core'=2] {'core'}, dimensions={0}, use_global_device_ids=true | all-gather | bytes 589824 | tf_op jit(solution)/shard_map/all_gather | solution.py:505
  13.9 2.3 %collective-permute-done.1.near_ref = bf16[64,128]{1,0:T(8,128)(2,1)S(1)} collective-permute-done((bf16[64,128]{1,0:T(8,128)(2,1)S(1)}, bf16[64,128]{1,0:T(8,128)(2,1)S(1)}, u32[]{:S(2)}, u32[]{:S(2)}) %collective-permute-start.1) | collective-permute-done | bytes 16416 | tf_op jit(solution)/shard_map/ppermute | solution.py:504
  16.2 0.0 copy-done
  16.2 0.0 copy-done.1
  16.2 0.0 copy-done.2
  16.2 0.0 copy-done.3
  16.2 2.1 %local_kernel.1 = (bf16[32,48,128]{2,1,0:T(8,128)(2,1)}, bf16[192,256]{1,0:T(8,128)(2,1)S(1)}, f32[24,256]{1,0:T(8,128)S(1)}) custom-call(s32[1]{0:T(128)} %bitcast.side_ref, bf16[192,256]{1,0:T(8,128)(2,1)S(1)} %copy-done.2, bf16[192,256]{1,0:T(8,128)(2,1)S(1)} %copy-done, bf16[192,256]{1,0:T(8,128)(2,1)S(1)} %copy-done.1, ...), custom_call_target="tpu_custom_call" | custom-call | tf_op jit(solution)/shard_map/local_kernel/pallas_call | solution.py:464
  18.3 8.1 %all-to-all-start = ((bf16[32,48,128]{2,1,0:T(8,128)(2,1)}), bf16[32,48,128]{2,1,0:T(8,128)(2,1)S(1)}, u32[]{:S(2)}, u32[]{:S(2)}) async-start(bf16[32,48,128]{2,1,0:T(8,128)(2,1)} %get-tuple-element.28), calls=%async_computation | async-start | bytes 786432 | tf_op jit(solution)/shard_map/all_to_all | solution.py:513
  26.4 1.2 %local_grad_kernel.1 = (bf16[64,128]{1,0:T(8,128)(2,1)S(1)}, f32[192,256]{1,0:T(8,128)S(1)}, f32[192,256]{1,0:T(8,128)S(1)}, f32[192,256]{1,0:T(8,128)S(1)}) custom-call(bf16[192,256]{1,0:T(8,128)(2,1)S(1)} %copy-done.2, bf16[192,256]{1,0:T(8,128)(2,1)S(1)} %copy-done, bf16[192,256]{1,0:T(8,128)(2,1)S(1)} %copy-done.1, ...), custom_call_target="tpu_custom_call" | custom-call | tf_op jit(solution)/shard_map/local_grad_kernel/pallas_call | solution.py:464
  27.6 4.2 %collective-permute-start.2 = (bf16[64,128]{1,0:T(8,128)(2,1)S(1)}, bf16[64,128]{1,0:T(8,128)(2,1)S(1)}, u32[]{:S(2)}, u32[]{:S(2)}) collective-permute-start(bf16[64,128]{1,0:T(8,128)(2,1)S(1)} %get-tuple-element.31.own_ref), channel_id=1, source_target_pairs={{0,4},{4,0},{8,12},{12,8},{1,5},{5,1},{9,13},{13,9},{2,6},{6,2},{1... | collective-permute-start | bytes 49160 | tf_op jit(solution)/shard_map/ppermute | solution.py:519
  31.9 2.3 %collective-permute-done.2.partner_ref = bf16[64,128]{1,0:T(8,128)(2,1)S(1)} collective-permute-done((bf16[64,128]{1,0:T(8,128)(2,1)S(1)}, bf16[64,128]{1,0:T(8,128)(2,1)S(1)}, u32[]{:S(2)}, u32[]{:S(2)}) %collective-permute-start.2) | collective-permute-done | bytes 16416 | tf_op jit(solution)/shard_map/ppermute | solution.py:519
  34.2 0.7 prepare_kernel.1
  34.8 6.0 %all-to-all-done.slots_ref = bf16[32,48,128]{2,1,0:T(8,128)(2,1)S(1)} async-done(((bf16[32,48,128]{2,1,0:T(8,128)(2,1)}), bf16[32,48,128]{2,1,0:T(8,128)(2,1)S(1)}, u32[]{:S(2)}, u32[]{:S(2)}) %all-to-all-start) | async-done | bytes 393248 | tf_op jit(solution)/shard_map/all_to_all | solution.py:513
  40.8 0.1 merge_kernel.1
  40.9 15.9 %all_to_all.15.merged_ref = bf16[4,304,128]{2,1,0:T(8,128)(2,1)S(1)} all-to-all(bf16[4,304,128]{2,1,0:T(8,128)(2,1)S(1)} %merge_kernel.1), channel_id=1, replica_groups=mesh['xz'=32,'yh'=4,'chip'=2,'core'=2] {'yh'}, dimensions={0} | all-to-all | bytes 622592 | tf_op jit(solution)/shard_map/all_to_all | solution.py:544
  56.9 1.1 %far_kernel.1 = bf16[32,48,128]{2,1,0:T(8,128)(2,1)S(1)} custom-call(s32[1]{0:T(128)} %bitcast.3.plane_ref, bf16[4,304,128]{2,1,0:T(8,128)(2,1)S(1)} %all_to_all.15.merged_ref), custom_call_target="tpu_custom_call" | custom-call | tf_op jit(solution)/shard_map/far_kernel/pallas_call | solution.py:464
  58.0 19.2 %all_to_all.16.slots_ref = bf16[32,48,128]{2,1,0:T(8,128)(2,1)S(1)} all-to-all(bf16[32,48,128]{2,1,0:T(8,128)(2,1)S(1)} %far_kernel.1), channel_id=1, replica_groups=mesh['xz'=32,'yh'=4,'chip'=2,'core'=2] {'xz'}, dimensions={0} | all-to-all | bytes 786432 | tf_op jit(solution)/shard_map/all_to_all | solution.py:552
  77.2 1.8 %final_kernel.1 = (bf16[192,256]{1,0:T(8,128)(2,1)}, bf16[192,256]{1,0:T(8,128)(2,1)}, bf16[192,256]{1,0:T(8,128)(2,1)}, f32[192,768]{1,0:T(8,128)}) custom-call(bf16[48,128]{1,0:T(8,128)(2,1)S(1)} %get-tuple-element.42.rows_ref, f32[48,384]{1,0:T(8,128)S(1)} %get-tuple-element.43.scores_ref, f32[48,384]{1,0:T(8,128)S(1)} %get-tuple-element.44.grad_probs_ref, ...), custom_call_target="tpu_custom_call" | custom-call | tf_op jit(solution)/shard_map/final_kernel/pallas_call | solution.py:464
  (1 shorter events, 0.0 us)
Async XLA Ops:
  0.6 11.0 %copy-start.4 = (bf16[192,256]{1,0:T(8,128)(2,1)S(1)}, bf16[192,256]{1,0:T(8,128)(2,1)}, u32[]{:S(2)}) copy-start(bf16[192,256]{1,0:T(8,128)(2,1)} %param.9) | copy-start | bytes 294916
  0.6 11.0 %collective-permute-start = (bf16[192,256]{1,0:T(8,128)(2,1)}, bf16[192,256]{1,0:T(8,128)(2,1)S(1)}, u32[]{:S(2)}, u32[]{:S(2)}) collective-permute-start(bf16[192,256]{1,0:T(8,128)(2,1)} %param.9), channel_id=1, source_target_pairs={{0,2},{2,0},{1,3},{3,1},{4,6},{6,4},{5,7},{7,5},{8,10},{10,8},{9,1... | collective-permute-start | bytes 294920 | tf_op jit(solution)/shard_map/ppermute | solution.py:495
  9.7 6.5 %collective-permute-start.1 = (bf16[64,128]{1,0:T(8,128)(2,1)S(1)}, bf16[64,128]{1,0:T(8,128)(2,1)S(1)}, u32[]{:S(2)}, u32[]{:S(2)}) collective-permute-start(bf16[64,128]{1,0:T(8,128)(2,1)S(1)} %near_kernel.1), channel_id=1, source_target_pairs={{0,4},{4,0},{8,12},{12,8},{1,5},{5,1},{9,13},{13,9},{2,6},{6,2},{1... | collective-permute-start | bytes 49160 | tf_op jit(solution)/shard_map/ppermute | solution.py:504
  11.7 4.5 %copy-start = (bf16[192,256]{1,0:T(8,128)(2,1)S(1)}, bf16[192,256]{1,0:T(8,128)(2,1)}, u32[]{:S(2)}) copy-start(bf16[192,256]{1,0:T(8,128)(2,1)} %key_ref.5) | copy-start | bytes 294916
  11.7 4.5 %copy-start.1 = (bf16[192,256]{1,0:T(8,128)(2,1)S(1)}, bf16[192,256]{1,0:T(8,128)(2,1)}, u32[]{:S(2)}) copy-start(bf16[192,256]{1,0:T(8,128)(2,1)} %value_ref.5) | copy-start | bytes 294916
  11.7 4.5 %copy-start.2 = (bf16[192,256]{1,0:T(8,128)(2,1)S(1)}, bf16[192,256]{1,0:T(8,128)(2,1)}, u32[]{:S(2)}) copy-start(bf16[192,256]{1,0:T(8,128)(2,1)} %query_ref.3) | copy-start | bytes 294916
  11.7 4.5 %copy-start.3 = (bf16[192,768]{1,0:T(8,128)(2,1)S(1)}, bf16[192,768]{1,0:T(8,128)(2,1)}, u32[]{:S(2)}) copy-start(bf16[192,768]{1,0:T(8,128)(2,1)} %weight_ref.1) | copy-start | bytes 884740
  18.3 22.6 %all-to-all-start = ((bf16[32,48,128]{2,1,0:T(8,128)(2,1)}), bf16[32,48,128]{2,1,0:T(8,128)(2,1)S(1)}, u32[]{:S(2)}, u32[]{:S(2)}) async-start(bf16[32,48,128]{2,1,0:T(8,128)(2,1)} %get-tuple-element.28), calls=%async_computation | async-start | bytes 786432 | tf_op jit(solution)/shard_map/all_to_all | solution.py:513
  27.6 6.5 %collective-permute-start.2 = (bf16[64,128]{1,0:T(8,128)(2,1)S(1)}, bf16[64,128]{1,0:T(8,128)(2,1)S(1)}, u32[]{:S(2)}, u32[]{:S(2)}) collective-permute-start(bf16[64,128]{1,0:T(8,128)(2,1)S(1)} %get-tuple-element.31.own_ref), channel_id=1, source_target_pairs={{0,4},{4,0},{8,12},{12,8},{1,5},{5,1},{9,13},{13,9},{2,6},{6,2},{1... | collective-permute-start | bytes 49160 | tf_op jit(solution)/shard_map/ppermute | solution.py:519
